TPU v7x, 32 devices: a whole 2x2x4 slice. The times are simulated.
32 devices in a mesh: dp: 8 (over z, y), head: 4 (over x, core).
Axes of the slice: x: 2, y: 2, z: 4, core: 2. Of those that a mesh axis runs over, the one named last changes fastest.
Arguments:
- tokens: int32 [8, 1024], P('dp'), may hold values from 0 to 32767
- targets: int32 [8, 1024], P('dp'), may hold values from 0 to 32767
- lengths: int32 [8], P('dp'), may hold values from 341 to 1024
- table: float32 [512, 32768], P('dp', 'head'), may hold values from -0.6629126 to 0.6629126
- table_first: float32 [512, 32768], P('dp', 'head'), may hold values from -9.691891e-05 to 9.691891e-05
- table_second: float32 [512, 32768], P('dp', 'head'), may hold values from 3.75731e-11 to 1.502924e-10
- attn_in: float32 [3, 512, 8, 224], P(None, 'dp', 'head'), may hold values from -0.25 to 0.25
- attn_in_first: float32 [3, 512, 8, 224], P(None, 'dp', 'head'), may hold values from -9.691891e-05 to 9.691891e-05
- attn_in_second: float32 [3, 512, 8, 224], P(None, 'dp', 'head'), may hold values from 3.75731e-11 to 1.502924e-10
- attn_out: float32 [3, 8, 64, 512], P(None, 'head', None, 'dp'), may hold values from -1 to 1
- attn_out_first: float32 [3, 8, 64, 512], P(None, 'head', None, 'dp'), may hold values from -9.691891e-05 to 9.691891e-05
- attn_out_second: float32 [3, 8, 64, 512], P(None, 'head', None, 'dp'), may hold values from 3.75731e-11 to 1.502924e-10
- ffn_up: float32 [3, 512, 2048], P(None, 'dp', 'head'), may hold values from -0.25 to 0.25
- ffn_up_first: float32 [3, 512, 2048], P(None, 'dp', 'head'), may hold values from -9.691891e-05 to 9.691891e-05
- ffn_up_second: float32 [3, 512, 2048], P(None, 'dp', 'head'), may hold values from 3.75731e-11 to 1.502924e-10
- ffn_down: float32 [3, 2048, 512], P(None, 'head', 'dp'), may hold values from -0.1875 to 0.1875
- ffn_down_first: float32 [3, 2048, 512], P(None, 'head', 'dp'), may hold values from -9.691891e-05 to 9.691891e-05
- ffn_down_second: float32 [3, 2048, 512], P(None, 'head', 'dp'), may hold values from 3.75731e-11 to 1.502924e-10
- norms: float32 [7, 2, 512], P(None, None, 'head'), may hold values from -1.5 to 1.8
- norms_first: float32 [7, 2, 512], P(None, None, 'head'), may hold values from -9.691891e-05 to 9.691891e-05
- norms_second: float32 [7, 2, 512], P(None, None, 'head'), may hold values from 3.75731e-11 to 1.502924e-10
Outputs:
- loss_parts: float32 [2], replicated
- clip_norm: float32 [], replicated
- refreshed_table: float32 [512, 32768], P('dp', 'head')
- table_copy: bfloat16 [512, 32768], P('dp', 'head')
- table_first_new: float32 [512, 32768], P('dp', 'head')
- table_second_new: float32 [512, 32768], P('dp', 'head')
- attn_in_new: float32 [3, 512, 8, 224], P(None, 'dp', 'head')
- attn_in_copy: bfloat16 [3, 512, 8, 224], P(None, 'dp', 'head')
- attn_in_first_new: float32 [3, 512, 8, 224], P(None, 'dp', 'head')
- attn_in_second_new: float32 [3, 512, 8, 224], P(None, 'dp', 'head')
- attn_out_new: float32 [3, 8, 64, 512], P(None, 'head', None, 'dp')
- attn_out_copy: bfloat16 [3, 8, 64, 512], P(None, 'head', None, 'dp')
- attn_out_first_new: float32 [3, 8, 64, 512], P(None, 'head', None, 'dp')
- attn_out_second_new: float32 [3, 8, 64, 512], P(None, 'head', None, 'dp')
- ffn_up_new: float32 [3, 512, 2048], P(None, 'dp', 'head')
- ffn_up_copy: bfloat16 [3, 512, 2048], P(None, 'dp', 'head')
- ffn_up_first_new: float32 [3, 512, 2048], P(None, 'dp', 'head')
- ffn_up_second_new: float32 [3, 512, 2048], P(None, 'dp', 'head')
- ffn_down_new: float32 [3, 2048, 512], P(None, 'head', 'dp')
- ffn_down_copy: bfloat16 [3, 2048, 512], P(None, 'head', 'dp')
- ffn_down_first_new: float32 [3, 2048, 512], P(None, 'head', 'dp')
- ffn_down_second_new: float32 [3, 2048, 512], P(None, 'head', 'dp')
- norms_new: float32 [7, 2, 512], P(None, None, 'head')
- norms_first_new: float32 [7, 2, 512], P(None, None, 'head')
- norms_second_new: float32 [7, 2, 512], P(None, None, 'head')
All inputs are finite; a program needn't handle non-finite values.
Results may differ from a plain program's by a relative error of at most 0.0092.
Values may be sent and summed in bfloat16 or wider, within the bound.
A program may use at most 256 MiB of HBM per device.

v0:
```python
import math

import jax
import jax.numpy as jnp
from jax import lax
from jax.sharding import PartitionSpec as P

HD = 64
BLOCK = 32
SINK = 8
STEP = 10


EPSILON = 1e-05
NEGATIVE = -1000000000.0
TEMPER = 0.75
BETA_ONE = 0.9
BETA_TWO = 0.999
ADAM_FLOOR = 1e-08
WEIGHT_DECAY = 0.01
RATE_MATRIX = 0.1
RATE_NORM = 0.5
CLIP_LIMIT = 1.0
ROWS_CONTRACT = (((0,), (0,)), ((), ()))
COLS_CONTRACT = (((1,), (1,)), ((), ()))


def alternating_marginal_scaling(vocabulary_score_lines):
    block_total = vocabulary_score_lines.shape[-1]
    row_index = lax.broadcasted_iota(jnp.int32, (block_total, block_total), 0)
    column_index = lax.broadcasted_iota(jnp.int32, (block_total, block_total), 1)
    allowed = column_index < row_index
    log_plan = jnp.where(allowed, vocabulary_score_lines / TEMPER, NEGATIVE)
    for sweep_index in range(SINK):
        log_plan = jnp.where(
            allowed, log_plan - jax.nn.logsumexp(log_plan, -2, keepdims=True), NEGATIVE
        )
        log_plan = jnp.where(
            allowed, log_plan - jax.nn.logsumexp(log_plan, -1, keepdims=True), NEGATIVE
        )
    return jnp.where(allowed, jnp.exp(log_plan), 0.0)


def block_view(tensor, block_count):
    seq_count, length_all, group_count, trailing = tensor.shape
    return tensor.reshape(
        seq_count, block_count, length_all // block_count, group_count, trailing
    ).transpose(0, 3, 1, 2, 4)


def unblock(tensor):
    seq_count, group_count, block_count, block_size, trailing = tensor.shape
    return tensor.transpose(0, 2, 3, 1, 4).reshape(
        seq_count * block_count * block_size, group_count * trailing
    )


def attend_mask(block_count, block_size):
    shape = (block_count, block_size, 2 * block_size)
    block_index = lax.broadcasted_iota(jnp.int32, shape, 0)
    query_index = lax.broadcasted_iota(jnp.int32, shape, 1)
    slot_index = lax.broadcasted_iota(jnp.int32, shape, 2)
    own_block = (slot_index >= block_size) & (slot_index - block_size <= query_index)
    return own_block | (slot_index < block_size) & (block_index >= 1)


def row_sums(left_term, right_term):
    return lax.psum((jnp.sum(left_term, 1), jnp.sum(right_term, 1)), "head")


def collect(piece):
    return lax.all_gather(piece, "head", axis=1, tiled=True)


def settle(partial_rows):
    return lax.psum_scatter(
        partial_rows.astype(jnp.bfloat16), "head", scatter_dimension=1, tiled=True
    ).astype(jnp.float32)


def norm_forward(stream, norm_pair):
    full_width = stream.shape[1] * lax.axis_size("head")
    totals, squares = row_sums(stream, stream * stream)
    average = totals / full_width
    inv_std = lax.rsqrt(squares / full_width - average * average + EPSILON)
    normed = (stream - average[:, None]) * inv_std[:, None]
    return (collect((normed * norm_pair[0] + norm_pair[1]).astype(jnp.bfloat16)), normed, inv_std)


def norm_backward(upstream, normed, inv_std, norm_pair):
    full_width = upstream.shape[1] * lax.axis_size("head")
    scaled = upstream * norm_pair[0]
    totals, crossed = row_sums(scaled, scaled * normed)
    back = inv_std[:, None] * (
        scaled - totals[:, None] / full_width - normed * crossed[:, None] / full_width
    )
    return (back, jnp.stack([jnp.sum(upstream * normed, 0), jnp.sum(upstream, 0)]))


def attend_forward(hidden, w_in, seq_count):
    row_count, full_width = hidden.shape
    group_count, column_count = (w_in.shape[1], w_in.shape[2])
    length_all = row_count // seq_count
    block_count = length_all // BLOCK
    projected = jnp.dot(
        hidden,
        w_in.reshape(full_width, group_count * column_count),
        preferred_element_type=jnp.float32,
    )
    projected = projected.reshape(seq_count, length_all, group_count, column_count)
    packed = projected[..., : 3 * HD].astype(jnp.bfloat16)
    queries = block_view(packed[..., :HD], block_count)
    key_blocks = block_view(packed[..., HD : 2 * HD], block_count)
    value_blocks = block_view(packed[..., 2 * HD :], block_count)
    vocabulary_score_lines = jnp.sum(
        block_view(projected[..., 3 * HD :], block_count), 3
    ) / math.sqrt(BLOCK)
    doubly_stochastic_matrix, balancing_adjoint_sweep = jax.vjp(
        alternating_marginal_scaling, vocabulary_score_lines
    )
    perm_low = doubly_stochastic_matrix.astype(jnp.bfloat16)
    sorted_keys = jnp.einsum(
        "shij,shjtc->shitc", perm_low, key_blocks, preferred_element_type=jnp.float32
    ).astype(jnp.bfloat16)
    permuted_value_blocks = jnp.einsum(
        "shij,shjtc->shitc", perm_low, value_blocks, preferred_element_type=jnp.float32
    ).astype(jnp.bfloat16)
    key_set = jnp.concatenate([sorted_keys, key_blocks], 3)
    value_set = jnp.concatenate([permuted_value_blocks, value_blocks], 3)
    scores = jnp.einsum(
        "shitc,shiuc->shitu", queries, key_set, preferred_element_type=jnp.float32
    ) / math.sqrt(HD)
    attn_weights = jax.nn.softmax(jnp.where(attend_mask(block_count, BLOCK), scores, NEGATIVE), -1)
    weights_low = attn_weights.astype(jnp.bfloat16)
    mixed = jnp.einsum(
        "shitu,shiuc->shitc", weights_low, value_set, preferred_element_type=jnp.float32
    ).astype(jnp.bfloat16)
    flat_mixed = unblock(mixed)
    kept = (
        queries,
        key_blocks,
        value_blocks,
        perm_low,
        balancing_adjoint_sweep,
        key_set,
        value_set,
        attn_weights,
        weights_low,
        flat_mixed,
    )
    return (flat_mixed, kept)


def attend_backward(upstream_low, hidden, w_in, w_out, kept, seq_count):
    (
        queries,
        key_blocks,
        value_blocks,
        perm_low,
        balancing_adjoint_sweep,
        key_set,
        value_set,
        attn_weights,
        weights_low,
        flat_mixed,
    ) = kept
    group_count, block_count, block_size = (queries.shape[1], queries.shape[2], queries.shape[3])
    full_width = hidden.shape[1]
    grad_out = lax.dot_general(
        flat_mixed, upstream_low, ROWS_CONTRACT, preferred_element_type=jnp.float32
    )
    grad_flat = lax.dot_general(
        upstream_low,
        w_out.reshape(group_count * HD, full_width),
        COLS_CONTRACT,
        preferred_element_type=jnp.float32,
    )
    grad_mixed = block_view(
        grad_flat.astype(jnp.bfloat16).reshape(
            seq_count, block_count * block_size, group_count, HD
        ),
        block_count,
    )
    grad_weights = jnp.einsum(
        "shitc,shiuc->shitu", grad_mixed, value_set, preferred_element_type=jnp.float32
    )
    grad_scores = (
        attn_weights * (grad_weights - jnp.sum(attn_weights * grad_weights, -1, keepdims=True))
    ).astype(jnp.bfloat16)
    grad_query = jnp.einsum(
        "shitu,shiuc->shitc", grad_scores, key_set, preferred_element_type=jnp.float32
    ) / math.sqrt(HD)
    grad_keyset = jnp.einsum(
        "shitu,shitc->shiuc", grad_scores, queries, preferred_element_type=jnp.float32
    ) / math.sqrt(HD)
    grad_valueset = jnp.einsum(
        "shitu,shitc->shiuc", weights_low, grad_mixed, preferred_element_type=jnp.float32
    )
    grad_sorted_keys = grad_keyset[..., :block_size, :].astype(jnp.bfloat16)
    grad_sorted_values = grad_valueset[..., :block_size, :].astype(jnp.bfloat16)
    grad_key_blocks = grad_keyset[..., block_size:, :] + jnp.einsum(
        "shij,shitc->shjtc", perm_low, grad_sorted_keys, preferred_element_type=jnp.float32
    )
    grad_value_blocks = grad_valueset[..., block_size:, :] + jnp.einsum(
        "shij,shitc->shjtc", perm_low, grad_sorted_values, preferred_element_type=jnp.float32
    )
    shuffle_matrix_derivative = jnp.einsum(
        "shitc,shjtc->shij", grad_sorted_keys, key_blocks, preferred_element_type=jnp.float32
    )
    shuffle_matrix_derivative = shuffle_matrix_derivative + jnp.einsum(
        "shitc,shjtc->shij", grad_sorted_values, value_blocks, preferred_element_type=jnp.float32
    )
    (score_derivative,) = balancing_adjoint_sweep(shuffle_matrix_derivative)
    grad_sort = jnp.broadcast_to(
        score_derivative[:, :, :, None, :] / math.sqrt(BLOCK),
        score_derivative.shape[:3] + (block_size, score_derivative.shape[3]),
    )
    grad_packed = jnp.concatenate([grad_query, grad_key_blocks, grad_value_blocks, grad_sort], -1)
    grad_projected = unblock(grad_packed).astype(jnp.bfloat16)
    grad_in = lax.dot_general(
        hidden, grad_projected, ROWS_CONTRACT, preferred_element_type=jnp.float32
    ).reshape(w_in.shape)
    grad_hidden = lax.dot_general(
        grad_projected,
        w_in.reshape(full_width, -1),
        COLS_CONTRACT,
        preferred_element_type=jnp.float32,
    )
    return (grad_hidden, grad_in, grad_out.reshape(w_out.shape))


def ffn_forward(hidden, w_up):
    upward = jnp.dot(hidden, w_up, preferred_element_type=jnp.float32)
    activated, gelu_back = jax.vjp(jax.nn.gelu, upward)
    return (activated.astype(jnp.bfloat16), gelu_back)


def ffn_backward(upstream_low, hidden, w_up, w_down, activated, gelu_back):
    grad_down = lax.dot_general(
        activated, upstream_low, ROWS_CONTRACT, preferred_element_type=jnp.float32
    )
    (grad_upward,) = gelu_back(
        lax.dot_general(upstream_low, w_down, COLS_CONTRACT, preferred_element_type=jnp.float32)
    )
    grad_rounded = grad_upward.astype(jnp.bfloat16)
    grad_up = lax.dot_general(
        hidden, grad_rounded, ROWS_CONTRACT, preferred_element_type=jnp.float32
    )
    grad_hidden = lax.dot_general(
        grad_rounded, w_up, COLS_CONTRACT, preferred_element_type=jnp.float32
    )
    return (grad_hidden, grad_up, grad_down)


def layer_forward(stream, layer_params, norm_one, norm_two, seq_count):
    w_in, w_out, w_up, w_down = layer_params
    hidden, normed_one, inv_one = norm_forward(stream, norm_one)
    flat_mixed, kept = attend_forward(hidden, w_in, seq_count)
    middle = stream + settle(
        jnp.dot(flat_mixed, w_out.reshape(-1, w_out.shape[2]), preferred_element_type=jnp.float32)
    )
    hidden_two, normed_two, inv_two = norm_forward(middle, norm_two)
    activated, gelu_back = ffn_forward(hidden_two, w_up)
    result = middle + settle(jnp.dot(activated, w_down, preferred_element_type=jnp.float32))
    return (
        result,
        (hidden, normed_one, inv_one, kept, hidden_two, normed_two, inv_two, activated, gelu_back),
    )


def layer_backward(stream, upstream, layer_params, norm_one, norm_two, seq_count):
    w_in, w_out, w_up, w_down = layer_params
    unused, kept_values = layer_forward(stream, layer_params, norm_one, norm_two, seq_count)
    hidden, normed_one, inv_one, kept, hidden_two, normed_two, inv_two, activated, gelu_back = (
        kept_values
    )
    grad_hidden, grad_up, grad_down = ffn_backward(
        collect(upstream.astype(jnp.bfloat16)), hidden_two, w_up, w_down, activated, gelu_back
    )
    back_two, pair_two = norm_backward(settle(grad_hidden), normed_two, inv_two, norm_two)
    upstream = upstream + back_two
    grad_hidden, grad_in, grad_out = attend_backward(
        collect(upstream.astype(jnp.bfloat16)), hidden, w_in, w_out, kept, seq_count
    )
    back_one, pair_one = norm_backward(settle(grad_hidden), normed_one, inv_one, norm_one)
    return (upstream + back_one, (grad_in, grad_out, grad_up, grad_down), pair_one, pair_two)


def adamw(weight, gradient, moment_one, moment_two, factor, step_rate):
    gradient = gradient * factor
    moment_one = BETA_ONE * moment_one + (1.0 - BETA_ONE) * gradient
    moment_two = BETA_TWO * moment_two + (1.0 - BETA_TWO) * gradient * gradient
    adam_step = (
        moment_one
        / (1.0 - BETA_ONE**STEP)
        / (jnp.sqrt(moment_two / (1.0 - BETA_TWO**STEP)) + ADAM_FLOOR)
    )
    return (weight - step_rate * (adam_step + WEIGHT_DECAY * weight), moment_one, moment_two)


def body(
    tokens,
    targets,
    lengths,
    table,
    table_first,
    table_second,
    attn_in,
    attn_in_first,
    attn_in_second,
    attn_out,
    attn_out_first,
    attn_out_second,
    ffn_up,
    ffn_up_first,
    ffn_up_second,
    ffn_down,
    ffn_down_first,
    ffn_down_second,
    norms,
    norms_first,
    norms_second,
):
    low_type = jnp.bfloat16
    w_table, w_in, w_out, w_up, w_down = (
        lax.all_gather(table.astype(low_type), "dp", axis=0, tiled=True),
        lax.all_gather(attn_in.astype(low_type), "dp", axis=1, tiled=True),
        lax.all_gather(attn_out.astype(low_type), "dp", axis=3, tiled=True),
        lax.all_gather(ffn_up.astype(low_type), "dp", axis=1, tiled=True),
        lax.all_gather(ffn_down.astype(low_type), "dp", axis=2, tiled=True),
    )
    seq_count, length_all = tokens.shape
    row_count = seq_count * length_all
    full_width, vocab_size = w_table.shape
    layer_total = w_in.shape[0]
    vocab_ids = jnp.arange(vocab_size, dtype=jnp.int32) + lax.axis_index("head") * vocab_size
    token_hot = (tokens.reshape(row_count, 1) == vocab_ids[None, :]).astype(low_type)
    target_hot = targets.reshape(row_count, 1) == vocab_ids[None, :]
    positions = jnp.arange(length_all, dtype=jnp.int32)
    counted = (positions[None, :] < lengths[:, None]).astype(jnp.float32).reshape(row_count)
    embed_scale = math.sqrt(full_width)
    stream = settle(
        lax.dot_general(token_hot, w_table, COLS_CONTRACT, preferred_element_type=jnp.float32)
        * embed_scale
    )
    inputs = []
    for layer_at in range(layer_total):
        inputs.append(stream)
        stream, unused = layer_forward(
            stream,
            (w_in[layer_at], w_out[layer_at], w_up[layer_at], w_down[layer_at]),
            norms[2 * layer_at],
            norms[2 * layer_at + 1],
            seq_count,
        )
    final_rows, final_normed, final_inv = norm_forward(stream, norms[2 * layer_total])
    vocabulary_score_lines = jnp.dot(final_rows, w_table, preferred_element_type=jnp.float32)
    top_logit = jnp.max(vocabulary_score_lines, 1)
    picked = jnp.sum(jnp.where(target_hot, vocabulary_score_lines, 0.0), 1)
    top_logit = lax.pmax(top_logit, "head")
    exp_total, picked = lax.psum(
        (jnp.sum(jnp.exp(vocabulary_score_lines - top_logit[:, None]), 1), picked), "head"
    )
    log_total = top_logit + jnp.log(exp_total)
    loss_sum = jnp.sum((log_total - picked) * counted)
    score_derivative = (
        (jnp.exp(vocabulary_score_lines - log_total[:, None]) - target_hot.astype(jnp.float32))
        * counted[:, None]
    ).astype(low_type)
    grad_table = lax.dot_general(
        final_rows, score_derivative, ROWS_CONTRACT, preferred_element_type=jnp.float32
    )
    grad_final = settle(
        lax.dot_general(
            score_derivative, w_table, COLS_CONTRACT, preferred_element_type=jnp.float32
        )
    )
    upstream, final_pair = norm_backward(
        grad_final, final_normed, final_inv, norms[2 * layer_total]
    )
    pair_grads = [final_pair] * (2 * layer_total + 1)
    layer_grads = [None] * layer_total
    for layer_at in reversed(range(layer_total)):
        upstream, weight_grads, pair_one, pair_two = layer_backward(
            inputs[layer_at],
            upstream,
            (w_in[layer_at], w_out[layer_at], w_up[layer_at], w_down[layer_at]),
            norms[2 * layer_at],
            norms[2 * layer_at + 1],
            seq_count,
        )
        layer_grads[layer_at] = weight_grads
        pair_grads[2 * layer_at] = pair_one
        pair_grads[2 * layer_at + 1] = pair_two
    grad_table = grad_table + embed_scale * lax.dot_general(
        collect(upstream.astype(low_type)),
        token_hot,
        ROWS_CONTRACT,
        preferred_element_type=jnp.float32,
    )
    stacked = [jnp.stack([layer_set[member] for layer_set in layer_grads]) for member in range(4)]
    grad_table, grad_in, grad_out, grad_up, grad_down = (
        lax.psum_scatter(grad_table, "dp", scatter_dimension=0, tiled=True),
        lax.psum_scatter(stacked[0], "dp", scatter_dimension=1, tiled=True),
        lax.psum_scatter(stacked[1], "dp", scatter_dimension=3, tiled=True),
        lax.psum_scatter(stacked[2], "dp", scatter_dimension=1, tiled=True),
        lax.psum_scatter(stacked[3], "dp", scatter_dimension=2, tiled=True),
    )
    grad_norms = lax.psum(jnp.stack(pair_grads), "dp")
    matrices = (grad_table, grad_in, grad_out, grad_up, grad_down)
    squares = sum((jnp.sum(member_grad * member_grad) for member_grad in matrices)) + jnp.sum(
        grad_norms * grad_norms
    ) / lax.axis_size("dp")
    head_count = lax.axis_size("head")
    squares, loss_total, count_total = lax.psum(
        (squares, loss_sum / head_count, jnp.sum(counted) / head_count), ("dp", "head")
    )
    grad_norm = jnp.sqrt(squares)
    factor = jnp.minimum(1.0, CLIP_LIMIT / (grad_norm + 1e-06))
    refreshed_table, table_one, table_two = adamw(
        table, grad_table, table_first, table_second, factor, RATE_MATRIX
    )
    in_new, in_one, in_two = adamw(
        attn_in, grad_in, attn_in_first, attn_in_second, factor, RATE_MATRIX
    )
    out_new, out_one, out_two = adamw(
        attn_out, grad_out, attn_out_first, attn_out_second, factor, RATE_MATRIX
    )
    up_new, up_one, up_two = adamw(
        ffn_up, grad_up, ffn_up_first, ffn_up_second, factor, RATE_MATRIX
    )
    down_new, down_one, down_two = adamw(
        ffn_down, grad_down, ffn_down_first, ffn_down_second, factor, RATE_MATRIX
    )
    norms_new, norms_one, norms_two = adamw(
        norms, grad_norms, norms_first, norms_second, factor, RATE_NORM
    )
    return (
        jnp.stack([loss_total, count_total]),
        grad_norm,
        refreshed_table,
        refreshed_table.astype(low_type),
        table_one,
        table_two,
        in_new,
        in_new.astype(low_type),
        in_one,
        in_two,
        out_new,
        out_new.astype(low_type),
        out_one,
        out_two,
        up_new,
        up_new.astype(low_type),
        up_one,
        up_two,
        down_new,
        down_new.astype(low_type),
        down_one,
        down_two,
        norms_new,
        norms_one,
        norms_two,
    )


def solution(mesh):
    return jax.shard_map(
        body,
        mesh=mesh,
        in_specs=(
            P("dp", None),
            P("dp", None),
            P("dp"),
            P("dp", "head"),
            P("dp", "head"),
            P("dp", "head"),
            P(None, "dp", "head", None),
            P(None, "dp", "head", None),
            P(None, "dp", "head", None),
            P(None, "head", None, "dp"),
            P(None, "head", None, "dp"),
            P(None, "head", None, "dp"),
            P(None, "dp", "head"),
            P(None, "dp", "head"),
            P(None, "dp", "head"),
            P(None, "head", "dp"),
            P(None, "head", "dp"),
            P(None, "head", "dp"),
            P(None, None, "head"),
            P(None, None, "head"),
            P(None, None, "head"),
        ),
        out_specs=(
            P(),
            P(),
            P("dp", "head"),
            P("dp", "head"),
            P("dp", "head"),
            P("dp", "head"),
            P(None, "dp", "head", None),
            P(None, "dp", "head", None),
            P(None, "dp", "head", None),
            P(None, "dp", "head", None),
            P(None, "head", None, "dp"),
            P(None, "head", None, "dp"),
            P(None, "head", None, "dp"),
            P(None, "head", None, "dp"),
            P(None, "dp", "head"),
            P(None, "dp", "head"),
            P(None, "dp", "head"),
            P(None, "dp", "head"),
            P(None, "head", "dp"),
            P(None, "head", "dp"),
            P(None, "head", "dp"),
            P(None, "head", "dp"),
            P(None, None, "head"),
            P(None, None, "head"),
            P(None, None, "head"),
        ),
        check_vma=False,
    )
```

profile of v0, /device:TPU:0, one launch (start us, length us, event | category | flops | bytes accessed | tf_op | source)
XLA Modules:
  0.0 2122.9 jit_solution(1845311449914283263)
XLA Ops:
  10.0 128.4 %all-gather.19.cloned.1.call-done = bf16[512,8192]{1,0:T(8,128)(2,1)} async-done(((bf16[64,8192]{1,0:T(8,128)(2,1)}), bf16[512,8192]{1,0:T(8,128)(2,1)}) %all-gather.19.cloned.1.call-update) | async-done | bytes 8388624 | tf_op jit(solution)/shard_map/all_gather | solution.py:326
  153.6 21.6 %reduce-scatter.52.cloned.1.call-done = bf16[128,1024]{1,0:T(8,128)(2,1)} async-done(((bf16[512,1024]{1,0:T(8,128)(2,1)}), bf16[128,1024]{1,0:T(8,128)(2,1)}) %reduce-scatter.52.cloned.1.call-update) | async-done | bytes 262160
  183.8 34.1 %all_gather.66 = bf16[3,2,64,512]{2,1,0,3:T(2,128)(2,1)S(1)} all-gather(bf16[3,2,64,64]{2,1,0,3:T(2,128)(2,1)S(1)} %copy.477), channel_id=1, replica_groups=mesh['dp'=8,'head'=4] {'dp'}, dimensions={3}, use_global_device_ids=true | all-gather | bytes 442368 | tf_op jit(solution)/shard_map/all_gather | solution.py:328
  274.1 24.2 %reduce-scatter.54.cloned.1.call-done = bf16[128,1024]{1,0:T(8,128)(2,1)} async-done(((bf16[512,1024]{1,0:T(8,128)(2,1)}), bf16[128,1024]{1,0:T(8,128)(2,1)}) %reduce-scatter.54.cloned.1.call-update) | async-done | bytes 262160
  318.0 27.1 %all-gather.27.cloned.1.call-done = bf16[3,512,512]{2,1,0:T(8,128)(2,1)} async-done(((bf16[3,64,512]{2,1,0:T(8,128)(2,1)}), bf16[3,512,512]{2,1,0:T(8,128)(2,1)}) %all-gather.27.cloned.1.call-update) | async-done | bytes 1572880 | tf_op jit(solution)/shard_map/all_gather | solution.py:329
  345.1 17.8 all-gather.25.cloned.1.call-done
  366.3 43.6 %all-gather.29.cloned.1.call-done = bf16[3,512,512]{1,2,0:T(8,128)(2,1)} async-done(((bf16[3,512,64]{1,2,0:T(8,128)(2,1)}), bf16[3,512,512]{1,2,0:T(8,128)(2,1)}) %all-gather.29.cloned.1.call-update) | async-done | bytes 1572880 | tf_op jit(solution)/shard_map/all_gather | solution.py:330
  413.8 23.8 %reduce-scatter.56.cloned.1.call-done = bf16[128,1024]{1,0:T(8,128)(2,1)} async-done(((bf16[512,1024]{1,0:T(8,128)(2,1)}), bf16[128,1024]{1,0:T(8,128)(2,1)}) %reduce-scatter.56.cloned.1.call-update) | async-done | bytes 262160
  503.0 25.0 %reduce-scatter.58.cloned.1.call-done = bf16[128,1024]{1,0:T(8,128)(2,1)} async-done(((bf16[512,1024]{1,0:T(8,128)(2,1)}), bf16[128,1024]{1,0:T(8,128)(2,1)}) %reduce-scatter.58.cloned.1.call-update) | async-done | bytes 262160
  536.7 17.9 all-gather.33.cloned.1.call-done
  563.3 25.0 %reduce-scatter.60.cloned.1.call-done = bf16[128,1024]{1,0:T(8,128)(2,1)} async-done(((bf16[512,1024]{1,0:T(8,128)(2,1)}), bf16[128,1024]{1,0:T(8,128)(2,1)}) %reduce-scatter.60.cloned.1.call-update) | async-done | bytes 262160
  662.9 25.0 %reduce-scatter.62.cloned.1.call-done = bf16[128,1024]{1,0:T(8,128)(2,1)} async-done(((bf16[512,1024]{1,0:T(8,128)(2,1)}), bf16[128,1024]{1,0:T(8,128)(2,1)}) %reduce-scatter.62.cloned.1.call-update) | async-done | bytes 262160
  723.1 25.0 %reduce-scatter.64.cloned.1.call-done = bf16[128,1024]{1,0:T(8,128)(2,1)} async-done(((bf16[512,1024]{1,0:T(8,128)(2,1)}), bf16[128,1024]{1,0:T(8,128)(2,1)}) %reduce-scatter.64.cloned.1.call-update) | async-done | bytes 262160
  775.4 17.7 fusion.439
  821.0 20.4 fusion.10
  859.4 26.3 %reduce-scatter.66.cloned.1.call-done = bf16[128,1024]{1,0:T(8,128)(2,1)} async-done(((bf16[512,1024]{1,0:T(8,128)(2,1)}), bf16[128,1024]{1,0:T(8,128)(2,1)}) %reduce-scatter.66.cloned.1.call-update) | async-done | bytes 262160
  898.8 18.1 all-gather.41.cloned.1.call-done
  926.9 25.0 %reduce-scatter.68.cloned.1.call-done = bf16[128,1024]{1,0:T(8,128)(2,1)} async-done(((bf16[512,1024]{1,0:T(8,128)(2,1)}), bf16[128,1024]{1,0:T(8,128)(2,1)}) %reduce-scatter.68.cloned.1.call-update) | async-done | bytes 262160
  1021.7 25.0 %reduce-scatter.70.cloned.1.call-done = bf16[128,1024]{1,0:T(8,128)(2,1)} async-done(((bf16[512,1024]{1,0:T(8,128)(2,1)}), bf16[128,1024]{1,0:T(8,128)(2,1)}) %reduce-scatter.70.cloned.1.call-update) | async-done | bytes 262160
  1057.4 18.1 all-gather.45.cloned.1.call-done
  1085.5 25.0 %reduce-scatter.72.cloned.1.call-done = bf16[128,1024]{1,0:T(8,128)(2,1)} async-done(((bf16[512,1024]{1,0:T(8,128)(2,1)}), bf16[128,1024]{1,0:T(8,128)(2,1)}) %reduce-scatter.72.cloned.1.call-update) | async-done | bytes 262160
  1120.1 18.1 all-gather.47.cloned.1.call-done
  1172.2 25.0 %reduce-scatter.74.cloned.1.call-done = bf16[128,1024]{1,0:T(8,128)(2,1)} async-done(((bf16[512,1024]{1,0:T(8,128)(2,1)}), bf16[128,1024]{1,0:T(8,128)(2,1)}) %reduce-scatter.74.cloned.1.call-update) | async-done | bytes 262160
  1207.8 18.1 all-gather.49.cloned.1.call-done
  1235.8 25.0 %reduce-scatter.76.cloned.1.call-done = bf16[128,1024]{1,0:T(8,128)(2,1)} async-done(((bf16[512,1024]{1,0:T(8,128)(2,1)}), bf16[128,1024]{1,0:T(8,128)(2,1)}) %reduce-scatter.76.cloned.1.call-update) | async-done | bytes 262160
  1272.0 18.1 all-gather.51.cloned.1.call-done
  1320.0 25.0 %reduce-scatter.78.cloned.1.call-done = bf16[128,1024]{1,0:T(8,128)(2,1)} async-done(((bf16[512,1024]{1,0:T(8,128)(2,1)}), bf16[128,1024]{1,0:T(8,128)(2,1)}) %reduce-scatter.78.cloned.1.call-update) | async-done | bytes 262160
  1447.5 20.2 psum.306
  1469.0 52.9 %reduce-scatter.50.cloned.1.call-done = f32[3,64,512]{2,1,0:T(8,128)} async-done(((f32[3,512,512]{2,1,0:T(8,128)}), f32[3,64,512]{2,1,0:T(8,128)}) %reduce-scatter.50.cloned.1.call-update) | async-done | bytes 393232 | tf_op jit(solution)/shard_map/reduce_scatter | solution.py:406
  1523.6 244.4 %all-reduce.20.cloned.1.call-done = (f32[3,512,2,224]{3,2,0,1:T(2,128)}, f32[3,512,512]{1,0,2:T(4,128)}) async-done(((f32[3,512,2,224]{3,2,0,1:T(2,128)}, f32[3,512,512]{1,0,2:T(4,128)}), (f32[3,512,2,224]{3,2,0,1:T(2,128)}, f32[3,512,512]{1,0,2:T(4,128)})) %all-reduce.20.cloned.1.call-update) | async-done | bytes 5898256
  1771.9 280.7 %reduce-scatter.48.cloned.1.call-done = f32[64,8192]{1,0:T(8,128)} async-done(((f32[512,8192]{1,0:T(8,128)}), f32[64,8192]{1,0:T(8,128)}) %reduce-scatter.48.cloned.1.call-update) | async-done | bytes 2097168 | tf_op jit(solution)/shard_map/reduce_scatter | solution.py:403
  2058.6 40.4 %all-reduce.2 = (f32[1]{0:T(128)}, f32[1]{0:T(128)}, f32[]{:T(128)}) all-reduce(f32[1]{0:T(128)} %bitcast.105, f32[1]{0:T(128)} %bitcast.104, f32[]{:T(128)S(6)} %add.1006), channel_id=1, replica_groups=mesh['dp'=8,'head'=4] {'dp','head'}, use_global_device_ids=true, to_apply=%region_149.150 | all-reduce | flops 3 | bytes 24 | tf_op jit(solution)/shard_map/psum | solution.py:415
  (1533 shorter events, 711.7 us)
Async XLA Ops:
  7.2 131.2 %all-gather.19.cloned.1.call-start = ((), (), s32[]{:S(2)}) async-start(), calls=%async_computation.17 | async-start | bytes 9437184 | tf_op jit(solution)/shard_map/all_gather | solution.py:326
  10.0 165.3 %reduce-scatter.52.cloned.1.call-start = ((), (), s32[]{:S(2)}) async-start(), calls=%async_computation.37 | async-start | bytes 1310720
  152.0 74.7 %all-gather.23.cloned.1.call-start = ((), (), s32[]{:S(2)}) async-start(), calls=%async_computation.19 | async-start | bytes 1769472 | tf_op jit(solution)/shard_map/all_gather | solution.py:327
  152.9 92.7 %all-gather.21.cloned.1.call-start = ((), (), s32[]{:S(2)}) async-start(), calls=%async_computation.18 | async-start | bytes 1310720 | tf_op jit(solution)/shard_map/all_gather | solution.py:72
  183.6 114.6 %reduce-scatter.54.cloned.1.call-start = ((), (), s32[]{:S(2)}) async-start(), calls=%async_computation.38 | async-start | bytes 1310720
  273.2 71.9 %all-gather.27.cloned.1.call-start = ((), (), s32[]{:S(2)}) async-start(), calls=%async_computation.21 | async-start | bytes 1769472 | tf_op jit(solution)/shard_map/all_gather | solution.py:329
  274.0 88.9 %all-gather.25.cloned.1.call-start = ((), (), s32[]{:S(2)}) async-start(), calls=%async_computation.20 | async-start | bytes 1310720 | tf_op jit(solution)/shard_map/all_gather | solution.py:72
  307.4 102.5 %all-gather.29.cloned.1.call-start = ((), (), s32[]{:S(2)}) async-start(), calls=%async_computation.22 | async-start | bytes 1769472 | tf_op jit(solution)/shard_map/all_gather | solution.py:330
  308.2 129.4 %reduce-scatter.56.cloned.1.call-start = ((), (), s32[]{:S(2)}) async-start(), calls=%async_computation.39 | async-start | bytes 1310720
  446.6 81.4 %reduce-scatter.58.cloned.1.call-start = ((), (), s32[]{:S(2)}) async-start(), calls=%async_computation.40 | async-start | bytes 1310720
  536.5 51.8 %reduce-scatter.60.cloned.1.call-start = ((), (), s32[]{:S(2)}) async-start(), calls=%async_computation.41 | async-start | bytes 1310720
  596.7 91.2 %reduce-scatter.62.cloned.1.call-start = ((), (), s32[]{:S(2)}) async-start(), calls=%async_computation.42 | async-start | bytes 1310720
  696.4 51.7 %reduce-scatter.64.cloned.1.call-start = ((), (), s32[]{:S(2)}) async-start(), calls=%async_computation.43 | async-start | bytes 1310720
  723.1 52.3 %all-gather.39.cloned.1.call-start = ((), (), s32[]{:S(2)}) async-start(), calls=%async_computation.27 | async-start | bytes 1310720 | tf_op jit(solution)/shard_map/all_gather | solution.py:72
  757.3 128.5 %reduce-scatter.66.cloned.1.call-start = ((), (), s32[]{:S(2)}) async-start(), calls=%async_computation.44 | async-start | bytes 1310720
  859.4 57.5 %all-gather.41.cloned.1.call-start = ((), (), s32[]{:S(2)}) async-start(), calls=%async_computation.28 | async-start | bytes 1310720 | tf_op jit(solution)/shard_map/all_gather | solution.py:72
  898.7 53.2 %reduce-scatter.68.cloned.1.call-start = ((), (), s32[]{:S(2)}) async-start(), calls=%async_computation.45 | async-start | bytes 1310720
  926.8 58.0 %all-gather.43.cloned.1.call-start = ((), (), s32[]{:S(2)}) async-start(), calls=%async_computation.29 | async-start | bytes 1310720 | tf_op jit(solution)/shard_map/all_gather | solution.py:72
  966.7 80.0 %reduce-scatter.70.cloned.1.call-start = ((), (), s32[]{:S(2)}) async-start(), calls=%async_computation.46 | async-start | bytes 1310720
  1021.7 53.8 %all-gather.45.cloned.1.call-start = ((), (), s32[]{:S(2)}) async-start(), calls=%async_computation.30 | async-start | bytes 1310720 | tf_op jit(solution)/shard_map/all_gather | solution.py:72
  1057.3 53.1 %reduce-scatter.72.cloned.1.call-start = ((), (), s32[]{:S(2)}) async-start(), calls=%async_computation.47 | async-start | bytes 1310720
  1085.4 52.8 %all-gather.47.cloned.1.call-start = ((), (), s32[]{:S(2)}) async-start(), calls=%async_computation.31 | async-start | bytes 1310720 | tf_op jit(solution)/shard_map/all_gather | solution.py:72
  1120.0 77.1 %reduce-scatter.74.cloned.1.call-start = ((), (), s32[]{:S(2)}) async-start(), calls=%async_computation.48 | async-start | bytes 1310720
  1172.2 53.7 %all-gather.49.cloned.1.call-start = ((), (), s32[]{:S(2)}) async-start(), calls=%async_computation.32 | async-start | bytes 1310720 | tf_op jit(solution)/shard_map/all_gather | solution.py:72
  1207.8 53.0 %reduce-scatter.76.cloned.1.call-start = ((), (), s32[]{:S(2)}) async-start(), calls=%async_computation.49 | async-start | bytes 1310720
  1235.8 54.3 %all-gather.51.cloned.1.call-start = ((), (), s32[]{:S(2)}) async-start(), calls=%async_computation.33 | async-start | bytes 1310720 | tf_op jit(solution)/shard_map/all_gather | solution.py:72
  1272.0 73.0 %reduce-scatter.78.cloned.1.call-start = ((), (), s32[]{:S(2)}) async-start(), calls=%async_computation.50 | async-start | bytes 1310720
  1319.9 97.7 %all-gather.53.cloned.1.call-start = ((), (), s32[]{:S(2)}) async-start(), calls=%async_computation.34 | async-start | bytes 1310720 | tf_op jit(solution)/shard_map/all_gather | solution.py:72
  1359.7 83.8 %reduce-scatter.80.cloned.1.call-start = ((), (), s32[]{:S(2)}) async-start(), calls=%async_computation.51 | async-start | bytes 884736
  1365.6 156.2 %reduce-scatter.50.cloned.1.call-start = ((), (), s32[]{:S(2)}) async-start(), calls=%async_computation.36 | async-start | bytes 3538944 | tf_op jit(solution)/shard_map/reduce_scatter | solution.py:406
  1372.3 395.7 %all-reduce.20.cloned.1.call-start = ((), (), s32[]{:S(2)}) async-start(), calls=%async_computation.52 | async-start | bytes 14680064
  1400.6 652.0 %reduce-scatter.48.cloned.1.call-start = ((), (), s32[]{:S(2)}) async-start(), calls=%async_computation.35 | async-start | bytes 18874368 | tf_op jit(solution)/shard_map/reduce_scatter | solution.py:403
  (433 other events, 5660.6 us)
Sparse Core Ops, SparseCore 0:
  10.7 127.6 all-gather.18
  152.1 23.0 reduce-scatter.51
  178.2 48.4 all-gather.22
  273.3 24.8 reduce-scatter.53
  300.9 44.1 all-gather.26
  365.7 44.1 all-gather.28
  413.9 23.6 reduce-scatter.55
  446.8 17.9 all-gather.30
  503.1 24.8 reduce-scatter.57
  536.6 17.9 all-gather.32
  563.3 24.8 reduce-scatter.59
  596.9 17.9 all-gather.34
  663.0 24.8 reduce-scatter.61
  723.2 24.8 reduce-scatter.63
  757.4 17.9 all-gather.38
  859.5 26.2 reduce-scatter.65
  898.8 17.9 all-gather.40
  927.0 24.8 reduce-scatter.67
  966.8 17.9 all-gather.42
  1021.8 24.8 reduce-scatter.69
  1057.5 17.9 all-gather.44
  1085.5 24.8 reduce-scatter.71
  1120.2 17.9 all-gather.46
  1172.3 24.8 reduce-scatter.73
  1235.9 24.8 reduce-scatter.75
  1272.1 17.9 all-gather.50
  1320.0 24.8 reduce-scatter.77
  1359.8 17.9 all-gather.52
  1381.0 62.5 reduce-scatter.79
  1447.6 74.2 reduce-scatter.49
  1526.5 241.4 all-reduce.19
  1771.6 280.9 reduce-scatter.47
  (4 shorter events, 68.1 us)
where the time goes:
time: 2140 us; the launch traced here: 2120 us
  waiting for transfers between devices  1360 us (64%)
  matrix products  214 us (10%)
  blocking collectives  195 us (9%)
  other arithmetic  158 us (7%)
  local copies, waits for them, and re-layouts  151 us (7%)
  between operations  29.4 us (1%)
    unnamed x52, waiting for transfers between devices  597 us
    reduce_scatter x1, waiting for transfers between devices, body(): lax.psum_scatter(grad_table, 'dp', scatter_dimension=0, tiled=True)  281 us
    all_gather x14, waiting for transfers between devices, collect(): return lax.all_gather(piece, 'head', axis=1, tiled=True)  226 us
    all_gather x1, waiting for transfers between devices, body(): lax.all_gather(table.astype(low_type), 'dp', axis=0, tiled=True)  128 us
    unnamed x903, local copies, waits for them, and re-layouts  98.4 us
    psum x13, blocking collectives, row_sums(): return lax.psum((jnp.sum(left_term, 1), jnp.sum(right_term, 1)), 'head')  78.1 us
    reduce_scatter x1, waiting for transfers between devices, body(): lax.psum_scatter(stacked[2], 'dp', scatter_dimension=1, tiled=True)  52.9 us
    all_gather x1, waiting for transfers between devices, body(): lax.all_gather(ffn_down.astype(low_type), 'dp', axis=2, tiled=True)  43.6 us
  transfers between devices with their start and end apart: 36, of which 35 were waited for; matrix products, arithmetic and copies ran while one was open for 5% of the time, Pallas kernels for 0%

commit v1 on v0

v1 whole, which is shorter than its diff:
```python
import functools
import math

import jax
import jax.numpy as jnp
from jax import lax
from jax.experimental import pallas as pl
from jax.experimental.pallas import tpu as pltpu
from jax.sharding import PartitionSpec as P

HD = 64
BLOCK = 32
SINK = 8
STEP = 10
EPSILON = 1e-05
NEGATIVE = -1000000000.0
TEMPER = 0.75
BETA_ONE = 0.9
BETA_TWO = 0.999
ADAM_FLOOR = 1e-08
WEIGHT_DECAY = 0.01
RATE_MATRIX = 0.1
RATE_NORM = 0.5
CLIP_LIMIT = 1.0

BF = jnp.bfloat16
F32 = jnp.float32
GROUP = 2
GELU_C = math.sqrt(2.0 / math.pi)
GELU_A = 0.044715

C_Q = (0, 128)
C_KVS = (128, 512)
C_OUT = (512, 640)
C_UP = (640, 1152)
C_DOWN = (1152, 1664)
PACKED = 1664
VMEM_LIMIT = 56 * 1024 * 1024


def dot_nn(a, b):
    return lax.dot_general(a, b, (((1,), (0,)), ((), ())), preferred_element_type=F32)


def dot_nt(a, b):
    return lax.dot_general(a, b, (((1,), (1,)), ((), ())), preferred_element_type=F32)


def dot_tn(a, b):
    return lax.dot_general(a, b, (((0,), (0,)), ((), ())), preferred_element_type=F32)


def iota(shape, axis):
    return lax.broadcasted_iota(jnp.int32, shape, axis)


def norm_stats(stream):
    average = jnp.mean(stream, -1, keepdims=True)
    variance = jnp.mean(stream * stream, -1, keepdims=True) - average * average
    inv_std = lax.rsqrt(variance + EPSILON)
    return (stream - average) * inv_std, inv_std


def norm_apply(stream, gain, bias):
    normed, _ = norm_stats(stream)
    return (normed * gain + bias).astype(BF)


def norm_back(upstream, stream, gain):
    normed, inv_std = norm_stats(stream)
    scaled = upstream * gain
    back = inv_std * (
        scaled
        - jnp.mean(scaled, -1, keepdims=True)
        - normed * jnp.mean(scaled * normed, -1, keepdims=True)
    )
    pair = jnp.concatenate(
        [jnp.sum(upstream * normed, 0, keepdims=True), jnp.sum(upstream, 0, keepdims=True)], 0
    )
    return back, pair


def allowed_mask(shape):
    return iota(shape, len(shape) - 1) < iota(shape, len(shape) - 2)


def log_total(x, axis):
    top = jnp.max(x, axis, keepdims=True)
    return top + jnp.log(jnp.sum(jnp.exp(x - top), axis, keepdims=True))


def balance(scores, keep):
    allowed = allowed_mask(scores.shape)
    plan = jnp.where(allowed, scores / TEMPER, NEGATIVE)
    for _ in range(SINK):
        for axis in (-2, -1):
            plan = jnp.where(allowed, plan - log_total(plan, axis), NEGATIVE)
            if keep is not None:
                keep.append(plan)
    return jnp.where(allowed, jnp.exp(plan), 0.0)


def balance_back(scores, upstream):
    allowed = allowed_mask(scores.shape)
    plans = []
    perm = balance(scores, plans)
    grad = jnp.where(allowed, upstream * perm, 0.0)
    for step in reversed(range(2 * SINK)):
        axis = (-2, -1)[step % 2]
        share = jnp.exp(plans[step])
        grad = jnp.where(allowed, grad - share * jnp.sum(grad, axis, keepdims=True), 0.0)
    return grad / TEMPER


def kron_rows(perm_rows, length):
    own, blocks = perm_rows.shape
    rows = own * BLOCK
    tall = jnp.broadcast_to(perm_rows[:, None, :], (own, BLOCK, blocks)).reshape(rows, blocks)
    spread = (iota((blocks, length), 1) // BLOCK == iota((blocks, length), 0)).astype(BF)
    wide = dot_nn(tall.astype(BF), spread)
    same = (iota((rows, length), 0) & (BLOCK - 1)) == (iota((rows, length), 1) & (BLOCK - 1))
    return jnp.where(same, wide, 0.0).astype(BF)


def group_mask(first_block, rows):
    shape = (rows, 2 * rows)
    row, slot = iota(shape, 0), iota(shape, 1)
    row_block = row // BLOCK
    in_sorted = slot < rows
    place = jnp.where(in_sorted, slot, slot - rows)
    same = (place // BLOCK) == row_block
    sorted_ok = in_sorted & (row_block + first_block >= 1)
    own_ok = (slot >= rows) & (place <= row)
    return same & (sorted_ok | own_ok)


def load_weights(pieces, w_ref, sems):
    copies = [pltpu.make_async_copy(piece, w_ref.at[p], sems.at[p]) for p, piece in enumerate(pieces)]
    for copy in copies:
        copy.start()
    return copies


def forward_kernel(
    me_ref, hid0_ref, hid1_ref, hid2in_ref, hid3_ref, stream_ref, w0_ref, w1_ref, w2_ref, w3_ref, nrm_ref,
    stream_out, mid_out, hnext_out, hid_ref, kv_out, q_out, skv_out, attw_out, mixed_out,
    permo_out, sort_out, hid2_out, upw_out, act_out,
    w_ref, perm_scr, acc_scr, sems,
):
    length, width = hid_ref.shape
    rows = stream_ref.shape[0]
    pairs = w_ref.shape[0]
    own_blocks = rows // BLOCK
    blocks = length // BLOCK
    my = me_ref[0]
    own = pl.multiple_of(my * rows, rows)
    own_block = pl.multiple_of(my * own_blocks, own_blocks)
    lower = iota((1, 128), 1) < HD
    copies = load_weights((w0_ref, w1_ref, w2_ref, w3_ref), w_ref, sems)
    for p, piece in enumerate((hid0_ref, hid1_ref, hid2in_ref, hid3_ref)):
        hid_ref[pl.ds(pl.multiple_of((my ^ p) * rows, rows), rows), :] = piece[...]
    for copy in copies:
        copy.wait()

    def project(step, _):
        j, tile = step // (length // rows), step % (length // rows)
        at = pl.multiple_of(tile * rows, rows)
        w = w_ref[j, :, :, C_KVS[0]:C_KVS[1]].reshape(width, C_KVS[1] - C_KVS[0])
        got = dot_nn(hid_ref[pl.ds(at, rows), :], w)
        kv_out[j, pl.ds(at, rows), :] = got[:, :256].astype(BF)
        sort_out[j, pl.ds(pl.multiple_of(tile * own_blocks, own_blocks), own_blocks), :] = jnp.sum(
            got[:, 256:].reshape(own_blocks, BLOCK, 128), 1
        ) / math.sqrt(BLOCK)
        return 0

    lax.fori_loop(0, pairs * (length // rows), project, 0)

    scores = jnp.stack(
        [sort_out[h // 2][:, (h % 2) * BLOCK:(h % 2) * BLOCK + blocks] for h in range(2 * pairs)]
    )
    perm_scr[...] = balance(scores, None)
    permo_out[...] = perm_scr[:, pl.ds(own_block, own_blocks), :]
    acc_scr[...] = stream_ref[...]
    take = GROUP * BLOCK

    def attend(j, _):
        wq = w_ref[j, :, :, C_Q[0]:C_Q[1]].reshape(width, 128)
        q = dot_nn(hid_ref[pl.ds(own, rows), :], wq).astype(BF)
        q_out[j] = q
        mixes = []
        for h in range(2):
            kron = kron_rows(permo_out[2 * j + h], length)
            skv = dot_nn(kron, kv_out[j, :, h * 128:(h + 1) * 128]).astype(BF)
            skv_out[j, h] = skv
            q_mine = jnp.where(lower if h == 0 else ~lower, q, jnp.zeros_like(q))
            kv_own = kv_out[j, pl.ds(own, rows), h * 128:(h + 1) * 128]
            pieces = []
            for g in range(rows // take):
                cut = slice(g * take, (g + 1) * take)
                kv_set = jnp.concatenate([skv[cut], kv_own[cut]], 0)
                raw = dot_nt(q_mine[cut], kv_set) * (1.0 / math.sqrt(HD))
                raw = jnp.where(group_mask(own_block + g * GROUP, take), raw, NEGATIVE)
                grown = jnp.exp(raw - jnp.max(raw, -1, keepdims=True))
                share = grown / jnp.sum(grown, -1, keepdims=True)
                attw_out[j, h, cut, :] = share
                pieces.append(dot_nn(share.astype(BF), kv_set))
            mixes.append(jnp.concatenate(pieces, 0))
        mixed = jnp.where(lower, mixes[1], mixes[0]).astype(BF)
        mixed_out[j] = mixed
        w_o = w_ref[j, :, :, C_OUT[0]:C_OUT[1]].reshape(width, 128)
        acc_scr[...] += dot_nt(mixed, w_o)
        return 0

    lax.fori_loop(0, pairs, attend, 0)

    middle = acc_scr[...]
    mid_out[...] = middle
    hid2_out[...] = norm_apply(middle, nrm_ref[0:1, :], nrm_ref[1:2, :])

    def feed(j, _):
        w_up = w_ref[j, :, :, C_UP[0]:C_UP[1]].reshape(width, 512)
        upward = dot_nn(hid2_out[...], w_up)
        upw_out[j] = upward
        bent = jnp.tanh(GELU_C * (upward + GELU_A * upward * upward * upward))
        act = (0.5 * upward * (1.0 + bent)).astype(BF)
        act_out[j] = act
        w_dn = w_ref[j, :, :, C_DOWN[0]:C_DOWN[1]].reshape(width, 512)
        acc_scr[...] += dot_nt(act, w_dn)
        return 0

    lax.fori_loop(0, pairs, feed, 0)
    result = acc_scr[...]
    stream_out[...] = result
    hnext_out[...] = norm_apply(result, nrm_ref[2:3, :], nrm_ref[3:4, :])


def ignore_tail(kernel, used, extra):
    def run(*refs):
        kernel(*refs[:used], *refs[used + extra:])
    return run


def layer_forward(me, hidden, stream, weights, nrm, after=()):
    rows, width = stream.shape
    pairs = len(hidden)
    length = rows * pairs
    own_blocks, blocks = rows // BLOCK, length // BLOCK
    shape = jax.ShapeDtypeStruct
    outs = [
        shape((rows, width), F32),
        shape((rows, width), F32),
        shape((rows, width), BF),
        shape((length, width), BF),
        shape((pairs, length, 256), BF),
        shape((pairs, rows, 128), BF),
        shape((pairs, 2, rows, 128), BF),
        shape((pairs, 2, rows, 2 * GROUP * BLOCK), F32),
        shape((pairs, rows, 128), BF),
        shape((2 * pairs, own_blocks, blocks), F32),
        shape((pairs, blocks, 128), F32),
        shape((rows, width), BF),
        shape((pairs, rows, 512), F32),
        shape((pairs, rows, 512), BF),
    ]
    vm = pl.BlockSpec(memory_space=pltpu.VMEM)
    far = pl.BlockSpec(memory_space=pl.ANY)
    return pl.pallas_call(
        ignore_tail(forward_kernel, 2 * pairs + 3, len(after)),
        out_shape=outs,
        in_specs=[pl.BlockSpec(memory_space=pltpu.SMEM)] + [vm] * (pairs + 1) + [far] * pairs + [vm]
        + [far] * len(after),
        out_specs=[vm] * len(outs),
        scratch_shapes=[
            pltpu.VMEM((pairs,) + weights[0].shape, BF),
            pltpu.VMEM((2 * pairs, blocks, blocks), F32),
            pltpu.VMEM((rows, width), F32),
            pltpu.SemaphoreType.DMA((pairs,)),
        ],
        compiler_params=pltpu.CompilerParams(vmem_limit_bytes=VMEM_LIMIT),
        cost_estimate=pl.CostEstimate(flops=20_000_000_000, bytes_accessed=18_000_000, transcendentals=0),
        name="layer_forward",
    )(me, *hidden, stream, *weights, nrm, *after)


def backward_kernel(
    me_ref, keep_ref, near_ref, far_ref, above_ref, carry_ref, gain_above_ref,
    w0_ref, w1_ref, w2_ref, w3_ref, gain_two_ref, mid_ref, hid_ref, kv_ref, q_ref, skv_ref, attw_ref,
    mixed_ref, permo_ref, sort_ref, hid2_ref, upw_ref, act_ref,
    gkeep_out, gsend_out, wkeep_out, wsend_out, carry_out, pair_above_out, pair_two_out,
    w_ref, acc_scr, ghid_scr, gkv_scr, gsrt_scr, gq_scr, dperm_scr, low_scr, wgrad_scr, sems,
):
    length, width = hid_ref.shape
    rows = carry_ref.shape[0]
    pairs, parts, depth = w_ref.shape[:3]
    own_blocks = rows // BLOCK
    blocks = length // BLOCK
    my = me_ref[0]
    own = pl.multiple_of(my * rows, rows)
    own_block = pl.multiple_of(my * own_blocks, own_blocks)
    lower = iota((1, 128), 1) < HD
    take = GROUP * BLOCK
    copies = load_weights((w0_ref, w1_ref, w2_ref, w3_ref), w_ref, sems)

    dy = keep_ref[0].astype(F32) + near_ref[0].astype(F32) + far_ref[...].astype(F32)
    back, pair = norm_back(dy, above_ref[...], gain_above_ref[...])
    pair_above_out[...] = pair
    upstream = carry_ref[...] + back
    carry_out[...] = upstream
    low_scr[...] = upstream.astype(BF)
    acc_scr[...] = jnp.zeros_like(acc_scr)
    for copy in copies:
        copy.wait()

    def put(j, columns, value):
        size = columns[1] - columns[0]
        wgrad_scr[j, :, :, columns[0]:columns[1]] = value.astype(BF).reshape(parts, depth, size)

    def feed(j, _):
        low = low_scr[...]
        w_dn = w_ref[j, :, :, C_DOWN[0]:C_DOWN[1]].reshape(width, 512)
        grad_act = dot_nn(low, w_dn)
        x = upw_ref[j]
        squared = x * x
        bent = jnp.tanh(GELU_C * (x + GELU_A * squared * x))
        slope = 0.5 * (1.0 + bent) + 0.5 * x * (1.0 - bent * bent) * (
            GELU_C * (1.0 + 3.0 * GELU_A * squared)
        )
        grad_up = (grad_act * slope).astype(BF)
        put(j, C_DOWN, dot_tn(low, act_ref[j]))
        put(j, C_UP, dot_tn(hid2_ref[...], grad_up))
        w_up = w_ref[j, :, :, C_UP[0]:C_UP[1]].reshape(width, 512)
        acc_scr[...] += dot_nt(grad_up, w_up)
        return 0

    lax.fori_loop(0, pairs, feed, 0)

    back, pair = norm_back(acc_scr[...], mid_ref[...], gain_two_ref[...])
    pair_two_out[...] = pair
    upstream = carry_out[...] + back
    carry_out[...] = upstream
    low_scr[...] = upstream.astype(BF)
    dperm_scr[...] = jnp.zeros_like(dperm_scr)
    scale_key = 1.0 / math.sqrt(HD)

    def attend(j, _):
        low = low_scr[...]
        w_o = w_ref[j, :, :, C_OUT[0]:C_OUT[1]].reshape(width, 128)
        grad_mixed = dot_nn(low, w_o).astype(BF)
        put(j, C_OUT, dot_tn(low, mixed_ref[j]))
        q = q_ref[j]
        zero = jnp.zeros_like(q)
        queries = []
        for h in range(2):
            key_lanes = lower if h == 0 else ~lower
            kron = kron_rows(permo_ref[2 * j + h], length)
            kv_all = kv_ref[j, :, h * 128:(h + 1) * 128]
            kv_own = kv_ref[j, pl.ds(own, rows), h * 128:(h + 1) * 128]
            skv = skv_ref[j, h]
            q_mine = jnp.where(key_lanes, q, zero)
            gm_mine = jnp.where(key_lanes, zero, grad_mixed)
            scale = jnp.where(key_lanes, scale_key, 1.0)
            gq, g_sorted, g_own = [], [], []
            for g in range(rows // take):
                cut = slice(g * take, (g + 1) * take)
                kv_set = jnp.concatenate([skv[cut], kv_own[cut]], 0)
                share = attw_ref[j, h, cut, :]
                grad_share = dot_nt(gm_mine[cut], kv_set)
                grad_raw = (
                    share * (grad_share - jnp.sum(share * grad_share, -1, keepdims=True))
                ).astype(BF)
                gq.append(dot_nn(grad_raw, kv_set) * scale_key)
                grad_set = (
                    dot_tn(grad_raw, q_mine[cut]) + dot_tn(share.astype(BF), gm_mine[cut])
                ) * scale
                g_sorted.append(grad_set[:take])
                g_own.append(grad_set[take:])
            queries.append(jnp.concatenate(gq, 0))
            grad_sorted = jnp.concatenate(g_sorted, 0).astype(BF)
            crossed = dot_nt(grad_sorted, kv_all)
            same = (iota((rows, length), 0) & (BLOCK - 1)) == (iota((rows, length), 1) & (BLOCK - 1))
            crossed = jnp.where(same, crossed, 0.0).reshape(own_blocks, BLOCK, length)
            dperm_scr[2 * j + h] = jnp.sum(crossed, 1)
            ghid_scr[:, 0:128] = dot_tn(kron, grad_sorted)
            ghid_scr[pl.ds(own, rows), 0:128] += jnp.concatenate(g_own, 0)
            gkv_scr[j, :, h * 128:(h + 1) * 128] = ghid_scr[:, 0:128].astype(BF)
        gq_scr[j] = jnp.where(lower, queries[0], queries[1]).astype(BF)
        return 0

    lax.fori_loop(0, pairs, attend, 0)

    heads = 2 * pairs
    gather = (iota((length, blocks), 0) // BLOCK == iota((length, blocks), 1)).astype(F32)
    dperm = lax.dot_general(
        dperm_scr[...].reshape(heads * own_blocks, length),
        gather,
        (((1,), (0,)), ((), ())),
        precision=lax.Precision.HIGHEST,
        preferred_element_type=F32,
    ).reshape(heads, own_blocks, blocks)
    scores = jnp.stack(
        [sort_ref[h // 2][:, (h % 2) * BLOCK:(h % 2) * BLOCK + blocks] for h in range(heads)]
    )
    full = jnp.concatenate([dperm] * (blocks // own_blocks), 1)
    block_at = iota(full.shape, 1)
    full = jnp.where((block_at >= own_block) & (block_at < own_block + own_blocks), full, 0.0)
    grad_sort = balance_back(scores, full) / math.sqrt(BLOCK)
    blank = jnp.zeros((blocks, 128 - 2 * blocks), F32)
    for j in range(pairs):
        gsrt_scr[j] = jnp.concatenate([grad_sort[2 * j], grad_sort[2 * j + 1], blank], 1)

    ghid_scr[...] = jnp.zeros_like(ghid_scr)

    def inward(j, _):
        w = w_ref[j, :, :, C_KVS[0]:C_KVS[1]].reshape(width, C_KVS[1] - C_KVS[0])
        spread = jnp.broadcast_to(gsrt_scr[j][:, None, :], (blocks, BLOCK, 128)).reshape(length, 128)
        grad = jnp.concatenate([gkv_scr[j], spread.astype(BF)], 1)
        put(j, C_KVS, dot_tn(hid_ref[...], grad))
        ghid_scr[...] += dot_nt(grad, w)
        wq = w_ref[j, :, :, C_Q[0]:C_Q[1]].reshape(width, 128)
        put(j, C_Q, dot_tn(hid_ref[pl.ds(own, rows), :], gq_scr[j]))
        ghid_scr[pl.ds(own, rows), :] += dot_nt(gq_scr[j], wq)
        return 0

    lax.fori_loop(0, pairs, inward, 0)
    for p in range(pairs):
        out = gsend_out if p & 1 else gkeep_out
        at = pl.multiple_of((my ^ p) * rows, rows)
        out[p >> 1] = ghid_scr[pl.ds(at, rows), :].astype(BF)
    outs = []
    for p in range(pairs):
        out = wsend_out if p & 1 else wkeep_out
        outs.append(pltpu.make_async_copy(wgrad_scr.at[p], out.at[p >> 1], sems.at[p]))
        outs[p].start()
    for copy in outs:
        copy.wait()


def layer_backward(me, dy, above, carry, gain_above, weights, gain_two, kept, after=()):
    rows, width = carry.shape
    pairs = len(weights)
    length = rows * pairs
    own_blocks, blocks = rows // BLOCK, length // BLOCK
    shape = jax.ShapeDtypeStruct
    outs = [
        shape((pairs // 2, rows, width), BF),
        shape((pairs // 2, rows, width), BF),
        shape((pairs // 2,) + weights[0].shape, BF),
        shape((pairs // 2,) + weights[0].shape, BF),
        shape((rows, width), F32),
        shape((2, width), F32),
        shape((2, width), F32),
    ]
    vm = pl.BlockSpec(memory_space=pltpu.VMEM)
    far = pl.BlockSpec(memory_space=pl.ANY)
    return pl.pallas_call(
        ignore_tail(backward_kernel, 8 + pairs + len(kept), len(after)),
        out_shape=outs,
        in_specs=[pl.BlockSpec(memory_space=pltpu.SMEM)] + [vm] * 6 + [far] * pairs
        + [vm] * (1 + len(kept)) + [far] * len(after),
        out_specs=[vm, vm, far, far, vm, vm, vm],
        scratch_shapes=[
            pltpu.VMEM((pairs,) + weights[0].shape, BF),
            pltpu.VMEM((rows, width), F32),
            pltpu.VMEM((length, width), F32),
            pltpu.VMEM((pairs, length, 256), BF),
            pltpu.VMEM((pairs, blocks, 128), F32),
            pltpu.VMEM((pairs, rows, 128), BF),
            pltpu.VMEM((2 * pairs, own_blocks, length), F32),
            pltpu.VMEM((rows, width), BF),
            pltpu.VMEM((pairs,) + weights[0].shape, BF),
            pltpu.SemaphoreType.DMA((pairs,)),
        ],
        compiler_params=pltpu.CompilerParams(vmem_limit_bytes=VMEM_LIMIT),
        cost_estimate=pl.CostEstimate(flops=30_000_000_000, bytes_accessed=25_000_000, transcendentals=0),
        name="layer_backward",
    )(me, *dy, above, carry, gain_above, *weights, gain_two, *kept, *after)


def embed_kernel(base_ref, tok_ref, table_ref, out_ref, tall_ref):
    features, vocab = table_ref.shape
    count = out_ref.shape[1]
    bins = vocab // 256

    @pl.when(pl.program_id(0) == 0)
    def _():
        for at in range(bins):
            tall_ref[at * features:(at + 1) * features, :] = table_ref[:, at * 256:(at + 1) * 256]

    local = tok_ref[...] - base_ref[0]
    high, low = local >> 8, local & 255
    hot = (iota((256, count), 0) == low).astype(BF)
    found = dot_nn(tall_ref[...], hot)
    total = jnp.zeros((features, count), F32)
    for at in range(bins):
        total = jnp.where(high == at, found[at * features:(at + 1) * features, :], total)
    out_ref[...] = total.astype(BF)


def embed_lookup(base, tokens, table):
    features, vocab = table.shape
    count = tokens.shape[1]
    tile = 512
    return pl.pallas_call(
        embed_kernel,
        grid=(count // tile,),
        out_shape=jax.ShapeDtypeStruct((features, count), BF),
        in_specs=[
            pl.BlockSpec(memory_space=pltpu.SMEM),
            pl.BlockSpec((1, tile), lambda i: (0, i)),
            pl.BlockSpec((features, vocab), lambda i: (0, 0)),
        ],
        out_specs=pl.BlockSpec((features, tile), lambda i: (0, i)),
        scratch_shapes=[pltpu.VMEM((features * (vocab // 256), 256), BF)],
        compiler_params=pltpu.CompilerParams(vmem_limit_bytes=VMEM_LIMIT),
        cost_estimate=pl.CostEstimate(flops=15_000_000_000, bytes_accessed=4_000_000, transcendentals=0),
        name="embed_lookup",
    )(base, tokens, table)


def embed_back_kernel(base_ref, tok_ref, grad_ref, out_ref, acc_ref):
    features = grad_ref.shape[0]
    count = grad_ref.shape[1]
    bins = acc_ref.shape[0] // features
    step = pl.program_id(0)
    local = tok_ref[...] - base_ref[0]
    high, low = local >> 8, local & 255
    hot = (iota((256, count), 0) == low).astype(BF)
    grad = grad_ref[...]
    wide = jnp.concatenate(
        [jnp.where(high == at, grad, jnp.zeros_like(grad)) for at in range(bins)], 0
    )
    found = dot_nt(wide, hot)

    @pl.when(step == 0)
    def _():
        acc_ref[...] = found

    @pl.when(step > 0)
    def _():
        acc_ref[...] += found

    @pl.when(step == pl.num_programs(0) - 1)
    def _():
        for at in range(bins):
            out_ref[:, at * 256:(at + 1) * 256] = acc_ref[at * features:(at + 1) * features, :]


def embed_back(base, tokens, grad, vocab):
    pieces, features, tile = grad.shape
    return pl.pallas_call(
        embed_back_kernel,
        grid=(pieces,),
        out_shape=jax.ShapeDtypeStruct((features, vocab), F32),
        in_specs=[
            pl.BlockSpec(memory_space=pltpu.SMEM),
            pl.BlockSpec((1, tile), lambda i: (0, i)),
            pl.BlockSpec((None, features, tile), lambda i: (i, 0, 0)),
        ],
        out_specs=pl.BlockSpec((features, vocab), lambda i: (0, 0)),
        scratch_shapes=[pltpu.VMEM((features * (vocab // 256), 256), F32)],
        compiler_params=pltpu.CompilerParams(vmem_limit_bytes=VMEM_LIMIT),
        cost_estimate=pl.CostEstimate(flops=15_000_000_000, bytes_accessed=4_000_000, transcendentals=0),
        name="embed_back",
    )(base, tokens, grad)


def start_kernel(raw_ref, nrm_ref, stream_out, hid_out, *, scale):
    stream = raw_ref[...].astype(F32).T * scale
    stream_out[...] = stream
    hid_out[...] = norm_apply(stream, nrm_ref[0:1, :], nrm_ref[1:2, :])


def start_stream(raw, nrm):
    width, rows = raw.shape
    return pl.pallas_call(
        functools.partial(start_kernel, scale=math.sqrt(width)),
        out_shape=[
            jax.ShapeDtypeStruct((rows, width), F32),
            jax.ShapeDtypeStruct((rows, width), BF),
        ],
        name="start_stream",
    )(raw, nrm)


def finish_kernel(keep_ref, near_ref, far_ref, above_ref, carry_ref, gain_ref, grad_out, pair_out):
    dy = keep_ref[0].astype(F32) + near_ref[0].astype(F32) + far_ref[...].astype(F32)
    back, pair = norm_back(dy, above_ref[...], gain_ref[...])
    pair_out[...] = pair
    grad_out[...] = (carry_ref[...] + back).T.astype(BF)


def finish_stream(dy, above, carry, gain, after=()):
    rows, width = above.shape
    vm = pl.BlockSpec(memory_space=pltpu.VMEM)
    return pl.pallas_call(
        ignore_tail(finish_kernel, 6, len(after)),
        in_specs=[vm] * 6 + [pl.BlockSpec(memory_space=pl.ANY)] * len(after),
        out_shape=[
            jax.ShapeDtypeStruct((width, rows), BF),
            jax.ShapeDtypeStruct((2, width), F32),
        ],
        name="finish_stream",
    )(*dy, above, carry, gain, *after)


def to_lanes(column):
    return jnp.broadcast_to(column, (column.shape[0], 128)).T[0:1, :]


def to_rows(line):
    return jnp.broadcast_to(line, (128, line.shape[1])).T[:, 0:1]


def head_stats_kernel(table_ref, final_ref, goal_ref, stat_out):
    logits = dot_nn(final_ref[...], table_ref[...])
    top = jnp.max(logits, 1, keepdims=True)
    total = jnp.sum(jnp.exp(logits - top), 1, keepdims=True)
    hit = iota(logits.shape, 1) == goal_ref[...]
    pick = jnp.sum(jnp.where(hit, logits, 0.0), 1, keepdims=True)
    stat_out[0:1, :] = to_lanes(top)
    stat_out[1:2, :] = to_lanes(total)
    stat_out[2:3, :] = to_lanes(pick)


def head_stats(table, final_all, goals):
    width, vocab = table.shape
    count = final_all.shape[0]
    tile = 256
    return pl.pallas_call(
        head_stats_kernel,
        grid=(count // tile,),
        out_shape=jax.ShapeDtypeStruct((3, count), F32),
        in_specs=[
            pl.BlockSpec((width, vocab), lambda i: (0, 0)),
            pl.BlockSpec((tile, width), lambda i: (i, 0)),
            pl.BlockSpec((tile, 1), lambda i: (i, 0)),
        ],
        out_specs=pl.BlockSpec((3, tile), lambda i: (0, i)),
        compiler_params=pltpu.CompilerParams(vmem_limit_bytes=VMEM_LIMIT),
        cost_estimate=pl.CostEstimate(flops=16_000_000_000, bytes_accessed=6_000_000, transcendentals=0),
        name="head_stats",
    )(table, final_all, goals)


def head_back_kernel(table_ref, final_ref, goal_ref, line_ref, gfin_out, gtab_out, acc_ref):
    step = pl.program_id(0)
    logits = dot_nn(final_ref[...], table_ref[...])
    hit = iota(logits.shape, 1) == goal_ref[...]
    chance = jnp.exp(logits - to_rows(line_ref[0:1, :]))
    grad = ((chance - jnp.where(hit, 1.0, 0.0)) * to_rows(line_ref[1:2, :])).astype(BF)
    gfin_out[...] = dot_nt(grad, table_ref[...]).astype(BF)
    part = dot_tn(final_ref[...], grad)

    @pl.when(step == 0)
    def _():
        acc_ref[...] = part

    @pl.when(step > 0)
    def _():
        acc_ref[...] += part

    @pl.when(step == pl.num_programs(0) - 1)
    def _():
        gtab_out[...] = acc_ref[...].astype(BF)


def head_back(table, final_all, goals, lines):
    width, vocab = table.shape
    count = final_all.shape[0]
    tile = 256
    return pl.pallas_call(
        head_back_kernel,
        grid=(count // tile,),
        out_shape=[
            jax.ShapeDtypeStruct((count, width), BF),
            jax.ShapeDtypeStruct((width, vocab), BF),
        ],
        in_specs=[
            pl.BlockSpec((width, vocab), lambda i: (0, 0)),
            pl.BlockSpec((tile, width), lambda i: (i, 0)),
            pl.BlockSpec((tile, 1), lambda i: (i, 0)),
            pl.BlockSpec((2, tile), lambda i: (0, i)),
        ],
        out_specs=[
            pl.BlockSpec((tile, width), lambda i: (i, 0)),
            pl.BlockSpec((width, vocab), lambda i: (0, 0)),
        ],
        scratch_shapes=[pltpu.VMEM((width, vocab), F32)],
        compiler_params=pltpu.CompilerParams(vmem_limit_bytes=VMEM_LIMIT),
        cost_estimate=pl.CostEstimate(flops=35_000_000_000, bytes_accessed=14_000_000, transcendentals=0),
        name="head_back",
    )(table, final_all, goals, lines)


def swap(value, axis, bit):
    return lax.ppermute(value, axis, [(at, at ^ bit) for at in range(lax.axis_size(axis))])


def has_bit(axis, bit):
    return (lax.axis_index(axis) & bit) != 0


def bits_of(axis):
    size = lax.axis_size(axis)
    return [1 << at for at in reversed(range(size.bit_length() - 1))]


def in_order(mine, other, axis, bit, dim):
    flag = has_bit(axis, bit)
    return jnp.concatenate([jnp.where(flag, other, mine), jnp.where(flag, mine, other)], dim)


def gather_dp(value):
    bits = bits_of("dp")
    whole = value.reshape((1,) * len(bits) + value.shape)
    for dim, bit in enumerate(bits):
        whole = in_order(whole, swap(whole, "dp", bit), "dp", bit, dim)
    return whole.reshape((-1,) + value.shape)


def scatter_dp(value):
    bits = bits_of("dp")
    value = value.reshape((2,) * len(bits) + value.shape[1:])
    for dim, bit in reversed(list(enumerate(bits))):
        flag = has_bit("dp", bit).astype(jnp.int32)
        low = value.astype(BF)
        other = swap(lax.dynamic_index_in_dim(low, 1 - flag, dim, False), "dp", bit)
        mine = lax.dynamic_index_in_dim(low, flag, dim, False)
        value = mine.astype(F32) + other.astype(F32)
    return value


def sum_all(value, combine=jnp.add):
    for axis in ("head", "dp"):
        for bit in reversed(bits_of(axis)):
            value = combine(value, swap(value, axis, bit))
    return value


def pieces_of_head(value):
    across = swap(value, "head", 2)
    return value, swap(value, "head", 1), across, swap(across, "head", 1)


def settle_head(keep, send):
    near = swap(send, "head", 1)
    across = (keep[1].astype(F32) + near[1].astype(F32)).astype(BF)
    return keep, near, swap(across, "head", 2)


def pack_weights(attn_in, attn_out, ffn_up, ffn_down):
    features = attn_in.shape[0]
    low = attn_in.astype(BF)
    q, k, v = low[..., :HD], low[..., HD:2 * HD], low[..., 2 * HD:3 * HD]
    s = low[..., 3 * HD:].reshape(features, -1)
    blank = jnp.zeros((features, 128 - s.shape[1]), BF)
    out = attn_out.astype(BF)
    out = jnp.concatenate([out[1], out[0]], 0).T
    return jnp.concatenate(
        [
            q[:, 0], q[:, 1], k[:, 0], v[:, 0], v[:, 1], k[:, 1], s, blank,
            out, ffn_up.astype(BF), ffn_down.astype(BF).T,
        ],
        1,
    )


def unpack_grads(packed, sort_width):
    def cut(at, size=HD):
        return packed[:, at:at + size]

    kv = C_KVS[0]
    srt = kv + 256
    first = jnp.concatenate([cut(0), cut(kv), cut(kv + 64), cut(srt, sort_width)], 1)
    second = jnp.concatenate(
        [cut(64), cut(kv + 192), cut(kv + 128), cut(srt + sort_width, sort_width)], 1
    )
    out = packed[:, C_OUT[0]:C_OUT[1]].T
    return (
        jnp.stack([first, second], 1),
        jnp.stack([out[HD:], out[:HD]], 0),
        packed[:, C_UP[0]:C_UP[1]],
        packed[:, C_DOWN[0]:C_DOWN[1]].T,
    )


class Gather:
    def __init__(self, packed):
        whole = gather_dp(packed)
        self.mine = whole.reshape(-1, max(64, packed.shape[0]), packed.shape[1])

    def finish(self):
        return pieces_of_head(self.mine)


class Scatter:
    def __init__(self, keep, send, features):
        self.keep, self.features = keep, features
        self.near = swap(send, "head", 1)
        self.pair = (keep[1].astype(F32) + self.near[1].astype(F32)).astype(BF)
        self.across = swap(self.pair, "head", 2)

    def finish(self):
        whole = self.keep[0].astype(F32) + self.near[0].astype(F32) + self.across.astype(F32)
        return scatter_dp(whole.reshape(-1, self.features, whole.shape[-1]))


def adamw(weight, gradient, moment_one, moment_two, factor, step_rate):
    gradient = gradient * factor
    moment_one = BETA_ONE * moment_one + (1.0 - BETA_ONE) * gradient
    moment_two = BETA_TWO * moment_two + (1.0 - BETA_TWO) * gradient * gradient
    adam_step = (
        moment_one
        / (1.0 - BETA_ONE**STEP)
        / (jnp.sqrt(moment_two / (1.0 - BETA_TWO**STEP)) + ADAM_FLOOR)
    )
    return (weight - step_rate * (adam_step + WEIGHT_DECAY * weight), moment_one, moment_two)


def body(
    tokens, targets, lengths,
    table, table_first, table_second,
    attn_in, attn_in_first, attn_in_second,
    attn_out, attn_out_first, attn_out_second,
    ffn_up, ffn_up_first, ffn_up_second,
    ffn_down, ffn_down_first, ffn_down_second,
    norms, norms_first, norms_second,
):
    dp, head = lax.axis_size("dp"), lax.axis_size("head")
    my_dp, my_head = lax.axis_index("dp"), lax.axis_index("head")
    seq_count, length = tokens.shape
    features, vocab = table.shape
    width = features * dp
    layers = attn_in.shape[0]
    rows = length // head
    total = dp * length
    me = my_head.astype(jnp.int32).reshape(1)
    odd = my_dp & 1
    outer = [[at for at in range(dp) if at % 2 == way] for way in range(2)]

    lines = jnp.concatenate([tokens, targets, jnp.broadcast_to(lengths[:, None], (seq_count, 128))], 1)
    lines = gather_dp(lines.reshape(-1))
    all_tokens = lines[:, :length].reshape(1, total)
    positions = jnp.arange(length, dtype=jnp.int32)
    counted = (positions[None, :] < lines[:, 2 * length:2 * length + 1]).astype(F32)
    nrm = norms
    for bit in (1, 2):
        nrm = in_order(nrm, swap(nrm, "head", bit), "head", bit, 2)

    low_table = table.astype(BF)
    gathers = [
        Gather(pack_weights(attn_in[at], attn_out[at], ffn_up[at], ffn_down[at]))
        for at in range(layers)
    ]
    weights = [one.finish() for one in gathers]

    half = vocab // 2
    other = swap(lax.dynamic_slice_in_dim(low_table, (1 - odd) * half, half, 1), "dp", 1)
    mine = lax.dynamic_slice_in_dim(low_table, odd * half, half, 1)
    head_table = lax.all_gather(
        in_order(mine, other, "dp", 1, 0), "dp", axis=0, tiled=True, axis_index_groups=outer
    )

    base = (my_head * vocab).astype(jnp.int32).reshape(1)
    found = embed_lookup(base, all_tokens, low_table).reshape(features, dp, head, rows)
    for bit in (1, 2):
        flag = (my_head & bit) // bit
        found = found.reshape(features, dp, -1, 2, rows) if bit == 1 else found.reshape(features, dp, 2, rows)
        dim = 3 if bit == 1 else 2
        other = swap(lax.dynamic_index_in_dim(found, 1 - flag, dim, False), "head", bit)
        found = lax.dynamic_index_in_dim(found, flag, dim, False) + other
    found = lax.all_to_all(found, "dp", split_axis=1, concat_axis=0, tiled=True)
    stream, hidden = start_stream(found.reshape(width, rows), nrm[0])

    kept = []
    for at in range(layers):
        pairs_now = jnp.concatenate([nrm[2 * at + 1], nrm[2 * at + 2]], 0)
        after = tuple(one.mine for one in gathers[at + 1:at + 2])
        got = layer_forward(me, pieces_of_head(hidden), stream, weights[at], pairs_now, after)
        kept.append((stream, (got[1],) + tuple(got[3:])))
        stream, hidden = got[0], got[2]

    def spread_rows(value):
        for axis, bit in (("dp", 1), ("head", 2), ("head", 1)):
            value = jnp.stack([value, swap(value, axis, bit)])
        return value

    def line_of(values):
        values = values.reshape(dp, head, rows)
        order = [(my_dp ^ y, my_head ^ (x * 2 + c)) for c in range(2) for x in range(2) for y in range(2)]
        picked = [
            lax.dynamic_slice(values, (d, h, 0), (1, 1, rows)).reshape(rows) for d, h in order
        ]
        return jnp.concatenate(picked)

    final_all = spread_rows(hidden).reshape(-1, width)
    goals = line_of(lines[:, length:2 * length]) - (my_head * vocab + odd * half).astype(jnp.int32)
    goals = goals.reshape(-1, 1)
    counted_here = line_of(counted)
    stats = head_stats(head_table, final_all, goals)
    for dim, (axis, bit) in enumerate((("head", 1), ("head", 2), ("dp", 1))):
        theirs = swap(stats, axis, bit).reshape(3, 2, 2, 2, rows)
        theirs = jnp.flip(theirs, dim + 1).reshape(stats.shape)
        peak = jnp.maximum(stats[0], theirs[0])
        sums = stats[1] * jnp.exp(stats[0] - peak) + theirs[1] * jnp.exp(theirs[0] - peak)
        stats = jnp.stack([peak, sums, stats[2] + theirs[2]])
    lse = stats[0] + jnp.log(stats[1])
    loss_here = jnp.sum((lse - stats[2]) * counted_here) / (2 * head)
    count_total = jnp.sum(counted)
    grad_final, grad_half = head_back(head_table, final_all, goals, jnp.stack([lse, counted_here]))
    grad_final = grad_final.reshape(2, 2, 2, rows, width)
    near = swap(grad_final[1], "head", 1)
    summed = grad_final[0].astype(F32) + near.astype(F32)
    across = swap(summed[1].astype(BF), "head", 2)
    summed = summed[0] + across.astype(F32)
    far = swap(summed[1].astype(BF), "dp", 1)
    nothing = jnp.zeros((1, rows, width), BF)
    dy = (summed[0:1], nothing, far)
    grad_half = lax.psum_scatter(
        grad_half, "dp", scatter_dimension=0, tiled=True, axis_index_groups=outer
    ).reshape(2, features, half)
    other = swap(lax.dynamic_index_in_dim(grad_half, 1 - odd, 0, False), "dp", 1)
    mine = lax.dynamic_index_in_dim(grad_half, odd, 0, False)
    grad_table = in_order(mine, other, "dp", 1, 1).astype(F32)

    carry = jnp.zeros((rows, width), F32)
    above = stream
    pair_grads = [None] * (2 * layers + 1)
    scatters = []
    for at in reversed(range(layers)):
        stream_in, rest = kept[at]
        after = [one.pair for one in scatters[-1:]] + [one.across for one in scatters[-2:-1]]
        if at == 0:
            after.append(grad_half)
        gkeep, gsend, wkeep, wsend, carry, pair_above, pair_two = layer_backward(
            me, dy, above, carry, nrm[2 * at + 2, 0:1], weights[at], nrm[2 * at + 1, 0:1], rest, after
        )
        pair_grads[2 * at + 2] = pair_above
        pair_grads[2 * at + 1] = pair_two
        dy = settle_head(gkeep, gsend)
        scatters.append(Scatter(wkeep, wsend, features))
        above = stream_in
    packed_grads = [one.finish() for one in reversed(scatters)]
    after = [scatters[-1].pair, scatters[-2].across, packed_grads[-1]]
    grad_stream, pair_grads[0] = finish_stream(dy, above, carry, nrm[0, 0:1], after)

    spread = lax.all_to_all(
        grad_stream.reshape(dp, features, rows), "dp", split_axis=0, concat_axis=0, tiled=True
    )
    spread = in_order(spread[:, None], swap(spread[:, None], "head", 1), "head", 1, 1)[:, None]
    spread = in_order(spread, swap(spread, "head", 2), "head", 2, 1)
    spread = spread.reshape(dp * head, features, rows)
    grad_table = grad_table + math.sqrt(width) * embed_back(base, all_tokens, spread, vocab)

    grad_norms = sum_all(jnp.stack(pair_grads))
    grad_norms = lax.dynamic_slice_in_dim(grad_norms, my_head * norms.shape[2], norms.shape[2], 2)
    sort_width = attn_in.shape[3] - 3 * HD
    layer_grads = [unpack_grads(packed, sort_width) for packed in packed_grads]
    grad_in, grad_out, grad_up, grad_down = (
        jnp.stack([one[member] for one in layer_grads]) for member in range(4)
    )
    squares = jnp.sum(grad_table * grad_table) + jnp.sum(grad_norms * grad_norms) / dp
    for packed in packed_grads:
        squares = squares + jnp.sum(packed * packed)
    totals = sum_all(jnp.stack([squares, loss_here]))
    grad_norm = jnp.sqrt(totals[0])
    loss_total = totals[1]
    factor = jnp.minimum(1.0, CLIP_LIMIT / (grad_norm + 1e-06))

    results = [jnp.stack([loss_total, count_total]), grad_norm]
    for weight, gradient, first, second in (
        (table, grad_table, table_first, table_second),
        (attn_in, grad_in, attn_in_first, attn_in_second),
        (attn_out, grad_out, attn_out_first, attn_out_second),
        (ffn_up, grad_up, ffn_up_first, ffn_up_second),
        (ffn_down, grad_down, ffn_down_first, ffn_down_second),
    ):
        new, one, two = adamw(weight, gradient, first, second, factor, RATE_MATRIX)
        results += [new, new.astype(BF), one, two]
    results += list(adamw(norms, grad_norms, norms_first, norms_second, factor, RATE_NORM))
    return tuple(results)


def solution(mesh):
    ints = [P("dp", None), P("dp", None), P("dp")]
    by_table = P("dp", "head")
    by_in = P(None, "dp", "head", None)
    by_out = P(None, "head", None, "dp")
    by_up = P(None, "dp", "head")
    by_down = P(None, "head", "dp")
    by_norm = P(None, None, "head")
    in_specs, out_specs = list(ints), [P(), P()]
    for spec in (by_table, by_in, by_out, by_up, by_down):
        in_specs += [spec] * 3
        out_specs += [spec] * 4
    in_specs += [by_norm] * 3
    out_specs += [by_norm] * 3
    return jax.shard_map(
        body, mesh=mesh, in_specs=tuple(in_specs), out_specs=tuple(out_specs), check_vma=False
    )
```

time: 2140 us -> 841 us (0.39)
  waiting for transfers between devices: 1360 us -> 318 us
  Pallas kernels: 0 us -> 306 us
  matrix products: 214 us -> 0 us
  blocking collectives: 195 us -> 0 us
  local copies, waits for them, and re-layouts: 151 us -> 43.9 us
  other arithmetic: 158 us -> 70 us
  starting transfers between devices: 12.5 us -> 70.5 us
    unnamed x52 -> x2, waiting for transfers between devices: 597 us -> 0.03 us
    all_gather x18 -> x1, waiting for transfers between devices: 432 us -> 0.01 us  [body(): lax.all_gather(in_order(mine, other, 'dp', 1, 0), 'dp', axis=0, tiled=Tru...]
    reduce_scatter x2 -> x1, waiting for transfers between devices: 334 us -> 0.02 us  [body(): lax.psum_scatter(grad_half, 'dp', scatter_dimension=0, tiled=True, axis_i...]
    ppermute x0 -> x78, waiting for transfers between devices: none -> 310 us  [swap(): lax.ppermute(value, axis, [(at, at ^ bit) for at in range(lax.axis_size(a...]
    pallas_call x0 -> x12, Pallas kernels: none -> 306 us  [the longest x3 115 us: layer_backward(): pl.pallas_call(ignore_tail(backward_kernel, 8 + pairs + len(kept), len(af...]
    dot_general x77 -> x0, matrix products: 214 us -> none  [the longest x3 19.7 us: attend_backward(): jnp.einsum('shitu,shitc->shiuc', weights_low, grad_mixed, preferred_eleme...]
    psum x17 -> x0, blocking collectives: 155 us -> none  [the longest x13 78.1 us: row_sums(): return lax.psum((jnp.sum(left_term, 1), jnp.sum(right_term, 1)), 'head')]
    unnamed x903 -> x194, local copies, waits for them, and re-layouts: 98.4 us -> 21.7 us
  transfers between devices with their start and end apart: 36 -> 82, of which waited for: 35 -> 41; matrix products, arithmetic and copies ran while one was open for 5% -> 9% of each run, Pallas kernels for 0% -> 25%
where the time goes in v1:
time: 841 us; the launch traced here: 831 us
  waiting for transfers between devices  318 us (38%)
  Pallas kernels  306 us (36%)
  starting transfers between devices  70.5 us (8%)
  other arithmetic  70 us (8%)
  local copies, waits for them, and re-layouts  43.9 us (5%)
  between operations  23 us (3%)
    ppermute x78, waiting for transfers between devices, swap(): lax.ppermute(value, axis, [(at, at ^ bit) for at in range(lax.axis_size(a...  310 us
    pallas_call x3, Pallas kernels, layer_backward(): pl.pallas_call(ignore_tail(backward_kernel, 8 + pairs + len(kept), len(af...  115 us
    pallas_call x3, Pallas kernels, layer_forward(): pl.pallas_call(ignore_tail(forward_kernel, 2 * pairs + 3, len(after)), ou...  86.9 us
    ppermute x78, starting transfers between devices, swap(): lax.ppermute(value, axis, [(at, at ^ bit) for at in range(lax.axis_size(a...  62.7 us
    pallas_call x1, Pallas kernels, head_back(): pl.pallas_call(head_back_kernel, grid=(count // tile,), out_shape=[jax.Sh...  39.5 us
    pallas_call x1, Pallas kernels, embed_back(): pl.pallas_call(embed_back_kernel, grid=(pieces,), out_shape=jax.ShapeDtyp...  25.7 us
    unnamed x194, local copies, waits for them, and re-layouts  21.7 us
    pallas_call x1, Pallas kernels, head_stats(): pl.pallas_call(head_stats_kernel, grid=(count // tile,), out_shape=jax.Sh...  20.4 us
  transfers between devices with their start and end apart: 82, of which 41 were waited for; matrix products, arithmetic and copies ran while one was open for 9% of the time, Pallas kernels for 25%

profile of v1, /device:TPU:0, one launch (start us, length us, event | category | flops | bytes accessed | tf_op | source)
XLA Modules:
  0.0 830.9 jit_solution(7743023701681902688)
XLA Ops:
  35.6 13.8 %embed_lookup.1 = bf16[64,8192]{1,0:T(8,128)(2,1)} custom-call(s32[1]{0:T(128)} %bitcast.1.base_ref, s32[1,8192]{1,0:T(1,128)} %bitcast.439, bf16[64,8192]{1,0:T(8,128)(2,1)} %convert_element_type.335.table_ref), custom_call_target="tpu_custom_call" | custom-call | flops 15000000512 | bytes 4000000 | tf_op jit(solution)/shard_map/embed_lookup/pallas_call | solution.py:503
  59.6 8.4 %collective-permute-done.12 = bf16[2,1,1,64,1664]{4,3,2,1,0:T(8,128)(2,1)S(1)} collective-permute-done((bf16[2,1,1,64,1664]{4,3,2,1,0:T(8,128)(2,1)S(1)}, bf16[2,1,1,64,1664]{4,3,2,1,0:T(8,128)(2,1)S(1)}, u32[]{:S(2)}, u32[]{:S(2)}) %collective-permute-start.12) | collective-permute-done | bytes 426016 | tf_op jit(solution)/shard_map/ppermute | solution.py:696
  68.6 8.4 %collective-permute-done.27 = bf16[2,1,1,64,1664]{4,3,2,1,0:T(8,128)(2,1)S(1)} collective-permute-done((bf16[2,1,1,64,1664]{4,3,2,1,0:T(8,128)(2,1)S(1)}, bf16[2,1,1,64,1664]{4,3,2,1,0:T(8,128)(2,1)S(1)}, u32[]{:S(2)}, u32[]{:S(2)}) %collective-permute-start.27) | collective-permute-done | bytes 426016 | tf_op jit(solution)/shard_map/ppermute | solution.py:696
  78.6 7.2 collective-permute-done.18
  94.9 13.5 %collective-permute-done.28 = bf16[2,2,1,64,1664]{4,3,2,1,0:T(8,128)(2,1)} collective-permute-done((bf16[2,2,1,64,1664]{4,3,2,1,0:T(8,128)(2,1)}, bf16[2,2,1,64,1664]{4,3,2,1,0:T(8,128)(2,1)}, u32[]{:S(2)}, u32[]{:S(2)}) %collective-permute-start.28) | collective-permute-done | bytes 852000 | tf_op jit(solution)/shard_map/ppermute | solution.py:696
  108.4 16.5 %collective-permute-done.19 = bf16[2,2,1,64,1664]{4,3,2,1,0:T(8,128)(2,1)} collective-permute-done((bf16[2,2,1,64,1664]{4,3,2,1,0:T(8,128)(2,1)}, bf16[2,2,1,64,1664]{4,3,2,1,0:T(8,128)(2,1)}, u32[]{:S(2)}, u32[]{:S(2)}) %collective-permute-start.19) | collective-permute-done | bytes 852000 | tf_op jit(solution)/shard_map/ppermute | solution.py:696
  142.1 27.9 %collective-permute-done.7 = f32[7,2,256]{2,1,0:T(2,128)S(1)} collective-permute-done((f32[7,2,256]{2,1,0:T(2,128)S(1)}, f32[7,2,256]{2,1,0:T(2,128)S(1)}, u32[]{:S(2)}, u32[]{:S(2)}) %collective-permute-start.7) | collective-permute-done | bytes 14368 | tf_op jit(solution)/shard_map/ppermute | solution.py:696
  184.8 28.8 %layer_forward.3 = (f32[256,512]{1,0:T(8,128)}, f32[256,512]{1,0:T(8,128)}, bf16[256,512]{1,0:T(8,128)(2,1)}, bf16[1024,512]{1,0:T(8,128)(2,1)}, bf16[4,1024,256...) custom-call(s32[1]{0:T(128)} %bitcast.refs_0_, ...), custom_call_target="tpu_custom_call" | custom-call | flops 20000000000 | bytes 18000000 | tf_op jit(solution)/shard_map/layer_forward/pallas_call | solution.py:267
  215.1 13.4 %collective-permute-done.21.refs_3_ = bf16[256,512]{1,0:T(8,128)(2,1)S(1)} collective-permute-done((bf16[256,512]{1,0:T(8,128)(2,1)}, bf16[256,512]{1,0:T(8,128)(2,1)S(1)}, u32[]{:S(2)}, u32[]{:S(2)}) %collective-permute-start.21) | collective-permute-done | bytes 262176 | tf_op jit(solution)/shard_map/ppermute | solution.py:696
  231.3 29.3 %layer_forward.4 = (f32[256,512]{1,0:T(8,128)}, f32[256,512]{1,0:T(8,128)}, bf16[256,512]{1,0:T(8,128)(2,1)}, bf16[1024,512]{1,0:T(8,128)(2,1)}, bf16[4,1024,256...) custom-call(s32[1]{0:T(128)} %bitcast.refs_0_, ...), custom_call_target="tpu_custom_call" | custom-call | flops 20000000000 | bytes 18000000 | tf_op jit(solution)/shard_map/layer_forward/pallas_call | solution.py:267
  262.9 6.7 collective-permute-done.30.refs_3_
  271.8 28.8 %layer_forward.5 = (f32[256,512]{1,0:T(8,128)}, f32[256,512]{1,0:T(8,128)}, bf16[256,512]{1,0:T(8,128)(2,1)}, bf16[1024,512]{1,0:T(8,128)(2,1)}, bf16[4,1024,256...) custom-call(s32[1]{0:T(128)} %bitcast.refs_0_, ...), custom_call_target="tpu_custom_call" | custom-call | flops 20000000000 | bytes 18000000 | tf_op jit(solution)/shard_map/layer_forward/pallas_call | solution.py:267
  300.8 8.5 %collective-permute-done.35 = bf16[256,512]{1,0:T(8,128)(2,1)S(1)} collective-permute-done((bf16[256,512]{1,0:T(8,128)(2,1)}, bf16[256,512]{1,0:T(8,128)(2,1)S(1)}, u32[]{:S(2)}, u32[]{:S(2)}) %collective-permute-start.35) | collective-permute-done | bytes 262176 | tf_op jit(solution)/shard_map/ppermute | solution.py:696
  312.9 10.6 %collective-permute-done.36 = bf16[2,256,512]{2,1,0:T(8,128)(2,1)S(1)} collective-permute-done((bf16[2,256,512]{2,1,0:T(8,128)(2,1)S(1)}, bf16[2,256,512]{2,1,0:T(8,128)(2,1)S(1)}, u32[]{:S(2)}, u32[]{:S(2)}) %collective-permute-start.36) | collective-permute-done | bytes 524320 | tf_op jit(solution)/shard_map/ppermute | solution.py:696
  327.9 20.4 %head_stats.1 = f32[3,2048]{1,0:T(4,128)} custom-call(bf16[512,4096]{1,0:T(8,128)(2,1)} %all-gather.2.cloned.1.call-done.table_ref, bf16[2048,512]{1,0:T(8,128)(2,1)} %bitcast.408, s32[2048,1]{1,0:T(8,128)} %broadcast_subtract_fusion.goal_ref), custom_call_target="tpu_custom_call" | custom-call | flops 16000000000 | bytes 6000000 | tf_op jit(solution)/shard_map/head_stats/pallas_call | solution.py:629
  361.4 39.5 %head_back.1 = (bf16[2048,512]{1,0:T(8,128)(2,1)}, bf16[512,4096]{1,0:T(8,128)(2,1)}) custom-call(bf16[512,4096]{1,0:T(8,128)(2,1)} %all-gather.2.cloned.1.call-done.table_ref, bf16[2048,512]{1,0:T(8,128)(2,1)} %bitcast.409, s32[2048,1]{1,0:T(8,128)} %broadcast_subtract_fusion.goal_ref, f32[2,2048]{1,0:T(2,128)} %pad_maximum_fusion.16.line_ref), custom_call_target="tpu_custom_call" | custom-call | flops 35000000512 | bytes 14000000 | tf_op jit(solution)/shard_map/head_back/pallas_call | solution.py:671
  407.3 12.5 %collective-permute-done.43 = bf16[2,256,512]{2,1,0:T(8,128)(2,1)S(1)} collective-permute-done((bf16[2,256,512]{2,1,0:T(8,128)(2,1)S(1)}, bf16[2,256,512]{2,1,0:T(8,128)(2,1)S(1)}, u32[]{:S(2)}, u32[]{:S(2)}) %collective-permute-start.43) | collective-permute-done | bytes 524320 | tf_op jit(solution)/shard_map/ppermute | solution.py:696
  429.2 38.2 %layer_backward.3 = (bf16[2,256,512]{2,1,0:T(8,128)(2,1)}, bf16[2,256,512]{2,1,0:T(8,128)(2,1)}, bf16[2,8,64,1664]{3,2,1,0:T(8,128)(2,1)}, bf16[2,8,64,1664]{3,2...) custom-call(s32[1]{0:T(128)} %bitcast.refs_0_, f32[1,256,512]{2,1,0:T(8,128)} %slice.723.refs_1_, ...), custom_call_target="tpu_custom_call" | custom-call | flops 30000001024 | bytes 25000000 | tf_op jit(solution)/shard_map/layer_backward/pallas_call | solution.py:455
  468.0 6.5 collective-permute-done.45.refs_2_
  485.6 38.2 %layer_backward.4 = (bf16[2,256,512]{2,1,0:T(8,128)(2,1)}, bf16[2,256,512]{2,1,0:T(8,128)(2,1)}, bf16[2,8,64,1664]{3,2,1,0:T(8,128)(2,1)}, bf16[2,8,64,1664]{3,2...) custom-call(s32[1]{0:T(128)} %bitcast.refs_0_, ...), custom_call_target="tpu_custom_call" | custom-call | flops 30000001024 | bytes 25000000 | tf_op jit(solution)/shard_map/layer_backward/pallas_call | solution.py:455
  530.3 17.9 %collective-permute-done.56 = bf16[2,2,64,1664]{3,2,0,1:T(8,128)(2,1)S(1)} collective-permute-done((bf16[2,2,64,1664]{3,2,0,1:T(8,128)(2,1)S(1)}, bf16[2,2,64,1664]{3,2,0,1:T(8,128)(2,1)S(1)}, u32[]{:S(2)}, u32[]{:S(2)}) %collective-permute-start.56) | collective-permute-done | bytes 852000 | tf_op jit(solution)/shard_map/ppermute | solution.py:696
  553.4 6.5 collective-permute-done.57
  574.8 27.9 %collective-permute-done.55.refs_7_ = bf16[8,64,1664]{2,1,0:T(8,128)(2,1)S(1)} collective-permute-done((bf16[8,64,1664]{2,1,0:T(8,128)(2,1)S(1)}, bf16[8,64,1664]{2,1,0:T(8,128)(2,1)S(1)}, u32[]{:S(2)}, u32[]{:S(2)}) %collective-permute-start.55) | collective-permute-done | bytes 1703968 | tf_op jit(solution)/shard_map/ppermute | solution.py:696
  607.3 38.2 %layer_backward.5 = (bf16[2,256,512]{2,1,0:T(8,128)(2,1)}, bf16[2,256,512]{2,1,0:T(8,128)(2,1)}, bf16[2,8,64,1664]{3,2,1,0:T(8,128)(2,1)}, bf16[2,8,64,1664]{3,2...) custom-call(s32[1]{0:T(128)} %bitcast.refs_0_, ...), custom_call_target="tpu_custom_call" | custom-call | flops 30000001024 | bytes 25000000 | tf_op jit(solution)/shard_map/layer_backward/pallas_call | solution.py:455
  647.2 11.0 %collective-permute-done.71 = bf16[2,64,1664]{2,1,0:T(8,128)(2,1)S(1)} collective-permute-done((bf16[2,64,1664]{2,1,0:T(8,128)(2,1)S(1)}, bf16[2,64,1664]{2,1,0:T(8,128)(2,1)S(1)}, u32[]{:S(2)}, u32[]{:S(2)}) %collective-permute-start.71) | collective-permute-done | bytes 426016 | tf_op jit(solution)/shard_map/ppermute | solution.py:696
  662.6 7.6 collective-permute-done.72
  684.8 7.7 all-to-all-done.1
  693.5 21.0 %collective-permute-done.62 = f32[7,2,512]{2,1,0:T(2,128)S(1)} collective-permute-done((f32[7,2,512]{2,1,0:T(2,128)S(1)}, f32[7,2,512]{2,1,0:T(2,128)S(1)}, u32[]{:S(2)}, u32[]{:S(2)}) %collective-permute-start.62) | collective-permute-done | bytes 28704 | tf_op jit(solution)/shard_map/ppermute | solution.py:696
  735.8 6.5 collective-permute-done.67
  743.8 25.7 %embed_back.1 = f32[64,8192]{1,0:T(8,128)} custom-call(s32[1]{0:T(128)} %bitcast.1.base_ref, s32[1,8192]{1,0:T(1,128)} %bitcast.440, bf16[32,64,256]{2,1,0:T(8,128)(2,1)} %bitcast.410), custom_call_target="tpu_custom_call" | custom-call | flops 15000000512 | bytes 4000000 | tf_op jit(solution)/shard_map/embed_back/pallas_call | solution.py:550
  773.8 6.3 collective-permute-done.69
  813.6 5.6 fusion.83
  (573 shorter events, 248.9 us)
Async XLA Ops:
  16.8 37.4 %collective-permute-start.11 = (bf16[1,1,1,64,1664]{4,3,2,1,0:T(8,128)(2,1)S(1)}, bf16[1,1,1,64,1664]{4,3,2,1,0:T(8,128)(2,1)}, u32[]{:S(2)}, u32[]{:S(2)}) collective-permute-start(bf16[1,1,1,64,1664]{4,3,2,1,0:T(8,128)(2,1)S(1)} %bitcast.420), channel_id=1, source_target_pairs={{0,16},{4,20},{8,24},{12,28},{16,0},{20,4},{24,8},{28,12},{1,17},{... | collective-permute-start | bytes 638984 | tf_op jit(solution)/shard_map/ppermute | solution.py:696
  17.8 37.5 %collective-permute-start.26 = (bf16[1,1,1,64,1664]{4,3,2,1,0:T(8,128)(2,1)S(1)}, bf16[1,1,1,64,1664]{4,3,2,1,0:T(8,128)(2,1)}, u32[]{:S(2)}, u32[]{:S(2)}) collective-permute-start(bf16[1,1,1,64,1664]{4,3,2,1,0:T(8,128)(2,1)S(1)} %bitcast.421), channel_id=1, source_target_pairs={{0,16},{4,20},{8,24},{12,28},{16,0},{20,4},{24,8},{28,12},{1,17},{... | collective-permute-start | bytes 638984 | tf_op jit(solution)/shard_map/ppermute | solution.py:696
  29.0 29.4 %collective-permute-start.17 = (bf16[1,1,1,64,1664]{4,3,2,1,0:T(8,128)(2,1)S(1)}, bf16[1,1,1,64,1664]{4,3,2,1,0:T(8,128)(2,1)}, u32[]{:S(2)}, u32[]{:S(2)}) collective-permute-start(bf16[1,1,1,64,1664]{4,3,2,1,0:T(8,128)(2,1)S(1)} %bitcast.422), channel_id=1, source_target_pairs={{0,16},{4,20},{8,24},{12,28},{16,0},{20,4},{24,8},{28,12},{1,17},{... | collective-permute-start | bytes 638984 | tf_op jit(solution)/shard_map/ppermute | solution.py:696
  54.1 39.0 %collective-permute-start.4 = (bf16[64,8,2,256]{3,1,2,0:T(8,128)(2,1)S(1)}, bf16[64,8,2,256]{3,1,2,0:T(8,128)(2,1)}, u32[]{:S(2)}, u32[]{:S(2)}) collective-permute-start(bf16[64,8,2,256]{3,1,2,0:T(8,128)(2,1)S(1)} %bitcast.423), channel_id=1, source_target_pairs={{0,1},{1,0},{2,3},{3,2},{4,5},{5,4},{6,7},{7,6},{8,9},{9,8},{10,11... | collective-permute-start | bytes 1572872 | tf_op jit(solution)/shard_map/ppermute | solution.py:696
  59.5 26.3 %collective-permute-start.18 = (bf16[2,1,1,64,1664]{4,3,2,1,0:T(8,128)(2,1)S(1)}, bf16[2,1,1,64,1664]{4,3,2,1,0:T(8,128)(2,1)S(1)}, u32[]{:S(2)}, u32[]{:S(2)}) collective-permute-start(bf16[2,1,1,64,1664]{4,3,2,1,0:T(8,128)(2,1)S(1)} %pad_maximum_fusion.12), channel_id=1, source_target_pairs={{0,8},{4,12},{8,0},{12,4},{16,24},{20,28},{24,16},{28,20},{1,9},{5... | collective-permute-start | bytes 1277960 | tf_op jit(solution)/shard_map/ppermute | solution.py:696
  78.1 30.3 %collective-permute-start.28 = (bf16[2,2,1,64,1664]{4,3,2,1,0:T(8,128)(2,1)}, bf16[2,2,1,64,1664]{4,3,2,1,0:T(8,128)(2,1)}, u32[]{:S(2)}, u32[]{:S(2)}) collective-permute-start(bf16[2,2,1,64,1664]{4,3,2,1,0:T(8,128)(2,1)} %pad_maximum_fusion.9), channel_id=1, source_target_pairs={{0,4},{4,0},{8,12},{12,8},{16,20},{20,16},{24,28},{28,24},{1,5},{5... | collective-permute-start | bytes 2555912 | tf_op jit(solution)/shard_map/ppermute | solution.py:696
  86.9 38.1 %collective-permute-start.19 = (bf16[2,2,1,64,1664]{4,3,2,1,0:T(8,128)(2,1)}, bf16[2,2,1,64,1664]{4,3,2,1,0:T(8,128)(2,1)}, u32[]{:S(2)}, u32[]{:S(2)}) collective-permute-start(bf16[2,2,1,64,1664]{4,3,2,1,0:T(8,128)(2,1)} %pad_maximum_fusion.8), channel_id=1, source_target_pairs={{0,4},{4,0},{8,12},{12,8},{16,20},{20,16},{24,28},{28,24},{1,5},{5... | collective-permute-start | bytes 2555912 | tf_op jit(solution)/shard_map/ppermute | solution.py:696
  91.7 39.1 %collective-permute-start.15 = (bf16[8,64,1664]{2,1,0:T(8,128)(2,1)}, bf16[8,64,1664]{2,1,0:T(8,128)(2,1)}, u32[]{:S(2)}, u32[]{:S(2)}) collective-permute-start(bf16[8,64,1664]{2,1,0:T(8,128)(2,1)} %bitcast.27.refs_6_.refs_7_), channel_id=1, source_target_pairs={{0,2},{1,3},{2,0},{3,1},{4,6},{5,7},{6,4},{7,5},{8,10},{9,11},{10,... | collective-permute-start | bytes 5111816 | tf_op jit(solution)/shard_map/ppermute | solution.py:696
  93.2 37.6 %collective-permute-start.6 = (f32[7,2,128]{2,1,0:T(2,128)S(1)}, f32[7,2,128]{2,1,0:T(2,128)S(1)}, u32[]{:S(2)}, u32[]{:S(2)}) collective-permute-start(f32[7,2,128]{2,1,0:T(2,128)S(1)} %copy-done.55), channel_id=1, source_target_pairs={{0,1},{1,0},{2,3},{3,2},{4,5},{5,4},{6,7},{7,6},{8,9},{9,8},{10,11... | collective-permute-start | bytes 21512 | tf_op jit(solution)/shard_map/ppermute | solution.py:696
  94.3 41.7 %collective-permute-start.5 = (bf16[64,8,256]{2,1,0:T(8,128)(2,1)S(1)}, bf16[64,8,256]{2,1,0:T(8,128)(2,1)S(1)}, u32[]{:S(2)}, u32[]{:S(2)}) collective-permute-start(bf16[64,8,256]{2,1,0:T(8,128)(2,1)S(1)} %dynamic-slice_bitcast_fusion.4), channel_id=1, source_target_pairs={{0,2},{1,3},{2,0},{3,1},{4,6},{5,7},{6,4},{7,5},{8,10},{9,11},{10,... | collective-permute-start | bytes 786440 | tf_op jit(solution)/shard_map/ppermute | solution.py:696
  108.4 74.9 %collective-permute-start.14 = (bf16[8,64,1664]{2,1,0:T(8,128)(2,1)}, bf16[8,64,1664]{2,1,0:T(8,128)(2,1)}, u32[]{:S(2)}, u32[]{:S(2)}) collective-permute-start(bf16[8,64,1664]{2,1,0:T(8,128)(2,1)} %bitcast.27.refs_6_.refs_7_), channel_id=1, source_target_pairs={{0,1},{1,0},{2,3},{3,2},{4,5},{5,4},{6,7},{7,6},{8,9},{9,8},{10,11... | collective-permute-start | bytes 5111816 | tf_op jit(solution)/shard_map/ppermute | solution.py:696
  129.3 55.5 %collective-permute-start.24 = (bf16[8,64,1664]{2,1,0:T(8,128)(2,1)}, bf16[8,64,1664]{2,1,0:T(8,128)(2,1)}, u32[]{:S(2)}, u32[]{:S(2)}) collective-permute-start(bf16[8,64,1664]{2,1,0:T(8,128)(2,1)} %bitcast.45.refs_11_.refs_6_.refs_7_), channel_id=1, source_target_pairs={{0,2},{1,3},{2,0},{3,1},{4,6},{5,7},{6,4},{7,5},{8,10},{9,11},{10,... | collective-permute-start | bytes 5111816 | tf_op jit(solution)/shard_map/ppermute | solution.py:696
  130.8 54.0 %collective-permute-start.16 = (bf16[8,64,1664]{2,1,0:T(8,128)(2,1)}, bf16[8,64,1664]{2,1,0:T(8,128)(2,1)}, u32[]{:S(2)}, u32[]{:S(2)}) collective-permute-start(bf16[8,64,1664]{2,1,0:T(8,128)(2,1)} %collective-permute-done.15.refs_8_.refs_9_), channel_id=1, source_target_pairs={{0,1},{1,0},{2,3},{3,2},{4,5},{5,4},{6,7},{7,6},{8,9},{9,8},{10,11... | collective-permute-start | bytes 5111816 | tf_op jit(solution)/shard_map/ppermute | solution.py:696
  136.8 33.9 %all-to-all-start = ((bf16[64,8,256]{2,0,1:T(8,128)(2,1)}), bf16[64,8,256]{2,0,1:T(8,128)(2,1)S(1)}, u32[]{:S(2)}, u32[]{:S(2)}) async-start(bf16[64,8,256]{2,0,1:T(8,128)(2,1)} %copy.236), calls=%async_computation | async-start | bytes 524288 | tf_op jit(solution)/shard_map/all_to_all | solution.py:872
  140.2 187.7 %all-gather.2.cloned.1.call-start = ((), (), s32[]{:S(2)}) async-start(), calls=%async_computation.3 | async-start | bytes 5242880 | tf_op jit(solution)/shard_map/all_gather | solution.py:860
  140.4 29.6 %collective-permute-start.7 = (f32[7,2,256]{2,1,0:T(2,128)S(1)}, f32[7,2,256]{2,1,0:T(2,128)S(1)}, u32[]{:S(2)}, u32[]{:S(2)}) collective-permute-start(f32[7,2,256]{2,1,0:T(2,128)S(1)} %pad_maximum_fusion.17), channel_id=1, source_target_pairs={{0,2},{1,3},{2,0},{3,1},{4,6},{5,7},{6,4},{7,5},{8,10},{9,11},{10,... | collective-permute-start | bytes 43016 | tf_op jit(solution)/shard_map/ppermute | solution.py:696
  181.5 32.8 %collective-permute-start = (bf16[64,4096]{1,0:T(8,128)(2,1)S(1)}, bf16[64,4096]{1,0:T(8,128)(2,1)S(1)}, u32[]{:S(2)}, u32[]{:S(2)}) collective-permute-start(bf16[64,4096]{1,0:T(8,128)(2,1)S(1)} %constant_dynamic-slice_fusion.26), channel_id=1, source_target_pairs={{0,4},{4,0},{8,12},{12,8},{16,20},{20,16},{24,28},{28,24},{1,5},{5... | collective-permute-start | bytes 1572872 | tf_op jit(solution)/shard_map/ppermute | solution.py:696
  183.0 46.8 %collective-permute-start.23 = (bf16[8,64,1664]{2,1,0:T(8,128)(2,1)}, bf16[8,64,1664]{2,1,0:T(8,128)(2,1)}, u32[]{:S(2)}, u32[]{:S(2)}) collective-permute-start(bf16[8,64,1664]{2,1,0:T(8,128)(2,1)} %bitcast.45.refs_11_.refs_6_.refs_7_), channel_id=1, source_target_pairs={{0,1},{1,0},{2,3},{3,2},{4,5},{5,4},{6,7},{7,6},{8,9},{9,8},{10,11... | collective-permute-start | bytes 5111816 | tf_op jit(solution)/shard_map/ppermute | solution.py:696
  183.3 47.2 %collective-permute-start.33 = (bf16[8,64,1664]{2,1,0:T(8,128)(2,1)}, bf16[8,64,1664]{2,1,0:T(8,128)(2,1)}, u32[]{:S(2)}, u32[]{:S(2)}) collective-permute-start(bf16[8,64,1664]{2,1,0:T(8,128)(2,1)} %bitcast.63.refs_11_.refs_6_.refs_7_), channel_id=1, source_target_pairs={{0,2},{1,3},{2,0},{3,1},{4,6},{5,7},{6,4},{7,5},{8,10},{9,11},{10,... | collective-permute-start | bytes 5111816 | tf_op jit(solution)/shard_map/ppermute | solution.py:696
  184.8 45.8 %collective-permute-start.25 = (bf16[8,64,1664]{2,1,0:T(8,128)(2,1)}, bf16[8,64,1664]{2,1,0:T(8,128)(2,1)}, u32[]{:S(2)}, u32[]{:S(2)}) collective-permute-start(bf16[8,64,1664]{2,1,0:T(8,128)(2,1)} %collective-permute-done.24.refs_8_.refs_9_), channel_id=1, source_target_pairs={{0,1},{1,0},{2,3},{3,2},{4,5},{5,4},{6,7},{7,6},{8,9},{9,8},{10,11... | collective-permute-start | bytes 5111816 | tf_op jit(solution)/shard_map/ppermute | solution.py:696
  229.6 330.6 %reduce-scatter.2.cloned.1.call-start = ((), (), s32[]{:S(2)}) async-start(), calls=%async_computation.4 | async-start | bytes 5242880 | tf_op jit(solution)/shard_map/reduce_scatter | solution.py:919
  229.9 39.7 %collective-permute-start.32 = (bf16[8,64,1664]{2,1,0:T(8,128)(2,1)}, bf16[8,64,1664]{2,1,0:T(8,128)(2,1)S(1)}, u32[]{:S(2)}, u32[]{:S(2)}) collective-permute-start(bf16[8,64,1664]{2,1,0:T(8,128)(2,1)} %bitcast.63.refs_11_.refs_6_.refs_7_), channel_id=1, source_target_pairs={{0,1},{1,0},{2,3},{3,2},{4,5},{5,4},{6,7},{7,6},{8,9},{9,8},{10,11... | collective-permute-start | bytes 5111816 | tf_op jit(solution)/shard_map/ppermute | solution.py:696
  230.4 39.2 %collective-permute-start.34 = (bf16[8,64,1664]{2,1,0:T(8,128)(2,1)}, bf16[8,64,1664]{2,1,0:T(8,128)(2,1)}, u32[]{:S(2)}, u32[]{:S(2)}) collective-permute-start(bf16[8,64,1664]{2,1,0:T(8,128)(2,1)} %collective-permute-done.33.refs_8_.refs_9_), channel_id=1, source_target_pairs={{0,1},{1,0},{2,3},{3,2},{4,5},{5,4},{6,7},{7,6},{8,9},{9,8},{10,11... | collective-permute-start | bytes 5111816 | tf_op jit(solution)/shard_map/ppermute | solution.py:696
  479.1 44.8 %collective-permute-start.51 = (bf16[8,64,1664]{2,1,0:T(8,128)(2,1)S(1)}, bf16[8,64,1664]{2,1,0:T(8,128)(2,1)S(1)}, u32[]{:S(2)}, u32[]{:S(2)}) collective-permute-start(bf16[8,64,1664]{2,1,0:T(8,128)(2,1)S(1)} %fusion.4.refs_24_), channel_id=1, source_target_pairs={{0,2},{1,3},{2,0},{3,1},{4,6},{5,7},{6,4},{7,5},{8,10},{9,11},{10,... | collective-permute-start | bytes 5111816 | tf_op jit(solution)/shard_map/ppermute | solution.py:696
  523.8 39.0 %collective-permute-start.50 = (bf16[2,8,64,1664]{3,2,1,0:T(8,128)(2,1)}, bf16[2,8,64,1664]{3,2,1,0:T(8,128)(2,1)}, u32[]{:S(2)}, u32[]{:S(2)}) collective-permute-start(bf16[2,8,64,1664]{3,2,1,0:T(8,128)(2,1)} %get-tuple-element.149), channel_id=1, source_target_pairs={{0,1},{1,0},{2,3},{3,2},{4,5},{5,4},{6,7},{7,6},{8,9},{9,8},{10,11... | collective-permute-start | bytes 10223624 | tf_op jit(solution)/shard_map/ppermute | solution.py:696
  551.9 54.7 %collective-permute-start.49 = (bf16[256,512]{1,0:T(8,128)(2,1)S(1)}, bf16[256,512]{1,0:T(8,128)(2,1)S(1)}, u32[]{:S(2)}, u32[]{:S(2)}) collective-permute-start(bf16[256,512]{1,0:T(8,128)(2,1)S(1)} %fusion.21), channel_id=1, source_target_pairs={{0,2},{1,3},{2,0},{3,1},{4,6},{5,7},{6,4},{7,5},{8,10},{9,11},{10,... | collective-permute-start | bytes 786440 | tf_op jit(solution)/shard_map/ppermute | solution.py:696
  561.3 85.8 %collective-permute-start.41 = (bf16[64,4096]{1,0:T(8,128)(2,1)S(1)}, bf16[64,4096]{1,0:T(8,128)(2,1)S(1)}, u32[]{:S(2)}, u32[]{:S(2)}) collective-permute-start(bf16[64,4096]{1,0:T(8,128)(2,1)S(1)} %dynamic-slice_bitcast_fusion), channel_id=1, source_target_pairs={{0,4},{4,0},{8,12},{12,8},{16,20},{20,16},{24,28},{28,24},{1,5},{5... | collective-permute-start | bytes 1572872 | tf_op jit(solution)/shard_map/ppermute | solution.py:696
  565.3 37.4 %collective-permute-start.55 = (bf16[8,64,1664]{2,1,0:T(8,128)(2,1)S(1)}, bf16[8,64,1664]{2,1,0:T(8,128)(2,1)S(1)}, u32[]{:S(2)}, u32[]{:S(2)}) collective-permute-start(bf16[8,64,1664]{2,1,0:T(8,128)(2,1)S(1)} %fusion.5.refs_24_), channel_id=1, source_target_pairs={{0,2},{1,3},{2,0},{3,1},{4,6},{5,7},{6,4},{7,5},{8,10},{9,11},{10,... | collective-permute-start | bytes 5111816 | tf_op jit(solution)/shard_map/ppermute | solution.py:696
  605.7 40.4 %collective-permute-start.70 = (bf16[2,2,64,1664]{3,2,0,1:T(8,128)(2,1)S(1)}, bf16[2,2,64,1664]{3,2,0,1:T(8,128)(2,1)S(1)}, u32[]{:S(2)}, u32[]{:S(2)}) collective-permute-start(bf16[2,2,64,1664]{3,2,0,1:T(8,128)(2,1)S(1)} %bitcast.419), channel_id=1, source_target_pairs={{0,4},{4,0},{8,12},{12,8},{16,20},{20,16},{24,28},{28,24},{1,5},{5... | collective-permute-start | bytes 2555912 | tf_op jit(solution)/shard_map/ppermute | solution.py:696
  645.6 27.5 %collective-permute-start.54 = (bf16[2,8,64,1664]{3,2,1,0:T(8,128)(2,1)}, bf16[2,8,64,1664]{3,2,1,0:T(8,128)(2,1)S(1)}, u32[]{:S(2)}, u32[]{:S(2)}) collective-permute-start(bf16[2,8,64,1664]{3,2,1,0:T(8,128)(2,1)} %get-tuple-element.154), channel_id=1, source_target_pairs={{0,1},{1,0},{2,3},{3,2},{4,5},{5,4},{6,7},{7,6},{8,9},{9,8},{10,11... | collective-permute-start | bytes 10223624 | tf_op jit(solution)/shard_map/ppermute | solution.py:696
  674.9 43.3 %collective-permute-start.66 = (bf16[8,64,1664]{2,1,0:T(8,128)(2,1)S(1)}, bf16[8,64,1664]{2,1,0:T(8,128)(2,1)}, u32[]{:S(2)}, u32[]{:S(2)}) collective-permute-start(bf16[8,64,1664]{2,1,0:T(8,128)(2,1)S(1)} %fusion.6.refs_6_), channel_id=1, source_target_pairs={{0,2},{1,3},{2,0},{3,1},{4,6},{5,7},{6,4},{7,5},{8,10},{9,11},{10,... | collective-permute-start | bytes 5111816 | tf_op jit(solution)/shard_map/ppermute | solution.py:696
  743.8 25.8 %collective-permute-start.68 = (bf16[2,64,1664]{2,1,0:T(8,128)(2,1)S(1)}, bf16[2,64,1664]{2,1,0:T(8,128)(2,1)S(1)}, u32[]{:S(2)}, u32[]{:S(2)}) collective-permute-start(bf16[2,64,1664]{2,1,0:T(8,128)(2,1)S(1)} %dynamic-slice_bitcast_fusion.2), channel_id=1, source_target_pairs={{0,8},{4,12},{8,0},{12,4},{16,24},{20,28},{24,16},{28,20},{1,9},{5... | collective-permute-start | bytes 1277960 | tf_op jit(solution)/shard_map/ppermute | solution.py:696
  (130 other events, 1266.1 us)
Sparse Core Ops, SparseCore 0:
  229.7 78.9 all-gather.1
  467.6 74.4 reduce-scatter.1

commit v2 on v1

--- a/solution.py
+++ b/solution.py
@@ -32,9 +32,10 @@
 C_Q = (0, 128)
 C_KVS = (128, 512)
 C_OUT = (512, 640)
-C_UP = (640, 1152)
-C_DOWN = (1152, 1664)
-PACKED = 1664
+ATTN = 640
+C_UP = (0, 512)
+C_DOWN = (512, 1024)
+FEED = 1024
 VMEM_LIMIT = 56 * 1024 * 1024
 
 
@@ -52,6 +53,104 @@
 
 def iota(shape, axis):
     return lax.broadcasted_iota(jnp.int32, shape, axis)
+
+
+MESH = pl.DeviceIdType.MESH
+
+
+def flipped(axis, bit):
+    mine = lax.axis_index(axis)
+    return mine + bit - 2 * bit * ((mine // bit) % 2)
+
+
+def call(kernel, outs, in_specs, out_specs, operands, after=(), flows=(), ident=0, **options):
+    used, spare, token, riders = len(operands), len(after), len(outs), len(flows)
+    asks = [flow.ask for flow in flows]
+    pairs = sorted({ask[1:] for ask in asks})
+    grid = options.get("grid")
+    scratch = list(options.pop("scratch_shapes", []))
+    far = pl.BlockSpec(memory_space=pl.ANY)
+
+    def run(*refs):
+        ins, rest = refs[:used], refs[used + spare:]
+        sends, rest = rest[:riders], rest[riders:]
+        results, token_ref, rest = rest[:token], rest[token], rest[token + 1:]
+        lands, rest = rest[:riders], rest[riders:]
+        if riders:
+            rest, (send_sems, recv_sems) = rest[:-2], rest[-2:]
+
+        def copies():
+            return [
+                pltpu.make_async_remote_copy(
+                    src_ref=sends[at],
+                    dst_ref=lands[at],
+                    send_sem=send_sems.at[at],
+                    recv_sem=recv_sems.at[at],
+                    device_id={axis: flipped(axis, bit)},
+                    device_id_type=MESH,
+                )
+                for at, (_, axis, bit) in enumerate(asks)
+            ]
+
+        def launch():
+            barrier = pltpu.get_barrier_semaphore()
+            for axis, bit in pairs:
+                pl.semaphore_signal(
+                    barrier, inc=1, device_id={axis: flipped(axis, bit)}, device_id_type=MESH
+                )
+            pl.semaphore_wait(barrier, len(pairs))
+            for copy in copies():
+                copy.start()
+
+        def settle():
+            for copy in copies():
+                copy.wait()
+
+        if riders:
+            pl.when(pl.program_id(0) == 0)(launch) if grid else launch()
+        token_ref[...] = jnp.zeros((1, 128), F32)
+        kernel(*ins, *results, *rest)
+        if riders:
+            pl.when(pl.program_id(0) == grid[0] - 1)(settle) if grid else settle()
+
+    if riders:
+        options["compiler_params"] = pltpu.CompilerParams(
+            vmem_limit_bytes=VMEM_LIMIT, collective_id=ident, has_side_effects=True
+        )
+        scratch += [pltpu.SemaphoreType.DMA((riders,))] * 2
+    token_spec = (
+        pl.BlockSpec((1, 128), lambda i: (0, 0)) if grid else pl.BlockSpec(memory_space=pltpu.VMEM)
+    )
+    got = pl.pallas_call(
+        run,
+        out_shape=list(outs)
+        + [jax.ShapeDtypeStruct((1, 128), F32)]
+        + [jax.ShapeDtypeStruct(ask[0].shape, ask[0].dtype) for ask in asks],
+        in_specs=list(in_specs) + [far] * (spare + riders),
+        out_specs=list(out_specs) + [token_spec] + [far] * riders,
+        scratch_shapes=scratch,
+        **options,
+    )(*operands, *after, *[ask[0] for ask in asks])
+    for flow, value in zip(flows, got[token + 1:]):
+        flow.give(value)
+    return (*got[:token], got[token][0, 0])
+
+
+class Flow:
+    def __init__(self, steps):
+        self.steps, self.value = steps, None
+        self.give(None)
+
+    def give(self, got):
+        try:
+            self.ask = self.steps.send(got)
+        except StopIteration as stop:
+            self.ask, self.value = None, stop.value
+
+    def finish(self):
+        while self.ask is not None:
+            self.give(swap(*self.ask))
+        return self.value
 
 
 def norm_stats(stream):
@@ -134,31 +233,43 @@
     return same & (sorted_ok | own_ok)
 
 
-def load_weights(pieces, w_ref, sems):
-    copies = [pltpu.make_async_copy(piece, w_ref.at[p], sems.at[p]) for p, piece in enumerate(pieces)]
-    for copy in copies:
-        copy.start()
+def turned(p):
+    mine = lax.axis_index("head")
+    low, high = mine % 2, (mine // 2) % 2
+    rest = mine - low - 2 * high
+    return rest + (1 - low if p & 1 else low) + 2 * (1 - high if p & 2 else high)
+
+
+def load_weights(sources, columns, layer, w_ref, sems):
+    copies = []
+    for p in range(w_ref.shape[0]):
+        if len(sources) > 1:
+            source = sources[p]
+        else:
+            source = sources[0].at[:, turned(p), layer, :, columns[0]:columns[1]]
+        copies.append(pltpu.make_async_copy(source, w_ref.at[p], sems.at[p]))
+        copies[p].start()
     return copies
 
 
-def forward_kernel(
-    me_ref, hid0_ref, hid1_ref, hid2in_ref, hid3_ref, stream_ref, w0_ref, w1_ref, w2_ref, w3_ref, nrm_ref,
-    stream_out, mid_out, hnext_out, hid_ref, kv_out, q_out, skv_out, attw_out, mixed_out,
-    permo_out, sort_out, hid2_out, upw_out, act_out,
-    w_ref, perm_scr, acc_scr, sems,
-):
+def attend_forward_kernel(layer, count, hid0_ref, hid1_ref, hid2in_ref, hid3_ref, stream_ref, nrm_ref, *refs):
+    sources = refs[:count]
+    (
+        mid_out, hid2_out, hid_ref, kv_out, q_out, skv_out, attw_out, mixed_out, permo_out, sort_out,
+        w_ref, perm_scr, acc_scr, sems,
+    ) = refs[count:]
     length, width = hid_ref.shape
     rows = stream_ref.shape[0]
     pairs = w_ref.shape[0]
     own_blocks = rows // BLOCK
     blocks = length // BLOCK
-    my = me_ref[0]
+    my = lax.axis_index("head")
     own = pl.multiple_of(my * rows, rows)
     own_block = pl.multiple_of(my * own_blocks, own_blocks)
     lower = iota((1, 128), 1) < HD
-    copies = load_weights((w0_ref, w1_ref, w2_ref, w3_ref), w_ref, sems)
+    copies = load_weights(sources, (0, ATTN), layer, w_ref, sems)
     for p, piece in enumerate((hid0_ref, hid1_ref, hid2in_ref, hid3_ref)):
-        hid_ref[pl.ds(pl.multiple_of((my ^ p) * rows, rows), rows), :] = piece[...]
+        hid_ref[pl.ds(pl.multiple_of(turned(p) * rows, rows), rows), :] = piece[...]
     for copy in copies:
         copy.wait()
 
@@ -217,9 +328,20 @@
     mid_out[...] = middle
     hid2_out[...] = norm_apply(middle, nrm_ref[0:1, :], nrm_ref[1:2, :])
 
+
+def feed_forward_kernel(layer, count, mid_ref, hid2_ref, nrm_ref, *refs):
+    sources = refs[:count]
+    stream_out, hnext_out, upw_out, act_out, w_ref, acc_scr, sems = refs[count:]
+    width = mid_ref.shape[1]
+    pairs = w_ref.shape[0]
+    copies = load_weights(sources, (ATTN, ATTN + FEED), layer, w_ref, sems)
+    acc_scr[...] = mid_ref[...]
+    for copy in copies:
+        copy.wait()
+
     def feed(j, _):
         w_up = w_ref[j, :, :, C_UP[0]:C_UP[1]].reshape(width, 512)
-        upward = dot_nn(hid2_out[...], w_up)
+        upward = dot_nn(hid2_ref[...], w_up)
         upw_out[j] = upward
         bent = jnp.tanh(GELU_C * (upward + GELU_A * upward * upward * upward))
         act = (0.5 * upward * (1.0 + bent)).astype(BF)
@@ -231,23 +353,34 @@
     lax.fori_loop(0, pairs, feed, 0)
     result = acc_scr[...]
     stream_out[...] = result
-    hnext_out[...] = norm_apply(result, nrm_ref[2:3, :], nrm_ref[3:4, :])
-
-
-def ignore_tail(kernel, used, extra):
-    def run(*refs):
-        kernel(*refs[:used], *refs[used + extra:])
-    return run
-
-
-def layer_forward(me, hidden, stream, weights, nrm, after=()):
+    hnext_out[...] = norm_apply(result, nrm_ref[0:1, :], nrm_ref[1:2, :])
+
+
+VM = pl.BlockSpec(memory_space=pltpu.VMEM)
+SM = pl.BlockSpec(memory_space=pltpu.SMEM)
+FAR = pl.BlockSpec(memory_space=pl.ANY)
+shape = jax.ShapeDtypeStruct
+
+
+def settings(flops, traffic, name):
+    return dict(
+        compiler_params=pltpu.CompilerParams(vmem_limit_bytes=VMEM_LIMIT),
+        cost_estimate=pl.CostEstimate(flops=flops, bytes_accessed=traffic, transcendentals=0),
+        name=name,
+    )
+
+
+def weight_slots(sources, pairs, columns):
+    parts, depth = (sources[0].shape[0], sources[0].shape[-2])
+    return pltpu.VMEM((pairs, parts, depth, columns), BF)
+
+
+def attend_forward(layer, hidden, stream, sources, nrm, after=(), flows=(), ident=0):
     rows, width = stream.shape
     pairs = len(hidden)
     length = rows * pairs
     own_blocks, blocks = rows // BLOCK, length // BLOCK
-    shape = jax.ShapeDtypeStruct
     outs = [
-        shape((rows, width), F32),
         shape((rows, width), F32),
         shape((rows, width), BF),
         shape((length, width), BF),
@@ -258,48 +391,79 @@
         shape((pairs, rows, 128), BF),
         shape((2 * pairs, own_blocks, blocks), F32),
         shape((pairs, blocks, 128), F32),
+    ]
+    return call(
+        functools.partial(attend_forward_kernel, layer, len(sources)),
+        outs,
+        [VM] * (pairs + 2) + [FAR] * len(sources),
+        [VM] * len(outs),
+        (*hidden, stream, nrm, *sources),
+        after,
+        flows,
+        ident,
+        scratch_shapes=[
+            weight_slots(sources, pairs, ATTN),
+            pltpu.VMEM((2 * pairs, blocks, blocks), F32),
+            pltpu.VMEM((rows, width), F32),
+            pltpu.SemaphoreType.DMA((pairs,)),
+        ],
+        **settings(18_000_000_000, 10_000_000, "attend_forward"),
+    )
+
+
+def feed_forward(layer, middle, hidden, sources, nrm, after=(), flows=(), ident=0):
+    rows, width = middle.shape
+    pairs = lax.axis_size("head")
+    outs = [
+        shape((rows, width), F32),
         shape((rows, width), BF),
         shape((pairs, rows, 512), F32),
         shape((pairs, rows, 512), BF),
     ]
-    vm = pl.BlockSpec(memory_space=pltpu.VMEM)
-    far = pl.BlockSpec(memory_space=pl.ANY)
-    return pl.pallas_call(
-        ignore_tail(forward_kernel, 2 * pairs + 3, len(after)),
-        out_shape=outs,
-        in_specs=[pl.BlockSpec(memory_space=pltpu.SMEM)] + [vm] * (pairs + 1) + [far] * pairs + [vm]
-        + [far] * len(after),
-        out_specs=[vm] * len(outs),
+    return call(
+        functools.partial(feed_forward_kernel, layer, len(sources)),
+        outs,
+        [VM] * 3 + [FAR] * len(sources),
+        [VM] * len(outs),
+        (middle, hidden, nrm, *sources),
+        after,
         scratch_shapes=[
-            pltpu.VMEM((pairs,) + weights[0].shape, BF),
-            pltpu.VMEM((2 * pairs, blocks, blocks), F32),
+            weight_slots(sources, pairs, FEED),
             pltpu.VMEM((rows, width), F32),
             pltpu.SemaphoreType.DMA((pairs,)),
         ],
-        compiler_params=pltpu.CompilerParams(vmem_limit_bytes=VMEM_LIMIT),
-        cost_estimate=pl.CostEstimate(flops=20_000_000_000, bytes_accessed=18_000_000, transcendentals=0),
-        name="layer_forward",
-    )(me, *hidden, stream, *weights, nrm, *after)
-
-
-def backward_kernel(
-    me_ref, keep_ref, near_ref, far_ref, above_ref, carry_ref, gain_above_ref,
-    w0_ref, w1_ref, w2_ref, w3_ref, gain_two_ref, mid_ref, hid_ref, kv_ref, q_ref, skv_ref, attw_ref,
-    mixed_ref, permo_ref, sort_ref, hid2_ref, upw_ref, act_ref,
-    gkeep_out, gsend_out, wkeep_out, wsend_out, carry_out, pair_above_out, pair_two_out,
-    w_ref, acc_scr, ghid_scr, gkv_scr, gsrt_scr, gq_scr, dperm_scr, low_scr, wgrad_scr, sems,
+        **settings(8_000_000_000, 8_000_000, "feed_forward"),
+    )
+
+
+def put(wgrad_scr, j, columns, value):
+    parts, depth = wgrad_scr.shape[1:3]
+    size = columns[1] - columns[0]
+    wgrad_scr[j, :, :, columns[0]:columns[1]] = value.astype(BF).reshape(parts, depth, size)
+
+
+def send_grads(wgrad_scr, keep_out, send_out, sems):
+    copies = []
+    for p in range(wgrad_scr.shape[0]):
+        out = send_out if p & 1 else keep_out
+        copies.append(pltpu.make_async_copy(wgrad_scr.at[p], out.at[p >> 1], sems.at[p]))
+        copies[p].start()
+    for copy in copies:
+        copy.wait()
+
+
+def feed_backward_kernel(
+    layer, count, keep_ref, near_ref, far_ref, above_ref, carry_ref, gain_above_ref, gain_two_ref,
+    mid_ref, hid2_ref, upw_ref, act_ref, *refs
 ):
-    length, width = hid_ref.shape
-    rows = carry_ref.shape[0]
-    pairs, parts, depth = w_ref.shape[:3]
-    own_blocks = rows // BLOCK
-    blocks = length // BLOCK
-    my = me_ref[0]
-    own = pl.multiple_of(my * rows, rows)
-    own_block = pl.multiple_of(my * own_blocks, own_blocks)
-    lower = iota((1, 128), 1) < HD
-    take = GROUP * BLOCK
-    copies = load_weights((w0_ref, w1_ref, w2_ref, w3_ref), w_ref, sems)
+    sources = refs[:count]
+    (
+        wkeep_out, wsend_out, carry_out, pair_above_out, pair_two_out,
+        w_ref, acc_scr, low_scr, wgrad_scr, sems,
+    ) = refs[count:]
+    width = carry_ref.shape[1]
+    pairs = w_ref.shape[0]
+    copies = load_weights(sources, (ATTN, ATTN + FEED), layer, w_ref, sems)
 
     dy = keep_ref[0].astype(F32) + near_ref[0].astype(F32) + far_ref[...].astype(F32)
     back, pair = norm_back(dy, above_ref[...], gain_above_ref[...])
@@ -310,10 +474,6 @@
     acc_scr[...] = jnp.zeros_like(acc_scr)
     for copy in copies:
         copy.wait()
-
-    def put(j, columns, value):
-        size = columns[1] - columns[0]
-        wgrad_scr[j, :, :, columns[0]:columns[1]] = value.astype(BF).reshape(parts, depth, size)
 
     def feed(j, _):
         low = low_scr[...]
@@ -326,8 +486,8 @@
             GELU_C * (1.0 + 3.0 * GELU_A * squared)
         )
         grad_up = (grad_act * slope).astype(BF)
-        put(j, C_DOWN, dot_tn(low, act_ref[j]))
-        put(j, C_UP, dot_tn(hid2_ref[...], grad_up))
+        put(wgrad_scr, j, C_DOWN, dot_tn(low, act_ref[j]))
+        put(wgrad_scr, j, C_UP, dot_tn(hid2_ref[...], grad_up))
         w_up = w_ref[j, :, :, C_UP[0]:C_UP[1]].reshape(width, 512)
         acc_scr[...] += dot_nt(grad_up, w_up)
         return 0
@@ -336,17 +496,41 @@
 
     back, pair = norm_back(acc_scr[...], mid_ref[...], gain_two_ref[...])
     pair_two_out[...] = pair
-    upstream = carry_out[...] + back
-    carry_out[...] = upstream
-    low_scr[...] = upstream.astype(BF)
+    carry_out[...] += back
+    send_grads(wgrad_scr, wkeep_out, wsend_out, sems)
+
+
+def attend_backward_kernel(
+    layer, count, carry_ref, hid_ref, kv_ref, q_ref, skv_ref, attw_ref, mixed_ref, permo_ref, sort_ref,
+    *refs
+):
+    sources = refs[:count]
+    (
+        gkeep_out, gsend_out, wkeep_out, wsend_out,
+        w_ref, ghid_scr, gkv_scr, gsrt_scr, gq_scr, dperm_scr, low_scr, wgrad_scr, sems,
+    ) = refs[count:]
+    length, width = hid_ref.shape
+    rows = carry_ref.shape[0]
+    pairs, parts, depth = w_ref.shape[:3]
+    own_blocks = rows // BLOCK
+    blocks = length // BLOCK
+    my = lax.axis_index("head")
+    own = pl.multiple_of(my * rows, rows)
+    own_block = pl.multiple_of(my * own_blocks, own_blocks)
+    lower = iota((1, 128), 1) < HD
+    take = GROUP * BLOCK
+    copies = load_weights(sources, (0, ATTN), layer, w_ref, sems)
+    low_scr[...] = carry_ref[...].astype(BF)
     dperm_scr[...] = jnp.zeros_like(dperm_scr)
+    for copy in copies:
+        copy.wait()
     scale_key = 1.0 / math.sqrt(HD)
 
     def attend(j, _):
         low = low_scr[...]
         w_o = w_ref[j, :, :, C_OUT[0]:C_OUT[1]].reshape(width, 128)
         grad_mixed = dot_nn(low, w_o).astype(BF)
-        put(j, C_OUT, dot_tn(low, mixed_ref[j]))
+        put(wgrad_scr, j, C_OUT, dot_tn(low, mixed_ref[j]))
         q = q_ref[j]
         zero = jnp.zeros_like(q)
         queries = []
@@ -414,66 +598,77 @@
         w = w_ref[j, :, :, C_KVS[0]:C_KVS[1]].reshape(width, C_KVS[1] - C_KVS[0])
         spread = jnp.broadcast_to(gsrt_scr[j][:, None, :], (blocks, BLOCK, 128)).reshape(length, 128)
         grad = jnp.concatenate([gkv_scr[j], spread.astype(BF)], 1)
-        put(j, C_KVS, dot_tn(hid_ref[...], grad))
+        put(wgrad_scr, j, C_KVS, dot_tn(hid_ref[...], grad))
         ghid_scr[...] += dot_nt(grad, w)
         wq = w_ref[j, :, :, C_Q[0]:C_Q[1]].reshape(width, 128)
-        put(j, C_Q, dot_tn(hid_ref[pl.ds(own, rows), :], gq_scr[j]))
+        put(wgrad_scr, j, C_Q, dot_tn(hid_ref[pl.ds(own, rows), :], gq_scr[j]))
         ghid_scr[pl.ds(own, rows), :] += dot_nt(gq_scr[j], wq)
         return 0
 
     lax.fori_loop(0, pairs, inward, 0)
     for p in range(pairs):
         out = gsend_out if p & 1 else gkeep_out
-        at = pl.multiple_of((my ^ p) * rows, rows)
+        at = pl.multiple_of(turned(p) * rows, rows)
         out[p >> 1] = ghid_scr[pl.ds(at, rows), :].astype(BF)
-    outs = []
-    for p in range(pairs):
-        out = wsend_out if p & 1 else wkeep_out
-        outs.append(pltpu.make_async_copy(wgrad_scr.at[p], out.at[p >> 1], sems.at[p]))
-        outs[p].start()
-    for copy in outs:
-        copy.wait()
-
-
-def layer_backward(me, dy, above, carry, gain_above, weights, gain_two, kept, after=()):
+    send_grads(wgrad_scr, wkeep_out, wsend_out, sems)
+
+
+def feed_backward(layer, dy, above, carry, gain_above, sources, gain_two, kept, after=(), flows=(), ident=0):
     rows, width = carry.shape
-    pairs = len(weights)
+    pairs = lax.axis_size("head")
+    slots = weight_slots(sources, pairs, FEED)
+    half = shape((pairs // 2,) + slots.shape[1:], BF)
+    outs = [half, half, shape((rows, width), F32), shape((2, width), F32), shape((2, width), F32)]
+    return call(
+        functools.partial(feed_backward_kernel, layer, len(sources)),
+        outs,
+        [VM] * (7 + len(kept)) + [FAR] * len(sources),
+        [FAR, FAR, VM, VM, VM],
+        (*dy, above, carry, gain_above, gain_two, *kept, *sources),
+        after,
+        flows,
+        ident,
+        scratch_shapes=[
+            slots,
+            pltpu.VMEM((rows, width), F32),
+            pltpu.VMEM((rows, width), BF),
+            slots,
+            pltpu.SemaphoreType.DMA((pairs,)),
+        ],
+        **settings(12_000_000_000, 12_000_000, "feed_backward"),
+    )
+
+
+def attend_backward(layer, carry, sources, kept, after=(), flows=(), ident=0):
+    rows, width = carry.shape
+    pairs = lax.axis_size("head")
     length = rows * pairs
     own_blocks, blocks = rows // BLOCK, length // BLOCK
-    shape = jax.ShapeDtypeStruct
-    outs = [
-        shape((pairs // 2, rows, width), BF),
-        shape((pairs // 2, rows, width), BF),
-        shape((pairs // 2,) + weights[0].shape, BF),
-        shape((pairs // 2,) + weights[0].shape, BF),
-        shape((rows, width), F32),
-        shape((2, width), F32),
-        shape((2, width), F32),
-    ]
-    vm = pl.BlockSpec(memory_space=pltpu.VMEM)
-    far = pl.BlockSpec(memory_space=pl.ANY)
-    return pl.pallas_call(
-        ignore_tail(backward_kernel, 8 + pairs + len(kept), len(after)),
-        out_shape=outs,
-        in_specs=[pl.BlockSpec(memory_space=pltpu.SMEM)] + [vm] * 6 + [far] * pairs
-        + [vm] * (1 + len(kept)) + [far] * len(after),
-        out_specs=[vm, vm, far, far, vm, vm, vm],
+    slots = weight_slots(sources, pairs, ATTN)
+    piece = shape((pairs // 2, rows, width), BF)
+    half = shape((pairs // 2,) + slots.shape[1:], BF)
+    return call(
+        functools.partial(attend_backward_kernel, layer, len(sources)),
+        [piece, piece, half, half],
+        [VM] * (1 + len(kept)) + [FAR] * len(sources),
+        [VM, VM, FAR, FAR],
+        (carry, *kept, *sources),
+        after,
+        flows,
+        ident,
         scratch_shapes=[
-            pltpu.VMEM((pairs,) + weights[0].shape, BF),
-            pltpu.VMEM((rows, width), F32),
+            slots,
             pltpu.VMEM((length, width), F32),
             pltpu.VMEM((pairs, length, 256), BF),
             pltpu.VMEM((pairs, blocks, 128), F32),
             pltpu.VMEM((pairs, rows, 128), BF),
             pltpu.VMEM((2 * pairs, own_blocks, length), F32),
             pltpu.VMEM((rows, width), BF),
-            pltpu.VMEM((pairs,) + weights[0].shape, BF),
+            slots,
             pltpu.SemaphoreType.DMA((pairs,)),
         ],
-        compiler_params=pltpu.CompilerParams(vmem_limit_bytes=VMEM_LIMIT),
-        cost_estimate=pl.CostEstimate(flops=30_000_000_000, bytes_accessed=25_000_000, transcendentals=0),
-        name="layer_backward",
-    )(me, *dy, above, carry, gain_above, *weights, gain_two, *kept, *after)
+        **settings(20_000_000_000, 16_000_000, "attend_backward"),
+    )
 
 
 def embed_kernel(base_ref, tok_ref, table_ref, out_ref, tall_ref):
@@ -496,25 +691,27 @@
     out_ref[...] = total.astype(BF)
 
 
-def embed_lookup(base, tokens, table):
+def embed_lookup(base, tokens, table, after=()):
     features, vocab = table.shape
     count = tokens.shape[1]
     tile = 512
-    return pl.pallas_call(
+    return call(
         embed_kernel,
-        grid=(count // tile,),
-        out_shape=jax.ShapeDtypeStruct((features, count), BF),
-        in_specs=[
+        [jax.ShapeDtypeStruct((features, count), BF)],
+        [
             pl.BlockSpec(memory_space=pltpu.SMEM),
             pl.BlockSpec((1, tile), lambda i: (0, i)),
             pl.BlockSpec((features, vocab), lambda i: (0, 0)),
         ],
-        out_specs=pl.BlockSpec((features, tile), lambda i: (0, i)),
+        [pl.BlockSpec((features, tile), lambda i: (0, i))],
+        (base, tokens, table),
+        after,
+        grid=(count // tile,),
         scratch_shapes=[pltpu.VMEM((features * (vocab // 256), 256), BF)],
         compiler_params=pltpu.CompilerParams(vmem_limit_bytes=VMEM_LIMIT),
         cost_estimate=pl.CostEstimate(flops=15_000_000_000, bytes_accessed=4_000_000, transcendentals=0),
         name="embed_lookup",
-    )(base, tokens, table)
+    )
 
 
 def embed_back_kernel(base_ref, tok_ref, grad_ref, out_ref, acc_ref):
@@ -545,23 +742,25 @@
             out_ref[:, at * 256:(at + 1) * 256] = acc_ref[at * features:(at + 1) * features, :]
 
 
-def embed_back(base, tokens, grad, vocab):
+def embed_back(base, tokens, grad, vocab, after=(), flows=(), ident=0):
     pieces, features, tile = grad.shape
-    return pl.pallas_call(
+    return call(
         embed_back_kernel,
-        grid=(pieces,),
-        out_shape=jax.ShapeDtypeStruct((features, vocab), F32),
-        in_specs=[
-            pl.BlockSpec(memory_space=pltpu.SMEM),
+        [shape((features, vocab), F32)],
+        [
+            SM,
             pl.BlockSpec((1, tile), lambda i: (0, i)),
             pl.BlockSpec((None, features, tile), lambda i: (i, 0, 0)),
         ],
-        out_specs=pl.BlockSpec((features, vocab), lambda i: (0, 0)),
+        [pl.BlockSpec((features, vocab), lambda i: (0, 0))],
+        (base, tokens, grad),
+        after,
+        flows,
+        ident,
+        grid=(pieces,),
         scratch_shapes=[pltpu.VMEM((features * (vocab // 256), 256), F32)],
-        compiler_params=pltpu.CompilerParams(vmem_limit_bytes=VMEM_LIMIT),
-        cost_estimate=pl.CostEstimate(flops=15_000_000_000, bytes_accessed=4_000_000, transcendentals=0),
-        name="embed_back",
-    )(base, tokens, grad)
+        **settings(15_000_000_000, 4_000_000, "embed_back"),
+    )
 
 
 def start_kernel(raw_ref, nrm_ref, stream_out, hid_out, *, scale):
@@ -570,16 +769,21 @@
     hid_out[...] = norm_apply(stream, nrm_ref[0:1, :], nrm_ref[1:2, :])
 
 
-def start_stream(raw, nrm):
+def start_stream(raw, nrm, after=()):
     width, rows = raw.shape
-    return pl.pallas_call(
+    vm = pl.BlockSpec(memory_space=pltpu.VMEM)
+    return call(
         functools.partial(start_kernel, scale=math.sqrt(width)),
-        out_shape=[
+        [
             jax.ShapeDtypeStruct((rows, width), F32),
             jax.ShapeDtypeStruct((rows, width), BF),
         ],
+        [vm] * 2,
+        [vm] * 2,
+        (raw, nrm),
+        after,
         name="start_stream",
-    )(raw, nrm)
+    )
 
 
 def finish_kernel(keep_ref, near_ref, far_ref, above_ref, carry_ref, gain_ref, grad_out, pair_out):
@@ -589,18 +793,23 @@
     grad_out[...] = (carry_ref[...] + back).T.astype(BF)
 
 
-def finish_stream(dy, above, carry, gain, after=()):
+def finish_stream(dy, above, carry, gain, after=(), flows=(), ident=0):
     rows, width = above.shape
     vm = pl.BlockSpec(memory_space=pltpu.VMEM)
-    return pl.pallas_call(
-        ignore_tail(finish_kernel, 6, len(after)),
-        in_specs=[vm] * 6 + [pl.BlockSpec(memory_space=pl.ANY)] * len(after),
-        out_shape=[
+    return call(
+        finish_kernel,
+        [
             jax.ShapeDtypeStruct((width, rows), BF),
             jax.ShapeDtypeStruct((2, width), F32),
         ],
+        [vm] * 6,
+        [vm] * 2,
+        (*dy, above, carry, gain),
+        after,
+        flows,
+        ident,
         name="finish_stream",
-    )(*dy, above, carry, gain, *after)
+    )
 
 
 def to_lanes(column):
@@ -718,16 +927,24 @@
     return whole.reshape((-1,) + value.shape)
 
 
-def scatter_dp(value):
-    bits = bits_of("dp")
-    value = value.reshape((2,) * len(bits) + value.shape[1:])
-    for dim, bit in reversed(list(enumerate(bits))):
-        flag = has_bit("dp", bit).astype(jnp.int32)
-        low = value.astype(BF)
-        other = swap(lax.dynamic_index_in_dim(low, 1 - flag, dim, False), "dp", bit)
-        mine = lax.dynamic_index_in_dim(low, flag, dim, False)
-        value = mine.astype(F32) + other.astype(F32)
-    return value
+def split(value, axis, bit, dim):
+    flag = has_bit(axis, bit).astype(jnp.int32)
+    low = value.astype(BF)
+    return (
+        lax.dynamic_index_in_dim(low, flag, dim, False),
+        lax.dynamic_index_in_dim(low, 1 - flag, dim, False),
+    )
+
+
+def nothing_of(value):
+    return value[(0,) * value.ndim].astype(F32) * 0.0
+
+
+def add_up(*values):
+    result = values[0].astype(F32)
+    for value in values[1:]:
+        result = result + (value.astype(F32) if value.ndim else value)
+    return result
 
 
 def sum_all(value, combine=jnp.add):
@@ -765,6 +982,10 @@
     )
 
 
+def depth_of(features):
+    return max(64, features)
+
+
 def unpack_grads(packed, sort_width):
     def cut(at, size=HD):
         return packed[:, at:at + size]
@@ -779,30 +1000,65 @@
     return (
         jnp.stack([first, second], 1),
         jnp.stack([out[HD:], out[:HD]], 0),
-        packed[:, C_UP[0]:C_UP[1]],
-        packed[:, C_DOWN[0]:C_DOWN[1]].T,
+        packed[:, ATTN + C_UP[0]:ATTN + C_UP[1]],
+        packed[:, ATTN + C_DOWN[0]:ATTN + C_DOWN[1]].T,
     )
 
 
 class Gather:
     def __init__(self, packed):
-        whole = gather_dp(packed)
-        self.mine = whole.reshape(-1, max(64, packed.shape[0]), packed.shape[1])
+        self.bits = bits_of("dp")
+        self.features = packed.shape[0]
+        value = packed.reshape((1,) * len(self.bits) + packed.shape)
+        for dim, bit in enumerate(self.bits[:-1]):
+            value = in_order(value, swap(value, "dp", bit), "dp", bit, dim)
+        self.value = value
+
+    def last(self, value):
+        dim, bit = len(self.bits) - 1, self.bits[-1]
+        return in_order(value, swap(value, "dp", bit), "dp", bit, dim)
+
+    def first_step(self):
+        self.one, two = self.value[..., :ATTN], self.value[..., ATTN:]
+        self.across = swap(self.one, "head", 2)
+        self.two = two, swap(two, "dp", self.bits[-1])
+
+    def second_step(self, token):
+        dim, bit = len(self.bits) - 1, self.bits[-1]
+        self.two = in_order(self.two[0], self.two[1] + token.astype(BF), "dp", bit, dim)
+        self.one = self.last(self.one)
+        self.across = self.last(self.across + token.astype(BF))
+
+    def pieces(self, mine, across):
+        return self.shape_pieces(mine, swap(mine, "head", 1), across, swap(across, "head", 1))
+
+    def shape_pieces(self, *got):
+        return [one.reshape(-1, depth_of(self.features), one.shape[-1]) for one in got]
 
     def finish(self):
-        return pieces_of_head(self.mine)
-
-
-class Scatter:
-    def __init__(self, keep, send, features):
-        self.keep, self.features = keep, features
-        self.near = swap(send, "head", 1)
-        self.pair = (keep[1].astype(F32) + self.near[1].astype(F32)).astype(BF)
-        self.across = swap(self.pair, "head", 2)
-
-    def finish(self):
-        whole = self.keep[0].astype(F32) + self.near[0].astype(F32) + self.across.astype(F32)
-        return scatter_dp(whole.reshape(-1, self.features, whole.shape[-1]))
+        return self.pieces(self.one, self.across)
+
+    def feed_flows(self):
+        def once(bit):
+            return (yield self.two, "head", bit)
+
+        self.flows = [Flow(once(2)), Flow(once(1))]
+        return self.flows
+
+    def finish_feed(self):
+        across, near = (flow.finish() for flow in self.flows)
+        return self.shape_pieces(self.two, near, across, swap(across, "head", 1))
+
+
+def gather_rest(packed):
+    dp, head = lax.axis_size("dp"), lax.axis_size("head")
+    layers, features, columns = packed.shape
+    whole = lax.all_gather(packed, ("dp", "head"), axis=0, tiled=True)
+    fold = depth_of(features) // features
+    if fold > 1:
+        whole = whole.reshape(dp // fold, fold, head, layers, features, columns)
+        whole = whole.transpose(0, 2, 3, 1, 4, 5)
+    return whole.reshape(dp // fold, head, layers, fold * features, columns)
 
 
 def adamw(weight, gradient, moment_one, moment_two, factor, step_rate):
@@ -834,7 +1090,6 @@
     layers = attn_in.shape[0]
     rows = length // head
     total = dp * length
-    me = my_head.astype(jnp.int32).reshape(1)
     odd = my_dp & 1
     outer = [[at for at in range(dp) if at % 2 == way] for way in range(2)]
 
@@ -848,37 +1103,53 @@
         nrm = in_order(nrm, swap(nrm, "head", bit), "head", bit, 2)
 
     low_table = table.astype(BF)
-    gathers = [
-        Gather(pack_weights(attn_in[at], attn_out[at], ffn_up[at], ffn_down[at]))
-        for at in range(layers)
+    packs = [
+        pack_weights(attn_in[at], attn_out[at], ffn_up[at], ffn_down[at]) for at in range(layers)
     ]
-    weights = [one.finish() for one in gathers]
+    leader = Gather(packs[0])
 
     half = vocab // 2
     other = swap(lax.dynamic_slice_in_dim(low_table, (1 - odd) * half, half, 1), "dp", 1)
     mine = lax.dynamic_slice_in_dim(low_table, odd * half, half, 1)
-    head_table = lax.all_gather(
-        in_order(mine, other, "dp", 1, 0), "dp", axis=0, tiled=True, axis_index_groups=outer
-    )
+    head_table = in_order(mine, other, "dp", 1, 0)
 
     base = (my_head * vocab).astype(jnp.int32).reshape(1)
-    found = embed_lookup(base, all_tokens, low_table).reshape(features, dp, head, rows)
+    found, token = embed_lookup(base, all_tokens, low_table, [leader.value])
+    leader.first_step()
+    rest_weights = gather_rest(jnp.stack(packs[1:]) + token.astype(BF))
+    found = found.reshape(features, dp, head, rows)
     for bit in (1, 2):
         flag = (my_head & bit) // bit
         found = found.reshape(features, dp, -1, 2, rows) if bit == 1 else found.reshape(features, dp, 2, rows)
         dim = 3 if bit == 1 else 2
         other = swap(lax.dynamic_index_in_dim(found, 1 - flag, dim, False), "head", bit)
         found = lax.dynamic_index_in_dim(found, flag, dim, False) + other
+    leader.second_step(token)
     found = lax.all_to_all(found, "dp", split_axis=1, concat_axis=0, tiled=True)
-    stream, hidden = start_stream(found.reshape(width, rows), nrm[0])
+    stream, hidden, token = start_stream(found.reshape(width, rows), nrm[0])
+    head_table = lax.all_gather(
+        head_table + token.astype(BF), "dp", axis=0, tiled=True, axis_index_groups=outer
+    )
+    hidden = pieces_of_head(hidden)
+    sources = [[leader.finish(), None]] + [[[rest_weights], [rest_weights]]] * (layers - 1)
 
     kept = []
     for at in range(layers):
-        pairs_now = jnp.concatenate([nrm[2 * at + 1], nrm[2 * at + 2]], 0)
-        after = tuple(one.mine for one in gathers[at + 1:at + 2])
-        got = layer_forward(me, pieces_of_head(hidden), stream, weights[at], pairs_now, after)
-        kept.append((stream, (got[1],) + tuple(got[3:])))
-        stream, hidden = got[0], got[2]
+        of = max(at - 1, 0)
+        for_attend, for_feed = sources[at]
+        middle, hidden_two, *saved, token = attend_forward(
+            of, hidden, stream, for_attend, nrm[2 * at + 1], [],
+            leader.feed_flows() if at == 0 else [],
+        )
+        if at == 0:
+            for_feed = sources[0][1] = leader.finish_feed()
+        result, hidden, upward, active, _ = feed_forward(
+            of, middle, hidden_two, for_feed, nrm[2 * at + 2]
+        )
+        kept.append((stream, (middle, hidden_two, upward, active), saved))
+        stream = result
+        if at + 1 < layers:
+            hidden = pieces_of_head(hidden)
 
     def spread_rows(value):
         for axis, bit in (("dp", 1), ("head", 2), ("head", 1)):
@@ -919,38 +1190,82 @@
     grad_half = lax.psum_scatter(
         grad_half, "dp", scatter_dimension=0, tiled=True, axis_index_groups=outer
     ).reshape(2, features, half)
-    other = swap(lax.dynamic_index_in_dim(grad_half, 1 - odd, 0, False), "dp", 1)
-    mine = lax.dynamic_index_in_dim(grad_half, odd, 0, False)
-    grad_table = in_order(mine, other, "dp", 1, 1).astype(F32)
 
     carry = jnp.zeros((rows, width), F32)
     above = stream
     pair_grads = [None] * (2 * layers + 1)
-    scatters = []
+    bits = bits_of("dp")
+
+    def shaped(value):
+        return value.reshape((2,) + (2,) * len(bits) + (features, value.shape[-1]))
+
+    def attn_steps(keep, send):
+        keep, near = shaped(keep), shaped((yield send, "head", 1))
+        across = yield add_up(keep[1], near[1]).astype(BF), "head", 2
+        here, there = split(add_up(keep[0], near[0], across), "dp", bits[-1], len(bits) - 1)
+        return add_up(here, (yield there, "dp", bits[-1]))
+
+    def feed_steps(keep, send):
+        keep, near = shaped(keep), shaped((yield send, "head", 1))
+        here, there = split(add_up(keep, near), "dp", bits[-1], len(bits))
+        value = add_up(here, (yield there, "dp", bits[-1]))
+        return add_up(value[0], (yield value[1].astype(BF), "head", 2))
+
+    def last_steps(attn, feed):
+        value = jnp.concatenate([attn.value, feed.value], -1)
+        for dim, bit in reversed(list(enumerate(bits[:-1]))):
+            here, there = split(value, "dp", bit, dim)
+            value = add_up(here, (yield there, "dp", bit))
+        return value
+
+    attns, feeds, lasts = [None] * layers, [None] * layers, [None] * layers
+
+    def active(*candidates):
+        return [flow for flow in candidates if flow is not None and flow.ask is not None]
+
+    idents = iter(range(1, 64))
     for at in reversed(range(layers)):
-        stream_in, rest = kept[at]
-        after = [one.pair for one in scatters[-1:]] + [one.across for one in scatters[-2:-1]]
-        if at == 0:
-            after.append(grad_half)
-        gkeep, gsend, wkeep, wsend, carry, pair_above, pair_two = layer_backward(
-            me, dy, above, carry, nrm[2 * at + 2, 0:1], weights[at], nrm[2 * at + 1, 0:1], rest, after
+        of = max(at - 1, 0)
+        stream_in, for_feed, for_attend = kept[at]
+        above_attn, above_feed = (attns + [None])[at + 1], (feeds + [None])[at + 1]
+        top_attn, top_feed = (attns + [None] * 2)[at + 2], (feeds + [None] * 2)[at + 2]
+        fkeep, fsend, carry, pair_above, pair_two, token = feed_backward(
+            of, dy, above, carry, nrm[2 * at + 2, 0:1], sources[at][1], nrm[2 * at + 1, 0:1], for_feed,
+            [grad_half] if at == 0 else [], active(above_attn, top_attn, top_feed), next(idents),
         )
+        feeds[at] = Flow(feed_steps(fkeep, fsend))
+        if at + 2 < layers:
+            lasts[at + 2] = Flow(last_steps(top_attn, top_feed))
+        gkeep, gsend, akeep, asend, token = attend_backward(
+            of, carry, sources[at][0], for_attend, [],
+            active(feeds[at], above_attn, above_feed, *lasts), next(idents),
+        )
+        attns[at] = Flow(attn_steps(akeep, asend))
+        dy = settle_head(gkeep, gsend)
         pair_grads[2 * at + 2] = pair_above
         pair_grads[2 * at + 1] = pair_two
-        dy = settle_head(gkeep, gsend)
-        scatters.append(Scatter(wkeep, wsend, features))
         above = stream_in
-    packed_grads = [one.finish() for one in reversed(scatters)]
-    after = [scatters[-1].pair, scatters[-2].across, packed_grads[-1]]
-    grad_stream, pair_grads[0] = finish_stream(dy, above, carry, nrm[0, 0:1], after)
+    grad_stream, pair_grads[0], token = finish_stream(
+        dy, above, carry, nrm[0, 0:1], [], active(attns[0]), next(idents)
+    )
 
     spread = lax.all_to_all(
         grad_stream.reshape(dp, features, rows), "dp", split_axis=0, concat_axis=0, tiled=True
     )
+    for flow in active(attns[0], feeds[0], attns[1], feeds[1], *lasts):
+        flow.give(swap(*flow.ask))
+    lasts[1] = Flow(last_steps(attns[1], feeds[1]))
+    other = swap(lax.dynamic_index_in_dim(grad_half, 1 - odd, 0, False), "dp", 1)
+    mine = lax.dynamic_index_in_dim(grad_half, odd, 0, False)
     spread = in_order(spread[:, None], swap(spread[:, None], "head", 1), "head", 1, 1)[:, None]
     spread = in_order(spread, swap(spread, "head", 2), "head", 2, 1)
     spread = spread.reshape(dp * head, features, rows)
-    grad_table = grad_table + math.sqrt(width) * embed_back(base, all_tokens, spread, vocab)
+    found, token = embed_back(
+        base, all_tokens, spread, vocab, [other], active(attns[0], feeds[0], *lasts), next(idents)
+    )
+    lasts[0] = Flow(last_steps(attns[0], feeds[0]))
+    grad_table = in_order(mine, other, "dp", 1, 1).astype(F32) + math.sqrt(width) * found
+    packed_grads = [flow.finish() for flow in lasts]
 
     grad_norms = sum_all(jnp.stack(pair_grads))
     grad_norms = lax.dynamic_slice_in_dim(grad_norms, my_head * norms.shape[2], norms.shape[2], 2)

time: 841 us -> 769 us (0.914)
  waiting for transfers between devices: 318 us -> 188 us
  Pallas kernels: 306 us -> 363 us
    ppermute x78 -> x62, waiting for transfers between devices: 310 us -> 187 us  [swap(): lax.ppermute(value, axis, [(at, at ^ bit) for at in range(lax.axis_size(a...]
    pallas_call x10 -> x16, Pallas kernels: 246 us -> 303 us  [call(): pl.pallas_call(run, out_shape=list(outs) + [jax.ShapeDtypeStruct((1, 128)...]
    add x0 -> x8, other arithmetic: none -> 11.5 us  [the longest x5 8.66 us: add_up(): result = result + (value.astype(F32) if value.ndim else value)]
    ppermute x78 -> x62, starting transfers between devices: 62.7 us -> 54.3 us  [swap(): lax.ppermute(value, axis, [(at, at ^ bit) for at in range(lax.axis_size(a...]
    unnamed x194 -> x212, local copies, waits for them, and re-layouts: 21.7 us -> 23.2 us
  transfers between devices with their start and end apart: 82 -> 67, of which waited for: 41 -> 41; matrix products, arithmetic and copies ran while one was open for 9% -> 10% of each run, Pallas kernels for 25% -> 28%
where the time goes in v2:
time: 769 us; the launch traced here: 759 us
  Pallas kernels  363 us (47%)
  waiting for transfers between devices  188 us (24%)
  other arithmetic  74 us (10%)
  starting transfers between devices  64.6 us (8%)
  local copies, waits for them, and re-layouts  47.8 us (6%)
  between operations  22.7 us (3%)
    pallas_call x16, Pallas kernels, call(): pl.pallas_call(run, out_shape=list(outs) + [jax.ShapeDtypeStruct((1, 128)...  303 us
    ppermute x62, waiting for transfers between devices, swap(): lax.ppermute(value, axis, [(at, at ^ bit) for at in range(lax.axis_size(a...  187 us
    ppermute x62, starting transfers between devices, swap(): lax.ppermute(value, axis, [(at, at ^ bit) for at in range(lax.axis_size(a...  54.3 us
    pallas_call x1, Pallas kernels, head_back(): pl.pallas_call(head_back_kernel, grid=(count // tile,), out_shape=[jax.Sh...  39.5 us
    unnamed x212, local copies, waits for them, and re-layouts  23.2 us
    pallas_call x1, Pallas kernels, head_stats(): pl.pallas_call(head_stats_kernel, grid=(count // tile,), out_shape=jax.Sh...  20.4 us
  transfers between devices with their start and end apart: 67, of which 41 were waited for; matrix products, arithmetic and copies ran while one was open for 10% of the time, Pallas kernels for 28%

profile of v2, /device:TPU:0, one launch (start us, length us, event | category | flops | bytes accessed | tf_op | source)
XLA Modules:
  0.0 759.1 jit_solution(17946272476060429000)
XLA Ops:
  30.1 9.9 %collective-permute-done.5 = bf16[2,1,1,64,1664]{4,3,2,1,0:T(8,128)(2,1)S(1)} collective-permute-done((bf16[2,1,1,64,1664]{4,3,2,1,0:T(8,128)(2,1)S(1)}, bf16[2,1,1,64,1664]{4,3,2,1,0:T(8,128)(2,1)S(1)}, u32[]{:S(2)}, u32[]{:S(2)}) %collective-permute-start.5) | collective-permute-done | bytes 426016 | tf_op jit(solution)/shard_map/ppermute | solution.py:905
  41.1 13.8 %embed_lookup.1 = (bf16[64,8192]{1,0:T(8,128)(2,1)}, f32[1,128]{1,0:T(1,128)}) custom-call(s32[1]{0:T(128)} %bitcast.refs_0_, s32[1,8192]{1,0:T(1,128)} %bitcast.483, bf16[64,8192]{1,0:T(8,128)(2,1)} %convert_element_type.422.refs_2_, bf16[2,2,1,64,1664]{4,3,2,1,0:T(8,128)(2,1)} %pad_maximum_fusion.1.refs_3_), custom_call_target="tpu_custom_call" | custom-call | flops 15000000512 | bytes 4000000 | tf_op jit(solution)/shard_map/embed_lookup/pallas_call | solution.py:124
  72.2 8.0 %collective-permute-done.15 = bf16[2,2,1,64,640]{4,3,2,1,0:T(8,128)(2,1)S(1)} collective-permute-done((bf16[2,2,1,64,640]{4,3,2,1,0:T(8,128)(2,1)}, bf16[2,2,1,64,640]{4,3,2,1,0:T(8,128)(2,1)S(1)}, u32[]{:S(2)}, u32[]{:S(2)}) %collective-permute-start.15) | collective-permute-done | bytes 327712 | tf_op jit(solution)/shard_map/ppermute | solution.py:905
  91.1 13.7 %collective-permute-done.16 = bf16[2,2,1,64,640]{4,3,2,1,0:T(8,128)(2,1)} collective-permute-done((bf16[2,2,1,64,640]{4,3,2,1,0:T(8,128)(2,1)}, bf16[2,2,1,64,640]{4,3,2,1,0:T(8,128)(2,1)}, u32[]{:S(2)}, u32[]{:S(2)}) %collective-permute-start.16) | collective-permute-done | bytes 327712 | tf_op jit(solution)/shard_map/ppermute | solution.py:905
  110.7 5.3 collective-permute-done.11.refs_2_
  119.4 50.5 %attend_forward.3 = (f32[256,512]{1,0:T(8,128)}, bf16[256,512]{1,0:T(8,128)(2,1)}, bf16[1024,512]{1,0:T(8,128)(2,1)}, bf16[4,1024,256]{2,1,0:T(8,128)(2,1)}, bf1...) custom-call(bf16[256,512]{1,0:T(8,128)(2,1)} %get-tuple-element.124., ...), custom_call_target="tpu_custom_call" | custom-call | flops 17999998976 | bytes 10000000 | tf_op jit(solution)/shard_map/attend_forward/pallas_call | solution.py:124
  173.8 7.4 feed_forward.3
  184.7 5.4 collective-permute-done.21.refs_2_
  192.4 23.5 %attend_forward.4 = (f32[256,512]{1,0:T(8,128)}, bf16[256,512]{1,0:T(8,128)(2,1)}, bf16[1024,512]{1,0:T(8,128)(2,1)}, bf16[4,1024,256]{2,1,0:T(8,128)(2,1)}, bf1...) custom-call(bf16[256,512]{1,0:T(8,128)(2,1)} %get-tuple-element.131., ...), custom_call_target="tpu_custom_call" | custom-call | flops 17999998976 | bytes 10000000 | tf_op jit(solution)/shard_map/attend_forward/pallas_call | solution.py:124
  215.9 7.5 feed_forward.4
  224.2 8.3 %collective-permute-done.24.refs_2_ = bf16[256,512]{1,0:T(8,128)(2,1)S(1)} collective-permute-done((bf16[256,512]{1,0:T(8,128)(2,1)}, bf16[256,512]{1,0:T(8,128)(2,1)S(1)}, u32[]{:S(2)}, u32[]{:S(2)}) %collective-permute-start.24) | collective-permute-done | bytes 262176 | tf_op jit(solution)/shard_map/ppermute | solution.py:905
  234.7 23.5 %attend_forward.5 = (f32[256,512]{1,0:T(8,128)}, bf16[256,512]{1,0:T(8,128)(2,1)}, bf16[1024,512]{1,0:T(8,128)(2,1)}, bf16[4,1024,256]{2,1,0:T(8,128)(2,1)}, bf1...) custom-call(bf16[256,512]{1,0:T(8,128)(2,1)} %get-tuple-element.135., ...), custom_call_target="tpu_custom_call" | custom-call | flops 17999998976 | bytes 10000000 | tf_op jit(solution)/shard_map/attend_forward/pallas_call | solution.py:124
  258.2 7.5 feed_forward.5
  267.1 7.2 collective-permute-done.26
  276.3 12.2 %collective-permute-done.27 = bf16[2,256,512]{2,1,0:T(8,128)(2,1)S(1)} collective-permute-done((bf16[2,256,512]{2,1,0:T(8,128)(2,1)S(1)}, bf16[2,256,512]{2,1,0:T(8,128)(2,1)S(1)}, u32[]{:S(2)}, u32[]{:S(2)}) %collective-permute-start.27) | collective-permute-done | bytes 524320 | tf_op jit(solution)/shard_map/ppermute | solution.py:905
  292.9 20.4 %head_stats.1 = f32[3,2048]{1,0:T(4,128)} custom-call(bf16[512,4096]{1,0:T(8,128)(2,1)} %all-gather.3.cloned.1.call-done.table_ref, bf16[2048,512]{1,0:T(8,128)(2,1)} %bitcast.448, s32[2048,1]{1,0:T(8,128)} %broadcast_subtract_fusion.goal_ref), custom_call_target="tpu_custom_call" | custom-call | flops 16000000000 | bytes 6000000 | tf_op jit(solution)/shard_map/head_stats/pallas_call | solution.py:838
  325.3 39.5 %head_back.1 = (bf16[2048,512]{1,0:T(8,128)(2,1)}, bf16[512,4096]{1,0:T(8,128)(2,1)}) custom-call(bf16[512,4096]{1,0:T(8,128)(2,1)} %all-gather.3.cloned.1.call-done.table_ref, bf16[2048,512]{1,0:T(8,128)(2,1)} %bitcast.449, s32[2048,1]{1,0:T(8,128)} %broadcast_subtract_fusion.goal_ref, f32[2,2048]{1,0:T(2,128)} %pad_maximum_fusion.11.line_ref), custom_call_target="tpu_custom_call" | custom-call | flops 35000000512 | bytes 14000000 | tf_op jit(solution)/shard_map/head_back/pallas_call | solution.py:880
  370.0 13.6 %collective-permute-done.34 = bf16[2,256,512]{2,1,0:T(8,128)(2,1)S(1)} collective-permute-done((bf16[2,256,512]{2,1,0:T(8,128)(2,1)S(1)}, bf16[2,256,512]{2,1,0:T(8,128)(2,1)S(1)}, u32[]{:S(2)}, u32[]{:S(2)}) %collective-permute-start.34) | collective-permute-done | bytes 524320 | tf_op jit(solution)/shard_map/ppermute | solution.py:905
  393.0 11.3 %feed_backward.3 = (bf16[2,8,64,1024]{3,2,1,0:T(8,128)(2,1)}, bf16[2,8,64,1024]{3,2,1,0:T(8,128)(2,1)}, f32[256,512]{1,0:T(8,128)}, f32[2,512]{1,0:T(2,128)}, f32[2,512]{1,0:T(2,128)}, /*index=5*/f32[1,128]{1,0:T(1,128)}) custom-call(f32[1,256,512]{2,1,0:T(8,128)} %slice.784.refs_0_, bf16[1,256,512]{2,1,0:T(8,128)(2,1)} %broadcast_in_dim.24.refs_1_, ...), custom_call_target="tpu_custom_call" | custom-call | flops 12000000000 | bytes 12000000 | tf_op jit(solution)/shard_map/feed_backward/pallas_call | solution.py:124
  404.4 30.0 %attend_backward.3 = (bf16[2,256,512]{2,1,0:T(8,128)(2,1)}, bf16[2,256,512]{2,1,0:T(8,128)(2,1)}, bf16[2,8,64,640]{3,2,1,0:T(8,128)(2,1)}, bf16[2,8,64,640]{3,2,...) custom-call(f32[256,512]{1,0:T(8,128)} %get-tuple-element.145.refs_0_.refs_4_, ...), custom_call_target="tpu_custom_call" | custom-call | flops 20000000000 | bytes 16000000 | tf_op jit(solution)/shard_map/attend_backward/pallas_call | solution.py:124
  449.0 11.6 %feed_backward.4 = (bf16[2,8,64,1024]{3,2,1,0:T(8,128)(2,1)}, bf16[2,8,64,1024]{3,2,1,0:T(8,128)(2,1)}, f32[256,512]{1,0:T(8,128)}, f32[2,512]{1,0:T(2,128)}, f3...) custom-call(bf16[2,256,512]{2,1,0:T(8,128)(2,1)} %get-tuple-element.155.refs_0_, ...), custom_call_target="tpu_custom_call" | custom-call | flops 12000000000 | bytes 12000000 | tf_op jit(solution)/shard_map/feed_backward/pallas_call | solution.py:124
  463.0 31.2 %attend_backward.4 = (bf16[2,256,512]{2,1,0:T(8,128)(2,1)}, bf16[2,256,512]{2,1,0:T(8,128)(2,1)}, bf16[2,8,64,640]{3,2,1,0:T(8,128)(2,1)}, bf16[2,8,64,640]{3,2,...) custom-call(f32[256,512]{1,0:T(8,128)} %get-tuple-element.160.refs_0, ...), custom_call_target="tpu_custom_call" | custom-call | flops 20000000000 | bytes 16000000 | tf_op jit(solution)/shard_map/attend_backward/pallas_call | solution.py:124
  508.6 17.3 %feed_backward.5 = (bf16[2,8,64,1024]{3,2,1,0:T(8,128)(2,1)}, bf16[2,8,64,1024]{3,2,1,0:T(8,128)(2,1)}, f32[256,512]{1,0:T(8,128)}, f32[2,512]{1,0:T(2,128)}, f3...) custom-call(bf16[2,256,512]{2,1,0:T(8,128)(2,1)} %get-tuple-element., ...), custom_call_target="tpu_custom_call" | custom-call | flops 12000000000 | bytes 12000000 | tf_op jit(solution)/shard_map/feed_backward/pallas_call | solution.py:124
  531.6 32.0 %attend_backward.5 = (bf16[2,256,512]{2,1,0:T(8,128)(2,1)}, bf16[2,256,512]{2,1,0:T(8,128)(2,1)}, bf16[2,8,64,640]{3,2,1,0:T(8,128)(2,1)}, bf16[2,8,64,640]{3,2,...) custom-call(f32[256,512]{1,0:T(8,128)} %get-tuple-element.181.refs_0, ...), custom_call_target="tpu_custom_call" | custom-call | flops 20000000000 | bytes 16000000 | tf_op jit(solution)/shard_map/attend_backward/pallas_call | solution.py:124
  574.8 9.9 %collective-permute-done.56 = bf16[64,1664]{1,0:T(8,128)(2,1)S(1)} collective-permute-done((bf16[64,1664]{1,0:T(8,128)(2,1)S(1)}, bf16[64,1664]{1,0:T(8,128)(2,1)S(1)}, u32[]{:S(2)}, u32[]{:S(2)}) %collective-permute-start.56) | collective-permute-done | bytes 213024 | tf_op jit(solution)/shard_map/ppermute | solution.py:905
  594.7 5.8 finish_stream.1
  601.5 7.0 collective-permute-done.46
  638.3 10.9 %collective-permute-done.44 = bf16[2,2,2,64,640]{4,3,1,0,2:T(8,128)(2,1)} collective-permute-done((bf16[2,2,2,64,640]{4,3,1,0,2:T(8,128)(2,1)}, bf16[2,2,2,64,640]{4,3,1,0,2:T(8,128)(2,1)}, u32[]{:S(2)}, u32[]{:S(2)}) %collective-permute-start.44) | collective-permute-done | bytes 655392 | tf_op jit(solution)/shard_map/ppermute | solution.py:905
  656.7 27.9 %embed_back.1 = (f32[64,8192]{1,0:T(8,128)}, f32[1,128]{1,0:T(1,128)}, bf16[2,2,64,640]{3,2,1,0:T(8,128)(2,1)}, bf16[2,2,64,1024]{3,2,1,0:T(8,128)(2,1)}, bf16[2,64,1664]{2,1,0:T(8,128)(2,1)}) custom-call(s32[1]{0:T(128)} %bitcast.refs_0_, s32[1,8192]{1,0:T(1,128)} %bitcast.484, bf16[32,64,256]{2,1,0:T(8,128)(2,1)} %bitcast.452, ...), custom_call_target="tpu_custom_call" | custom-call | flops 15000000512 | bytes 4000000 | tf_op jit(solution)/shard_map/embed_back/pallas_call | solution.py:124
  689.6 6.3 collective-permute-done.55
  703.3 5.4 collective-permute-done.54
  742.4 5.6 fusion.103
  (561 shorter events, 247.3 us)
Async XLA Ops:
  7.2 184.5 %all-gather.5.cloned.1.call-start = ((), (), s32[]{:S(2)}) async-start(), calls=%async_computation.4 | async-start | bytes 14057472 | tf_op jit(solution)/shard_map/all_gather | solution.py:1056
  16.8 12.3 %collective-permute-start.4 = (bf16[1,1,1,64,1664]{4,3,2,1,0:T(8,128)(2,1)S(1)}, bf16[1,1,1,64,1664]{4,3,2,1,0:T(8,128)(2,1)S(1)}, u32[]{:S(2)}, u32[]{:S(2)}) collective-permute-start(bf16[1,1,1,64,1664]{4,3,2,1,0:T(8,128)(2,1)S(1)} %bitcast.459), channel_id=1, source_target_pairs={{0,16},{4,20},{8,24},{12,28},{16,0},{20,4},{24,8},{28,12},{1,17},{... | collective-permute-start | bytes 638984 | tf_op jit(solution)/shard_map/ppermute | solution.py:905
  29.2 10.8 %collective-permute-start.5 = (bf16[2,1,1,64,1664]{4,3,2,1,0:T(8,128)(2,1)S(1)}, bf16[2,1,1,64,1664]{4,3,2,1,0:T(8,128)(2,1)S(1)}, u32[]{:S(2)}, u32[]{:S(2)}) collective-permute-start(bf16[2,1,1,64,1664]{4,3,2,1,0:T(8,128)(2,1)S(1)} %pad_maximum_fusion.8), channel_id=1, source_target_pairs={{0,8},{4,12},{8,0},{12,4},{16,24},{20,28},{24,16},{28,20},{1,9},{5... | collective-permute-start | bytes 1277960 | tf_op jit(solution)/shard_map/ppermute | solution.py:905
  67.8 22.1 %collective-permute-start.13 = (bf16[2,2,1,64,640]{4,3,2,1,0:T(8,128)(2,1)}, bf16[2,2,1,64,640]{4,3,2,1,0:T(8,128)(2,1)}, u32[]{:S(2)}, u32[]{:S(2)}) collective-permute-start(bf16[2,2,1,64,640]{4,3,2,1,0:T(8,128)(2,1)} %fusion.39), channel_id=1, source_target_pairs={{0,4},{4,0},{8,12},{12,8},{16,20},{20,16},{24,28},{28,24},{1,5},{5... | collective-permute-start | bytes 983048 | tf_op jit(solution)/shard_map/ppermute | solution.py:905
  69.3 10.9 %collective-permute-start.15 = (bf16[2,2,1,64,640]{4,3,2,1,0:T(8,128)(2,1)}, bf16[2,2,1,64,640]{4,3,2,1,0:T(8,128)(2,1)S(1)}, u32[]{:S(2)}, u32[]{:S(2)}) collective-permute-start(bf16[2,2,1,64,640]{4,3,2,1,0:T(8,128)(2,1)} %fusion.39), channel_id=1, source_target_pairs={{0,2},{1,3},{2,0},{3,1},{4,6},{5,7},{6,4},{7,5},{8,10},{9,11},{10,... | collective-permute-start | bytes 983048 | tf_op jit(solution)/shard_map/ppermute | solution.py:905
  71.0 12.7 %collective-permute-start.7 = (bf16[64,8,256]{2,1,0:T(8,128)(2,1)S(1)}, bf16[64,8,256]{2,1,0:T(8,128)(2,1)S(1)}, u32[]{:S(2)}, u32[]{:S(2)}) collective-permute-start(bf16[64,8,256]{2,1,0:T(8,128)(2,1)S(1)} %dynamic-slice_bitcast_fusion.6), channel_id=1, source_target_pairs={{0,2},{1,3},{2,0},{3,1},{4,6},{5,7},{6,4},{7,5},{8,10},{9,11},{10,... | collective-permute-start | bytes 786440 | tf_op jit(solution)/shard_map/ppermute | solution.py:905
  71.6 44.4 %collective-permute-start.18 = (bf16[2,2,1,64,1024]{4,3,2,1,0:T(8,128)(2,1)S(1)}, bf16[2,2,1,64,1024]{4,3,2,1,0:T(8,128)(2,1)}, u32[]{:S(2)}, u32[]{:S(2)}) collective-permute-start(bf16[2,2,1,64,1024]{4,3,2,1,0:T(8,128)(2,1)S(1)} %fusion.21), channel_id=1, source_target_pairs={{0,4},{4,0},{8,12},{12,8},{16,20},{20,16},{24,28},{28,24},{1,5},{5... | collective-permute-start | bytes 1572872 | tf_op jit(solution)/shard_map/ppermute | solution.py:905
  81.0 23.8 %collective-permute-start.16 = (bf16[2,2,1,64,640]{4,3,2,1,0:T(8,128)(2,1)}, bf16[2,2,1,64,640]{4,3,2,1,0:T(8,128)(2,1)}, u32[]{:S(2)}, u32[]{:S(2)}) collective-permute-start(bf16[2,2,1,64,640]{4,3,2,1,0:T(8,128)(2,1)} %broadcast_add_fusion), channel_id=1, source_target_pairs={{0,4},{4,0},{8,12},{12,8},{16,20},{20,16},{24,28},{28,24},{1,5},{5... | collective-permute-start | bytes 983048 | tf_op jit(solution)/shard_map/ppermute | solution.py:905
  84.5 21.4 %all-to-all-start = ((bf16[64,8,256]{2,0,1:T(8,128)(2,1)}), bf16[64,8,256]{2,0,1:T(8,128)(2,1)S(1)}, u32[]{:S(2)}, u32[]{:S(2)}) async-start(bf16[64,8,256]{2,0,1:T(8,128)(2,1)} %copy.229), calls=%async_computation | async-start | bytes 524288 | tf_op jit(solution)/shard_map/all_to_all | solution.py:1128
  89.7 203.2 %all-gather.3.cloned.1.call-start = ((), (), s32[]{:S(2)}) async-start(), calls=%async_computation.3 | async-start | bytes 5242880 | tf_op jit(solution)/shard_map/all_gather | solution.py:1130
  91.1 27.3 %collective-permute-start.14 = (bf16[2,2,2,64,640]{4,3,2,1,0:T(8,128)(2,1)S(1)}, bf16[2,2,2,64,640]{4,3,2,1,0:T(8,128)(2,1)}, u32[]{:S(2)}, u32[]{:S(2)}) collective-permute-start(bf16[2,2,2,64,640]{4,3,2,1,0:T(8,128)(2,1)S(1)} %pad_maximum_fusion.5), channel_id=1, source_target_pairs={{0,1},{1,0},{2,3},{3,2},{4,5},{5,4},{6,7},{7,6},{8,9},{9,8},{10,11... | collective-permute-start | bytes 1966088 | tf_op jit(solution)/shard_map/ppermute | solution.py:905
  170.1 14.4 %collective-permute-start = (bf16[64,4096]{1,0:T(8,128)(2,1)S(1)}, bf16[64,4096]{1,0:T(8,128)(2,1)S(1)}, u32[]{:S(2)}, u32[]{:S(2)}) collective-permute-start(bf16[64,4096]{1,0:T(8,128)(2,1)S(1)} %constant_dynamic-slice_fusion.23), channel_id=1, source_target_pairs={{0,4},{4,0},{8,12},{12,8},{16,20},{20,16},{24,28},{28,24},{1,5},{5... | collective-permute-start | bytes 1572872 | tf_op jit(solution)/shard_map/ppermute | solution.py:905
  181.3 8.8 %collective-permute-start.21 = (bf16[256,512]{1,0:T(8,128)(2,1)}, bf16[256,512]{1,0:T(8,128)(2,1)S(1)}, u32[]{:S(2)}, u32[]{:S(2)}) collective-permute-start(bf16[256,512]{1,0:T(8,128)(2,1)} %get-tuple-element.131.refs_0_), channel_id=1, source_target_pairs={{0,2},{1,3},{2,0},{3,1},{4,6},{5,7},{6,4},{7,5},{8,10},{9,11},{10,... | collective-permute-start | bytes 786440 | tf_op jit(solution)/shard_map/ppermute | solution.py:905
  191.4 316.5 %reduce-scatter.2.cloned.1.call-start = ((), (), s32[]{:S(2)}) async-start(), calls=%async_computation.5 | async-start | bytes 5242880 | tf_op jit(solution)/shard_map/reduce_scatter | solution.py:1190
  223.4 9.0 %collective-permute-start.24 = (bf16[256,512]{1,0:T(8,128)(2,1)}, bf16[256,512]{1,0:T(8,128)(2,1)S(1)}, u32[]{:S(2)}, u32[]{:S(2)}) collective-permute-start(bf16[256,512]{1,0:T(8,128)(2,1)} %get-tuple-element.135.refs_0_), channel_id=1, source_target_pairs={{0,2},{1,3},{2,0},{3,1},{4,6},{5,7},{6,4},{7,5},{8,10},{9,11},{10,... | collective-permute-start | bytes 786440 | tf_op jit(solution)/shard_map/ppermute | solution.py:905
  223.8 8.7 %collective-permute-start.23 = (bf16[256,512]{1,0:T(8,128)(2,1)}, bf16[256,512]{1,0:T(8,128)(2,1)S(1)}, u32[]{:S(2)}, u32[]{:S(2)}) collective-permute-start(bf16[256,512]{1,0:T(8,128)(2,1)} %get-tuple-element.135.refs_0_), channel_id=1, source_target_pairs={{0,1},{1,0},{2,3},{3,2},{4,5},{5,4},{6,7},{7,6},{8,9},{9,8},{10,11... | collective-permute-start | bytes 786440 | tf_op jit(solution)/shard_map/ppermute | solution.py:905
  265.7 8.6 %collective-permute-start.26 = (bf16[256,512]{1,0:T(8,128)(2,1)}, bf16[256,512]{1,0:T(8,128)(2,1)S(1)}, u32[]{:S(2)}, u32[]{:S(2)}) collective-permute-start(bf16[256,512]{1,0:T(8,128)(2,1)} %get-tuple-element.139), channel_id=1, source_target_pairs={{0,4},{4,0},{8,12},{12,8},{16,20},{20,16},{24,28},{28,24},{1,5},{5... | collective-permute-start | bytes 786440 | tf_op jit(solution)/shard_map/ppermute | solution.py:905
  275.3 13.2 %collective-permute-start.27 = (bf16[2,256,512]{2,1,0:T(8,128)(2,1)S(1)}, bf16[2,256,512]{2,1,0:T(8,128)(2,1)S(1)}, u32[]{:S(2)}, u32[]{:S(2)}) collective-permute-start(bf16[2,256,512]{2,1,0:T(8,128)(2,1)S(1)} %get-tuple-element.424), channel_id=1, source_target_pairs={{0,2},{1,3},{2,0},{3,1},{4,6},{5,7},{6,4},{7,5},{8,10},{9,11},{10,... | collective-permute-start | bytes 1572872 | tf_op jit(solution)/shard_map/ppermute | solution.py:905
  369.6 14.0 %collective-permute-start.34 = (bf16[2,256,512]{2,1,0:T(8,128)(2,1)S(1)}, bf16[2,256,512]{2,1,0:T(8,128)(2,1)S(1)}, u32[]{:S(2)}, u32[]{:S(2)}) collective-permute-start(bf16[2,256,512]{2,1,0:T(8,128)(2,1)S(1)} %fusion.17), channel_id=1, source_target_pairs={{0,2},{1,3},{2,0},{3,1},{4,6},{5,7},{6,4},{7,5},{8,10},{9,11},{10,... | collective-permute-start | bytes 1572872 | tf_op jit(solution)/shard_map/ppermute | solution.py:905
  499.3 8.6 %collective-permute-start.39 = (bf16[256,512]{1,0:T(8,128)(2,1)S(1)}, bf16[256,512]{1,0:T(8,128)(2,1)S(1)}, u32[]{:S(2)}, u32[]{:S(2)}) collective-permute-start(bf16[256,512]{1,0:T(8,128)(2,1)S(1)} %fusion.41), channel_id=1, source_target_pairs={{0,2},{1,3},{2,0},{3,1},{4,6},{5,7},{6,4},{7,5},{8,10},{9,11},{10,... | collective-permute-start | bytes 786440 | tf_op jit(solution)/shard_map/ppermute | solution.py:905
  563.6 23.1 %collective-permute-start.40 = (bf16[2,256,512]{2,1,0:T(8,128)(2,1)}, bf16[2,256,512]{2,1,0:T(8,128)(2,1)S(1)}, u32[]{:S(2)}, u32[]{:S(2)}) collective-permute-start(bf16[2,256,512]{2,1,0:T(8,128)(2,1)} %get-tuple-element.198), channel_id=1, source_target_pairs={{0,1},{1,0},{2,3},{3,2},{4,5},{5,4},{6,7},{7,6},{8,9},{9,8},{10,11... | collective-permute-start | bytes 1572872 | tf_op jit(solution)/shard_map/ppermute | solution.py:905
  564.5 45.6 %collective-permute-start.32 = (bf16[64,4096]{1,0:T(8,128)(2,1)}, bf16[64,4096]{1,0:T(8,128)(2,1)}, u32[]{:S(2)}, u32[]{:S(2)}) collective-permute-start(bf16[64,4096]{1,0:T(8,128)(2,1)} %dynamic-slice_bitcast_fusion.3), channel_id=1, source_target_pairs={{0,4},{4,0},{8,12},{12,8},{16,20},{20,16},{24,28},{28,24},{1,5},{5... | collective-permute-start | bytes 1572872 | tf_op jit(solution)/shard_map/ppermute | solution.py:905
  569.7 63.8 %collective-permute-start.45 = (bf16[2,2,2,64,1024]{4,3,2,1,0:T(8,128)(2,1)}, bf16[2,2,2,64,1024]{4,3,2,1,0:T(8,128)(2,1)}, u32[]{:S(2)}, u32[]{:S(2)}) collective-permute-start(bf16[2,2,2,64,1024]{4,3,2,1,0:T(8,128)(2,1)} %dynamic-slice_bitcast_fusion), channel_id=1, source_target_pairs={{0,4},{4,0},{8,12},{12,8},{16,20},{20,16},{24,28},{28,24},{1,5},{5... | collective-permute-start | bytes 3145736 | tf_op jit(solution)/shard_map/ppermute | solution.py:905
  570.8 43.2 %collective-permute-start.47 = (bf16[2,2,64,1024]{3,2,0,1:T(8,128)(2,1)S(1)}, bf16[2,2,64,1024]{3,2,0,1:T(8,128)(2,1)}, u32[]{:S(2)}, u32[]{:S(2)}) collective-permute-start(bf16[2,2,64,1024]{3,2,0,1:T(8,128)(2,1)S(1)} %fusion.20), channel_id=1, source_target_pairs={{0,2},{1,3},{2,0},{3,1},{4,6},{5,7},{6,4},{7,5},{8,10},{9,11},{10,... | collective-permute-start | bytes 1572872 | tf_op jit(solution)/shard_map/ppermute | solution.py:905
  572.4 12.3 %collective-permute-start.56 = (bf16[64,1664]{1,0:T(8,128)(2,1)S(1)}, bf16[64,1664]{1,0:T(8,128)(2,1)S(1)}, u32[]{:S(2)}, u32[]{:S(2)}) collective-permute-start(bf16[64,1664]{1,0:T(8,128)(2,1)S(1)} %dynamic-slice_bitcast_fusion.7), channel_id=1, source_target_pairs={{0,16},{4,20},{8,24},{12,28},{16,0},{20,4},{24,8},{28,12},{1,17},{... | collective-permute-start | bytes 638984 | tf_op jit(solution)/shard_map/ppermute | solution.py:905
  584.7 23.8 %collective-permute-start.46 = (bf16[2,2,64,640]{3,2,0,1:T(8,128)(2,1)S(1)}, bf16[2,2,64,640]{3,2,0,1:T(8,128)(2,1)S(1)}, u32[]{:S(2)}, u32[]{:S(2)}) collective-permute-start(bf16[2,2,64,640]{3,2,0,1:T(8,128)(2,1)S(1)} %dynamic-slice_bitcast_fusion.4), channel_id=1, source_target_pairs={{0,4},{4,0},{8,12},{12,8},{16,20},{20,16},{24,28},{28,24},{1,5},{5... | collective-permute-start | bytes 983048 | tf_op jit(solution)/shard_map/ppermute | solution.py:905
  615.2 18.1 %all-to-all-start.1 = ((bf16[8,64,256]{2,1,0:T(8,128)(2,1)}), bf16[8,64,256]{2,1,0:T(8,128)(2,1)}, u32[]{:S(2)}, u32[]{:S(2)}) async-start(bf16[8,64,256]{2,1,0:T(8,128)(2,1)} %bitcast.129), calls=%async_computation.2 | async-start | bytes 524288 | tf_op jit(solution)/shard_map/all_to_all | solution.py:1252
  631.2 18.0 %collective-permute-start.44 = (bf16[2,2,2,64,640]{4,3,1,0,2:T(8,128)(2,1)}, bf16[2,2,2,64,640]{4,3,1,0,2:T(8,128)(2,1)}, u32[]{:S(2)}, u32[]{:S(2)}) collective-permute-start(bf16[2,2,2,64,640]{4,3,1,0,2:T(8,128)(2,1)} %copy.251), channel_id=1, source_target_pairs={{0,2},{1,3},{2,0},{3,1},{4,6},{5,7},{6,4},{7,5},{8,10},{9,11},{10,... | collective-permute-start | bytes 1966088 | tf_op jit(solution)/shard_map/ppermute | solution.py:905
  636.2 19.3 %collective-permute-start.43 = (bf16[8,1,2,64,256]{4,3,2,1,0:T(8,128)(2,1)S(1)}, bf16[8,1,2,64,256]{4,3,2,1,0:T(8,128)(2,1)S(1)}, u32[]{:S(2)}, u32[]{:S(2)}) collective-permute-start(bf16[8,1,2,64,256]{4,3,2,1,0:T(8,128)(2,1)S(1)} %maximum_bitcast_fusion), channel_id=1, source_target_pairs={{0,2},{1,3},{2,0},{3,1},{4,6},{5,7},{6,4},{7,5},{8,10},{9,11},{10,... | collective-permute-start | bytes 1572872 | tf_op jit(solution)/shard_map/ppermute | solution.py:905
  686.1 12.6 %collective-permute-start.53 = (bf16[2,64,1664]{2,1,0:T(8,128)(2,1)S(1)}, bf16[2,64,1664]{2,1,0:T(8,128)(2,1)S(1)}, u32[]{:S(2)}, u32[]{:S(2)}) collective-permute-start(bf16[2,64,1664]{2,1,0:T(8,128)(2,1)S(1)} %fusion.24), channel_id=1, source_target_pairs={{0,8},{4,12},{8,0},{12,4},{16,24},{20,28},{24,16},{28,20},{1,9},{5... | collective-permute-start | bytes 1277960 | tf_op jit(solution)/shard_map/ppermute | solution.py:905
  686.6 9.4 %collective-permute-start.55 = (bf16[64,1664]{1,0:T(8,128)(2,1)S(1)}, bf16[64,1664]{1,0:T(8,128)(2,1)}, u32[]{:S(2)}, u32[]{:S(2)}) collective-permute-start(bf16[64,1664]{1,0:T(8,128)(2,1)S(1)} %dynamic-slice_bitcast_fusion.8), channel_id=1, source_target_pairs={{0,16},{4,20},{8,24},{12,28},{16,0},{20,4},{24,8},{28,12},{1,17},{... | collective-permute-start | bytes 638984 | tf_op jit(solution)/shard_map/ppermute | solution.py:905
  698.9 9.8 %collective-permute-start.54 = (bf16[64,1664]{1,0:T(8,128)(2,1)S(1)}, bf16[64,1664]{1,0:T(8,128)(2,1)S(1)}, u32[]{:S(2)}, u32[]{:S(2)}) collective-permute-start(bf16[64,1664]{1,0:T(8,128)(2,1)S(1)} %dynamic-slice_bitcast_fusion.9), channel_id=1, source_target_pairs={{0,16},{4,20},{8,24},{12,28},{16,0},{20,4},{24,8},{28,12},{1,17},{... | collective-permute-start | bytes 638984 | tf_op jit(solution)/shard_map/ppermute | solution.py:905
  (124 other events, 885.9 us)
Sparse Core Ops, SparseCore 0:
  56.5 125.3 all-gather.4
  191.5 80.9 all-gather.2
  386.0 76.1 reduce-scatter.1

commit v3 on v2

--- a/solution.py
+++ b/solution.py
@@ -63,10 +63,27 @@
     return mine + bit - 2 * bit * ((mine // bit) % 2)
 
 
-def call(kernel, outs, in_specs, out_specs, operands, after=(), flows=(), ident=0, **options):
+def remote(source, target, send_sem, recv_sem, axis, bit):
+    return pltpu.make_async_remote_copy(
+        src_ref=source,
+        dst_ref=target,
+        send_sem=send_sem,
+        recv_sem=recv_sem,
+        device_id={axis: flipped(axis, bit)},
+        device_id_type=MESH,
+    )
+
+
+HEADS = (("head", 1), ("head", 2))
+
+
+def call(
+    kernel, outs, in_specs, out_specs, operands, after=(), flows=(), ident=0, greet=(), greet_all=None, hold=None, **options
+):
     used, spare, token, riders = len(operands), len(after), len(outs), len(flows)
     asks = [flow.ask for flow in flows]
-    pairs = sorted({ask[1:] for ask in asks})
+    pairs = sorted({ask[1:] for ask in asks} | set(greet))
+    pairs = [pair for pair in pairs if pair[0] != greet_all]
     grid = options.get("grid")
     scratch = list(options.pop("scratch_shapes", []))
     far = pl.BlockSpec(memory_space=pl.ANY)
@@ -80,15 +97,10 @@
             rest, (send_sems, recv_sems) = rest[:-2], rest[-2:]
 
         def copies():
+            if not riders:
+                return []
             return [
-                pltpu.make_async_remote_copy(
-                    src_ref=sends[at],
-                    dst_ref=lands[at],
-                    send_sem=send_sems.at[at],
-                    recv_sem=recv_sems.at[at],
-                    device_id={axis: flipped(axis, bit)},
-                    device_id_type=MESH,
-                )
+                remote(sends[at], lands[at], send_sems.at[at], recv_sems.at[at], axis, bit)
                 for at, (_, axis, bit) in enumerate(asks)
             ]
 
@@ -98,7 +110,15 @@
                 pl.semaphore_signal(
                     barrier, inc=1, device_id={axis: flipped(axis, bit)}, device_id_type=MESH
                 )
-            pl.semaphore_wait(barrier, len(pairs))
+            others = lax.axis_size(greet_all) - 1 if greet_all else 0
+            for step in range(others):
+                peer = (lax.axis_index(greet_all) + step + 1) % (others + 1)
+                pl.semaphore_signal(barrier, inc=1, device_id={greet_all: peer}, device_id_type=MESH)
+            pl.semaphore_wait(barrier, len(pairs) + others)
+            if hold is None:
+                fly()
+
+        def fly():
             for copy in copies():
                 copy.start()
 
@@ -106,17 +126,25 @@
             for copy in copies():
                 copy.wait()
 
-        if riders:
+        if riders or greet:
             pl.when(pl.program_id(0) == 0)(launch) if grid else launch()
         token_ref[...] = jnp.zeros((1, 128), F32)
-        kernel(*ins, *results, *rest)
+        if hold is not None and grid:
+            if riders:
+                pl.when(pl.program_id(0) == hold)(fly)
+            kernel(*ins, *results, *rest)
+        elif hold is not None:
+            kernel(*ins, *results, *rest, fly=fly)
+        else:
+            kernel(*ins, *results, *rest)
         if riders:
             pl.when(pl.program_id(0) == grid[0] - 1)(settle) if grid else settle()
 
-    if riders:
+    if riders or greet:
         options["compiler_params"] = pltpu.CompilerParams(
             vmem_limit_bytes=VMEM_LIMIT, collective_id=ident, has_side_effects=True
         )
+    if riders:
         scratch += [pltpu.SemaphoreType.DMA((riders,))] * 2
     token_spec = (
         pl.BlockSpec((1, 128), lambda i: (0, 0)) if grid else pl.BlockSpec(memory_space=pltpu.VMEM)
@@ -138,19 +166,23 @@
 
 class Flow:
     def __init__(self, steps):
-        self.steps, self.value = steps, None
+        self.steps, self.parts = steps, None
         self.give(None)
+
+    @property
+    def value(self):
+        return self.parts
 
     def give(self, got):
         try:
             self.ask = self.steps.send(got)
         except StopIteration as stop:
-            self.ask, self.value = None, stop.value
+            self.ask, self.parts = None, stop.value
 
     def finish(self):
         while self.ask is not None:
             self.give(swap(*self.ask))
-        return self.value
+        return add_up(*self.parts) if isinstance(self.parts, tuple) else self.parts
 
 
 def norm_stats(stream):
@@ -442,31 +474,33 @@
     wgrad_scr[j, :, :, columns[0]:columns[1]] = value.astype(BF).reshape(parts, depth, size)
 
 
-def send_grads(wgrad_scr, keep_out, send_out, sems):
-    copies = []
-    for p in range(wgrad_scr.shape[0]):
-        out = send_out if p & 1 else keep_out
-        copies.append(pltpu.make_async_copy(wgrad_scr.at[p], out.at[p >> 1], sems.at[p]))
-        copies[p].start()
-    for copy in copies:
-        copy.wait()
+def take_part(ref, index, features):
+    depth = ref.shape[1]
+    if depth == features:
+        return ref[index].astype(F32)
+    fold = depth // features
+    whole = ref[index // fold].astype(F32).reshape(fold, features, ref.shape[2])
+    return jnp.sum(jnp.where(iota(whole.shape, 0) == index % fold, whole, 0.0), 0)
+
+
+def near_first(at):
+    return 2 * at + 1 - 5 * (at // 2)
 
 
 def feed_backward_kernel(
-    layer, count, keep_ref, near_ref, far_ref, above_ref, carry_ref, gain_above_ref, gain_two_ref,
+    layer, count, dy_ref, above_ref, carry_ref, gain_above_ref, gain_two_ref,
     mid_ref, hid2_ref, upw_ref, act_ref, *refs
 ):
     sources = refs[:count]
     (
-        wkeep_out, wsend_out, carry_out, pair_above_out, pair_two_out,
-        w_ref, acc_scr, low_scr, wgrad_scr, sems,
+        here_out, there_out, carry_out, pair_above_out, pair_two_out,
+        w_ref, acc_scr, low_scr, wgrad_scr, near_scr, sems, send_sems, recv_sems,
     ) = refs[count:]
     width = carry_ref.shape[1]
     pairs = w_ref.shape[0]
     copies = load_weights(sources, (ATTN, ATTN + FEED), layer, w_ref, sems)
 
-    dy = keep_ref[0].astype(F32) + near_ref[0].astype(F32) + far_ref[...].astype(F32)
-    back, pair = norm_back(dy, above_ref[...], gain_above_ref[...])
+    back, pair = norm_back(dy_ref[...], above_ref[...], gain_above_ref[...])
     pair_above_out[...] = pair
     upstream = carry_ref[...] + back
     carry_out[...] = upstream
@@ -475,7 +509,13 @@
     for copy in copies:
         copy.wait()
 
-    def feed(j, _):
+    def to_near(at):
+        return remote(
+            wgrad_scr.at[near_first(at)], near_scr.at[at], send_sems.at[at], recv_sems.at[at], *HEADS[0]
+        )
+
+    def feed(at, _):
+        j = near_first(at)
         low = low_scr[...]
         w_dn = w_ref[j, :, :, C_DOWN[0]:C_DOWN[1]].reshape(width, 512)
         grad_act = dot_nn(low, w_dn)
@@ -490,6 +530,11 @@
         put(wgrad_scr, j, C_UP, dot_tn(hid2_ref[...], grad_up))
         w_up = w_ref[j, :, :, C_UP[0]:C_UP[1]].reshape(width, 512)
         acc_scr[...] += dot_nt(grad_up, w_up)
+
+        @pl.when(at < pairs // 2)
+        def _():
+            to_near(at).start()
+
         return 0
 
     lax.fori_loop(0, pairs, feed, 0)
@@ -497,7 +542,15 @@
     back, pair = norm_back(acc_scr[...], mid_ref[...], gain_two_ref[...])
     pair_two_out[...] = pair
     carry_out[...] += back
-    send_grads(wgrad_scr, wkeep_out, wsend_out, sems)
+    odd = lax.axis_index("dp") % 2
+    for x in range(pairs // 2):
+        to_near(x).wait()
+        for at in range(here_out.shape[1]):
+            for out, way in ((here_out, odd), (there_out, 1 - odd)):
+                out[x, at] = (
+                    take_part(wgrad_scr.at[2 * x], 2 * at + way, out.shape[2])
+                    + take_part(near_scr.at[x], 2 * at + way, out.shape[2])
+                ).astype(BF)
 
 
 def attend_backward_kernel(
@@ -506,8 +559,9 @@
 ):
     sources = refs[:count]
     (
-        gkeep_out, gsend_out, wkeep_out, wsend_out,
-        w_ref, ghid_scr, gkv_scr, gsrt_scr, gq_scr, dperm_scr, low_scr, wgrad_scr, sems,
+        dy_out, mine_out, across_out,
+        w_ref, ghid_scr, gkv_scr, gsrt_scr, gq_scr, dperm_scr, low_scr, wgrad_scr, near_scr,
+        gsend_scr, gnear_scr, afar_scr, gfar_scr, sems, send_sems, recv_sems,
     ) = refs[count:]
     length, width = hid_ref.shape
     rows = carry_ref.shape[0]
@@ -594,46 +648,83 @@
 
     ghid_scr[...] = jnp.zeros_like(ghid_scr)
 
+    def inward_of(j):
+        spread = jnp.broadcast_to(gsrt_scr[j][:, None, :], (blocks, BLOCK, 128)).reshape(length, 128)
+        return jnp.concatenate([gkv_scr[j], spread.astype(BF)], 1)
+
     def inward(j, _):
         w = w_ref[j, :, :, C_KVS[0]:C_KVS[1]].reshape(width, C_KVS[1] - C_KVS[0])
-        spread = jnp.broadcast_to(gsrt_scr[j][:, None, :], (blocks, BLOCK, 128)).reshape(length, 128)
-        grad = jnp.concatenate([gkv_scr[j], spread.astype(BF)], 1)
-        put(wgrad_scr, j, C_KVS, dot_tn(hid_ref[...], grad))
-        ghid_scr[...] += dot_nt(grad, w)
+        ghid_scr[...] += dot_nt(inward_of(j), w)
         wq = w_ref[j, :, :, C_Q[0]:C_Q[1]].reshape(width, 128)
-        put(wgrad_scr, j, C_Q, dot_tn(hid_ref[pl.ds(own, rows), :], gq_scr[j]))
         ghid_scr[pl.ds(own, rows), :] += dot_nt(gq_scr[j], wq)
         return 0
 
     lax.fori_loop(0, pairs, inward, 0)
-    for p in range(pairs):
-        out = gsend_out if p & 1 else gkeep_out
-        at = pl.multiple_of(turned(p) * rows, rows)
-        out[p >> 1] = ghid_scr[pl.ds(at, rows), :].astype(BF)
-    send_grads(wgrad_scr, wkeep_out, wsend_out, sems)
-
-
-def feed_backward(layer, dy, above, carry, gain_above, sources, gain_two, kept, after=(), flows=(), ident=0):
+
+    def piece(p):
+        return ghid_scr[pl.ds(pl.multiple_of(turned(p) * rows, rows), rows), :]
+
+    for p in (1, 3):
+        gsend_scr[p // 2] = piece(p).astype(BF)
+    near = remote(gsend_scr, gnear_scr, send_sems.at[2], recv_sems.at[2], *HEADS[0])
+    near.start()
+
+    def to_near(at):
+        return remote(
+            wgrad_scr.at[near_first(at)], near_scr.at[at], send_sems.at[at], recv_sems.at[at], *HEADS[0]
+        )
+
+    def weigh(at, _):
+        j = near_first(at)
+        put(wgrad_scr, j, C_KVS, dot_tn(hid_ref[...], inward_of(j)))
+        put(wgrad_scr, j, C_Q, dot_tn(hid_ref[pl.ds(own, rows), :], gq_scr[j]))
+
+        @pl.when(at < pairs // 2)
+        def _():
+            to_near(at).start()
+
+        return 0
+
+    lax.fori_loop(0, pairs // 2, weigh, 0)
+    near.wait()
+    afar_scr[...] = (piece(2) + gnear_scr[1].astype(F32)).astype(BF)
+    far = remote(afar_scr, gfar_scr, send_sems.at[3], recv_sems.at[3], *HEADS[1])
+    far.start()
+    lax.fori_loop(pairs // 2, pairs, weigh, 0)
+    for x in range(pairs // 2):
+        to_near(x).wait()
+        out = across_out if x else mine_out
+        for at in range(parts):
+            out[at] = (wgrad_scr[2 * x, at].astype(F32) + near_scr[x, at].astype(F32)).astype(BF)
+    far.wait()
+    dy_out[...] = piece(0) + gnear_scr[0].astype(F32) + gfar_scr[...].astype(F32)
+
+
+def feed_backward(layer, dy, above, carry, gain_above, sources, gain_two, kept, features, after=(), flows=(), ident=0):
     rows, width = carry.shape
     pairs = lax.axis_size("head")
     slots = weight_slots(sources, pairs, FEED)
-    half = shape((pairs // 2,) + slots.shape[1:], BF)
+    half = shape((pairs // 2, lax.axis_size("dp") // 2, features, FEED), BF)
     outs = [half, half, shape((rows, width), F32), shape((2, width), F32), shape((2, width), F32)]
     return call(
         functools.partial(feed_backward_kernel, layer, len(sources)),
         outs,
-        [VM] * (7 + len(kept)) + [FAR] * len(sources),
-        [FAR, FAR, VM, VM, VM],
-        (*dy, above, carry, gain_above, gain_two, *kept, *sources),
+        [VM] * (5 + len(kept)) + [FAR] * len(sources),
+        [VM] * 5,
+        (dy, above, carry, gain_above, gain_two, *kept, *sources),
         after,
         flows,
         ident,
+        HEADS[:1],
         scratch_shapes=[
             slots,
             pltpu.VMEM((rows, width), F32),
             pltpu.VMEM((rows, width), BF),
             slots,
+            pltpu.VMEM((pairs // 2,) + slots.shape[1:], BF),
             pltpu.SemaphoreType.DMA((pairs,)),
+            pltpu.SemaphoreType.DMA((2,)),
+            pltpu.SemaphoreType.DMA((2,)),
         ],
         **settings(12_000_000_000, 12_000_000, "feed_backward"),
     )
@@ -645,17 +736,16 @@
     length = rows * pairs
     own_blocks, blocks = rows // BLOCK, length // BLOCK
     slots = weight_slots(sources, pairs, ATTN)
-    piece = shape((pairs // 2, rows, width), BF)
-    half = shape((pairs // 2,) + slots.shape[1:], BF)
     return call(
         functools.partial(attend_backward_kernel, layer, len(sources)),
-        [piece, piece, half, half],
+        [shape((rows, width), F32)] + [shape(slots.shape[1:], BF)] * 2,
         [VM] * (1 + len(kept)) + [FAR] * len(sources),
-        [VM, VM, FAR, FAR],
+        [VM] * 3,
         (carry, *kept, *sources),
         after,
         flows,
         ident,
+        HEADS,
         scratch_shapes=[
             slots,
             pltpu.VMEM((length, width), F32),
@@ -665,7 +755,14 @@
             pltpu.VMEM((2 * pairs, own_blocks, length), F32),
             pltpu.VMEM((rows, width), BF),
             slots,
+            pltpu.VMEM((pairs // 2,) + slots.shape[1:], BF),
+            pltpu.VMEM((2, rows, width), BF),
+            pltpu.VMEM((2, rows, width), BF),
+            pltpu.VMEM((rows, width), BF),
+            pltpu.VMEM((rows, width), BF),
             pltpu.SemaphoreType.DMA((pairs,)),
+            pltpu.SemaphoreType.DMA((4,)),
+            pltpu.SemaphoreType.DMA((4,)),
         ],
         **settings(20_000_000_000, 16_000_000, "attend_backward"),
     )
@@ -714,11 +811,40 @@
     )
 
 
-def embed_back_kernel(base_ref, tok_ref, grad_ref, out_ref, acc_ref):
+def stages_of_all():
+    return [(axis, bit) for axis in ("head", "dp") for bit in reversed(bits_of(axis))]
+
+
+def embed_back_kernel(
+    base_ref, tok_ref, grad_ref, head_ref, *refs, scale, count_pairs
+):
+    pair_refs = refs[:count_pairs]
+    out_ref, square_out, pair_out, acc_ref, sum_scr, come_scr, send_sems, recv_sems = refs[count_pairs:]
     features = grad_ref.shape[0]
     count = grad_ref.shape[1]
     bins = acc_ref.shape[0] // features
     step = pl.program_id(0)
+    stages = stages_of_all()
+    first_hop = pl.num_programs(0) // 2
+
+    def hop(at):
+        return remote(sum_scr, come_scr.at[at], send_sems.at[at], recv_sems.at[at], *stages[at])
+
+    for at in range(len(stages) + 1):
+
+        @pl.when(step == first_hop + 3 * at)
+        def _(at=at):
+            if at == 0:
+                for place, pair_ref in enumerate(pair_refs):
+                    sum_scr[place] = pair_ref[...]
+            else:
+                hop(at - 1).wait()
+                sum_scr[...] += come_scr[at - 1]
+            if at < len(stages):
+                hop(at).start()
+            else:
+                pair_out[...] = sum_scr[...]
+
     local = tok_ref[...] - base_ref[0]
     high, low = local >> 8, local & 255
     hot = (iota((256, count), 0) == low).astype(BF)
@@ -738,29 +864,198 @@
 
     @pl.when(step == pl.num_programs(0) - 1)
     def _():
+        squares = jnp.zeros((features, 256), F32)
         for at in range(bins):
-            out_ref[:, at * 256:(at + 1) * 256] = acc_ref[at * features:(at + 1) * features, :]
-
-
-def embed_back(base, tokens, grad, vocab, after=(), flows=(), ident=0):
+            cut = slice(at * 256, (at + 1) * 256)
+            total = scale * acc_ref[at * features:(at + 1) * features, :] + head_ref[:, cut].astype(F32)
+            out_ref[:, cut] = total
+            squares += total * total
+        square_out[...] = squares
+
+
+def embed_back(base, tokens, grad, head_grad, pair_grads, after=(), flows=(), ident=0):
     pieces, features, tile = grad.shape
+    vocab = head_grad.shape[1]
+    width = pair_grads[0].shape[1]
+    count_pairs = len(pair_grads)
+    all_pairs = (count_pairs, 2, width)
+    stages = len(stages_of_all())
+    still = lambda i: (0, 0)
     return call(
-        embed_back_kernel,
-        [shape((features, vocab), F32)],
+        functools.partial(embed_back_kernel, scale=math.sqrt(width), count_pairs=count_pairs),
+        [shape((features, vocab), F32), shape((features, 256), F32), shape(all_pairs, F32)],
         [
             SM,
             pl.BlockSpec((1, tile), lambda i: (0, i)),
             pl.BlockSpec((None, features, tile), lambda i: (i, 0, 0)),
+            pl.BlockSpec((features, vocab), still),
+        ]
+        + [pl.BlockSpec((2, width), still)] * count_pairs,
+        [
+            pl.BlockSpec((features, vocab), still),
+            pl.BlockSpec((features, 256), still),
+            pl.BlockSpec(all_pairs, lambda i: (0, 0, 0)),
         ],
-        [pl.BlockSpec((features, vocab), lambda i: (0, 0))],
-        (base, tokens, grad),
+        (base, tokens, grad, head_grad, *pair_grads),
         after,
         flows,
         ident,
+        tuple(stages_of_all()),
         grid=(pieces,),
-        scratch_shapes=[pltpu.VMEM((features * (vocab // 256), 256), F32)],
+        scratch_shapes=[
+            pltpu.VMEM((features * (vocab // 256), 256), F32),
+            pltpu.VMEM(all_pairs, F32),
+            pltpu.VMEM((stages,) + all_pairs, F32),
+            pltpu.SemaphoreType.DMA((stages,)),
+            pltpu.SemaphoreType.DMA((stages,)),
+        ],
         **settings(15_000_000_000, 4_000_000, "embed_back"),
     )
+
+
+def last_sums_kernel(
+    a_ref, a_more_ref, b_ref, b_more_ref, other_ref, other_more_ref, third_ref, square_ref, pair_ref, loss_ref,
+    out_ref, other_out, total_out,
+    sum_scr, low_scr, come_scr, part_scr, parts_scr, send_sems, recv_sems, part_send, part_recv, *, bits, shared
+):
+    count = a_ref.shape[0]
+    for t in range(count):
+        sum_scr[t, :, 0:ATTN] = a_ref[t].astype(F32) + a_more_ref[t].astype(F32)
+        sum_scr[t, :, ATTN:] = b_ref[t].astype(F32) + b_more_ref[t].astype(F32)
+    at = 0
+    place = 0
+    for bit in bits:
+        flag = (lax.axis_index("dp") // bit) % 2
+        half = count // 2
+        copies = []
+        for t in range(half):
+            low_scr[place + t] = sum_scr[2 * t + 1 - flag].astype(BF)
+            copies.append(
+                remote(
+                    low_scr.at[place + t], come_scr.at[place + t], send_sems.at[at], recv_sems.at[at], "dp", bit
+                )
+            )
+            copies[t].start()
+            at += 1
+        if place == 0:
+            other = other_ref[...].astype(F32) + other_more_ref[...].astype(F32)
+            other_out[...] = other
+            pairs = pair_ref[...]
+            square = jnp.sum(square_ref[...]) + jnp.sum(pairs * pairs) / shared + jnp.sum(other * other)
+            for piece in third_ref:
+                value = piece[...]
+                square = square + jnp.sum(value * value)
+        for t in range(half):
+            copies[t].wait()
+            sum_scr[t] = sum_scr[2 * t + flag] + come_scr[place + t].astype(F32)
+        place += half
+        count = half
+    value = sum_scr[0]
+    out_ref[...] = value
+    square = square + jnp.sum(value * value)
+    row, lane = iota((8, 128), 0), iota((8, 128), 1)
+    part_scr[...] = jnp.where(
+        row == 0, jnp.where(lane == 0, square, jnp.where(lane == 1, loss_ref[...], 0.0)), 0.0
+    )
+    for at, (axis, bit) in enumerate(stages_of_all()):
+        hop = remote(part_scr, parts_scr.at[at], part_send.at[at], part_recv.at[at], axis, bit)
+        hop.start()
+        hop.wait()
+        part_scr[...] += parts_scr[at]
+    total_out[...] = part_scr[...]
+
+
+def last_sums(attn, feed, other, thirds, squares, pair_grads, loss, bits, ident):
+    def flat(value):
+        return value.reshape((-1,) + value.shape[-2:])
+
+    operands = [flat(one) for one in (*attn, *feed)] + [*other]
+    count, features = operands[0].shape[:2]
+    columns = ATTN + FEED
+    stages = len(stages_of_all())
+    one = shape((features, columns), F32)
+    fixed, extra = len(operands), len(thirds)
+
+    def kernel(*refs):
+        last_sums_kernel(
+            *refs[:fixed], refs[fixed:fixed + extra], *refs[fixed + extra:], bits=bits,
+            shared=lax.axis_size("dp") * lax.axis_size("head"),
+        )
+
+    return call(
+        kernel,
+        [one, one, shape((8, 128), F32)],
+        [VM] * (fixed + extra + 3),
+        [VM] * 3,
+        (*operands, *thirds, squares, pair_grads, loss),
+        ident=ident,
+        greet=tuple(stages_of_all()),
+        scratch_shapes=[
+            pltpu.VMEM((count, features, columns), F32),
+            pltpu.VMEM((count - 1, features, columns), BF),
+            pltpu.VMEM((count - 1, features, columns), BF),
+            pltpu.VMEM((8, 128), F32),
+            pltpu.VMEM((stages, 8, 128), F32),
+            pltpu.SemaphoreType.DMA((count - 1,)),
+            pltpu.SemaphoreType.DMA((count - 1,)),
+            pltpu.SemaphoreType.DMA((stages,)),
+            pltpu.SemaphoreType.DMA((stages,)),
+        ],
+        **settings(1_000_000, 4_000_000, "last_sums"),
+    )
+
+
+def update_kernel(layers, sort_width, total_ref, table_grad_ref, norm_grad_ref, *refs):
+    packs, ins, outs = refs[:layers], list(refs[layers:layers + 18]), list(refs[layers + 18:])
+    norm = jnp.sqrt(total_ref[0:1, 0:1])
+    factor = jnp.minimum(1.0, CLIP_LIMIT / (norm + 1e-06))
+
+    def run(member, at, grad):
+        weight_ref, first_ref, second_ref = ins[3 * member:3 * member + 3]
+        rate = RATE_NORM if member == 5 else RATE_MATRIX
+        scale = factor.reshape((1,) * grad.ndim)
+        new, one, two = adamw(weight_ref[at], grad, first_ref[at], second_ref[at], scale, rate)
+        results = (new, one, two) if member == 5 else (new, new.astype(BF), one, two)
+        for target, result in zip(outs[4 * member:], results):
+            target[at] = result
+
+    def table_part(step, _):
+        at = (slice(None), pl.ds(pl.multiple_of(step * 512, 512), 512))
+        run(0, at, table_grad_ref[at])
+        return 0
+
+    lax.fori_loop(0, table_grad_ref.shape[1] // 512, table_part, 0)
+    kv, srt = C_KVS[0], C_KVS[0] + 256
+    starts = ((0, kv, kv + 64, srt), (64, kv + 192, kv + 128, srt + sort_width))
+    for layer, pack in enumerate(packs):
+        for h, (q, k, v, sort) in enumerate(starts):
+            parts = [pack[:, at:at + HD] for at in (q, k, v)] + [pack[:, sort:sort + sort_width]]
+            run(1, (layer, slice(None), h, slice(None)), jnp.concatenate(parts, 1))
+        out = pack[:, C_OUT[0]:C_OUT[1]].T
+        for h in range(2):
+            run(2, (layer, h), out[(1 - h) * HD:(2 - h) * HD])
+        run(3, layer, pack[:, ATTN + C_UP[0]:ATTN + C_UP[1]])
+        run(4, layer, pack[:, ATTN + C_DOWN[0]:ATTN + C_DOWN[1]])
+    run(5, slice(None), norm_grad_ref[...])
+
+
+def update(totals, packs, table_grad, norm_grad, sort_width, members):
+    outs = []
+    for weight, _, _ in members[:-1]:
+        full = shape(weight.shape, F32)
+        outs += [full, shape(weight.shape, BF), full, full]
+    outs += [shape(norm_grad.shape, F32)] * 3
+    operands = [totals, table_grad, norm_grad, *packs]
+    for member in members:
+        operands += member
+    return call(
+        functools.partial(update_kernel, len(packs), sort_width),
+        outs,
+        [VM] * len(operands),
+        [VM] * len(outs),
+        operands,
+        **settings(1_000_000, 30_000_000, "update"),
+    )[:-1]
 
 
 def start_kernel(raw_ref, nrm_ref, stream_out, hid_out, *, scale):
@@ -786,28 +1081,71 @@
     )
 
 
-def finish_kernel(keep_ref, near_ref, far_ref, above_ref, carry_ref, gain_ref, grad_out, pair_out):
-    dy = keep_ref[0].astype(F32) + near_ref[0].astype(F32) + far_ref[...].astype(F32)
-    back, pair = norm_back(dy, above_ref[...], gain_ref[...])
+def finish_kernel(
+    dy_ref, above_ref, carry_ref, gain_ref, pair_out, spread_out, piece_scr, own_sem, dp_send, dp_recv, send_sems, recv_sems, *, fly
+):
+    back, pair = norm_back(dy_ref[...], above_ref[...], gain_ref[...])
     pair_out[...] = pair
-    grad_out[...] = (carry_ref[...] + back).T.astype(BF)
+    piece_scr[...] = (carry_ref[...] + back).T.reshape(piece_scr.shape).astype(BF)
+    count = piece_scr.shape[0]
+    mine = lax.axis_index("dp")
+    here = spread_out.at[0, mine]
+    copies = [pltpu.make_async_copy(piece_scr.at[mine], here, own_sem)]
+    for step in range(count - 1):
+        peer = (mine + step + 1) % count
+        copies.append(
+            pltpu.make_async_remote_copy(
+                src_ref=piece_scr.at[peer],
+                dst_ref=here,
+                send_sem=dp_send.at[step],
+                recv_sem=dp_recv.at[step],
+                device_id={"dp": peer},
+                device_id_type=MESH,
+            )
+        )
+    for copy in copies:
+        copy.start()
+    fly()
+    for copy in copies:
+        copy.wait()
+
+    def hop(at, source, target, axis, bit):
+        return remote(spread_out.at[source], spread_out.at[target], send_sems.at[at], recv_sems.at[at], axis, bit)
+
+    far, near = hop(0, 0, 2, *HEADS[1]), hop(1, 0, 1, *HEADS[0])
+    far.start()
+    near.start()
+    far.wait()
+    cross = hop(2, 2, 3, *HEADS[0])
+    cross.start()
+    near.wait()
+    cross.wait()
 
 
 def finish_stream(dy, above, carry, gain, after=(), flows=(), ident=0):
     rows, width = above.shape
-    vm = pl.BlockSpec(memory_space=pltpu.VMEM)
+    dp, pairs = lax.axis_size("dp"), lax.axis_size("head")
+    features = width // dp
     return call(
         finish_kernel,
-        [
-            jax.ShapeDtypeStruct((width, rows), BF),
-            jax.ShapeDtypeStruct((2, width), F32),
-        ],
-        [vm] * 6,
-        [vm] * 2,
-        (*dy, above, carry, gain),
+        [shape((2, width), F32), shape((pairs, dp, features, rows), BF)],
+        [VM] * 4,
+        [VM, FAR],
+        (dy, above, carry, gain),
         after,
         flows,
         ident,
+        HEADS,
+        "dp",
+        hold=0,
+        scratch_shapes=[
+            pltpu.VMEM((dp, features, rows), BF),
+            pltpu.SemaphoreType.DMA,
+            pltpu.SemaphoreType.DMA((dp - 1,)),
+            pltpu.SemaphoreType.DMA((dp - 1,)),
+            pltpu.SemaphoreType.DMA((3,)),
+            pltpu.SemaphoreType.DMA((3,)),
+        ],
         name="finish_stream",
     )
 
@@ -820,85 +1158,211 @@
     return jnp.broadcast_to(line, (128, line.shape[1])).T[:, 0:1]
 
 
-def head_stats_kernel(table_ref, final_ref, goal_ref, stat_out):
-    logits = dot_nn(final_ref[...], table_ref[...])
-    top = jnp.max(logits, 1, keepdims=True)
-    total = jnp.sum(jnp.exp(logits - top), 1, keepdims=True)
-    hit = iota(logits.shape, 1) == goal_ref[...]
-    pick = jnp.sum(jnp.where(hit, logits, 0.0), 1, keepdims=True)
-    stat_out[0:1, :] = to_lanes(top)
-    stat_out[1:2, :] = to_lanes(total)
-    stat_out[2:3, :] = to_lanes(pick)
-
-
-def head_stats(table, final_all, goals):
-    width, vocab = table.shape
-    count = final_all.shape[0]
-    tile = 256
-    return pl.pallas_call(
-        head_stats_kernel,
-        grid=(count // tile,),
-        out_shape=jax.ShapeDtypeStruct((3, count), F32),
-        in_specs=[
-            pl.BlockSpec((width, vocab), lambda i: (0, 0)),
-            pl.BlockSpec((tile, width), lambda i: (i, 0)),
-            pl.BlockSpec((tile, 1), lambda i: (i, 0)),
+SLOTS = 8
+SLOT_HOPS = (("head", 1, 4), ("head", 2, 2), ("dp", 1, 1))
+GREET_SLOTS = HEADS + (("dp", 1),)
+
+
+def head_forward_kernel(
+    final_ref, table_ref, goal_ref, count_ref, rows_out, line_out, loss_out,
+    rows_scr, stat_scr, come_scr, send_sems, recv_sems, stat_send, stat_recv
+):
+    def hop(at, source, target, which):
+        axis, bit, _ = SLOT_HOPS[which]
+        return remote(rows_scr.at[source], rows_scr.at[target], send_sems.at[at], recv_sems.at[at], axis, bit)
+
+    rows_scr[0] = final_ref[...]
+    core_own, low_own = hop(0, 0, 4, 0), hop(1, 0, 1, 2)
+    far = [hop(2, 0, 2, 1), hop(3, 1, 3, 1)]
+    core = [hop(4, 1, 5, 0), hop(5, 2, 6, 0), hop(6, 3, 7, 0)]
+    core_own.start()
+    low_own.start()
+    far[0].start()
+
+    def slot(at, _):
+        @pl.when(at == 1)
+        def _():
+            core_own.wait()
+            low_own.wait()
+            far[1].start()
+            core[0].start()
+
+        @pl.when(at == 3)
+        def _():
+            core[0].wait()
+
+        @pl.when(at == 4)
+        def _():
+            far[0].wait()
+            core[1].start()
+            far[1].wait()
+            core[2].start()
+
+        @pl.when(at == 6)
+        def _():
+            core[1].wait()
+            core[2].wait()
+
+        late = at // 4
+        place = (1 - late) * (at // 2 + 4 * (at % 2)) + late * (2 + at % 2 + 4 * ((at // 2) % 2))
+        logits = dot_nn(rows_scr[place], table_ref[...])
+        top = jnp.max(logits, 1, keepdims=True)
+        sums = jnp.sum(jnp.exp(logits - top), 1, keepdims=True)
+        hit = iota(logits.shape, 1).astype(F32) == to_rows(goal_ref[place])
+        pick = jnp.sum(jnp.where(hit, logits, 0.0), 1, keepdims=True)
+        stat_scr[place, 0:1, :] = to_lanes(top)
+        stat_scr[place, 1:2, :] = to_lanes(sums)
+        stat_scr[place, 2:3, :] = to_lanes(pick)
+        return 0
+
+    lax.fori_loop(0, SLOTS, slot, 0)
+    for at, (axis, bit, mask) in enumerate(SLOT_HOPS):
+        meet = remote(stat_scr, come_scr.at[at], stat_send.at[at], stat_recv.at[at], axis, bit)
+        meet.start()
+        meet.wait()
+        for place in range(SLOTS):
+            mine, theirs = stat_scr[place], come_scr[at, place ^ mask]
+            peak = jnp.maximum(mine[0:1], theirs[0:1])
+            stat_scr[place, 1:2, :] = mine[1:2] * jnp.exp(mine[0:1] - peak) + theirs[1:2] * jnp.exp(
+                theirs[0:1] - peak
+            )
+            stat_scr[place, 0:1, :] = peak
+            stat_scr[place, 2:3, :] = mine[2:3] + theirs[2:3]
+    loss = jnp.zeros((1, 1), F32)
+    for place in range(SLOTS):
+        mine = stat_scr[place]
+        lse = mine[0:1] + jnp.log(mine[1:2])
+        line_out[place, 0:1, :] = lse
+        line_out[place, 1:2, :] = count_ref[place]
+        loss += jnp.sum((lse - mine[2:3]) * count_ref[place], 1, keepdims=True)
+    loss_out[...] = loss
+    rows_out[...] = rows_scr[...]
+
+
+def head_forward(final, table, goals, counted, ident):
+    rows, width = final.shape
+    hops = len(SLOT_HOPS)
+    return call(
+        head_forward_kernel,
+        [shape((SLOTS, rows, width), BF), shape((SLOTS, 2, rows), F32), shape((1, 1), F32)],
+        [VM] * 4,
+        [VM] * 3,
+        (final, table, goals, counted),
+        ident=ident,
+        greet=GREET_SLOTS,
+        scratch_shapes=[
+            pltpu.VMEM((SLOTS, rows, width), BF),
+            pltpu.VMEM((SLOTS, 8, rows), F32),
+            pltpu.VMEM((hops, SLOTS, 8, rows), F32),
+            pltpu.SemaphoreType.DMA((7,)),
+            pltpu.SemaphoreType.DMA((7,)),
+            pltpu.SemaphoreType.DMA((hops,)),
+            pltpu.SemaphoreType.DMA((hops,)),
         ],
-        out_specs=pl.BlockSpec((3, tile), lambda i: (0, i)),
-        compiler_params=pltpu.CompilerParams(vmem_limit_bytes=VMEM_LIMIT),
-        cost_estimate=pl.CostEstimate(flops=16_000_000_000, bytes_accessed=6_000_000, transcendentals=0),
-        name="head_stats",
-    )(table, final_all, goals)
-
-
-def head_back_kernel(table_ref, final_ref, goal_ref, line_ref, gfin_out, gtab_out, acc_ref):
-    step = pl.program_id(0)
-    logits = dot_nn(final_ref[...], table_ref[...])
-    hit = iota(logits.shape, 1) == goal_ref[...]
-    chance = jnp.exp(logits - to_rows(line_ref[0:1, :]))
-    grad = ((chance - jnp.where(hit, 1.0, 0.0)) * to_rows(line_ref[1:2, :])).astype(BF)
-    gfin_out[...] = dot_nt(grad, table_ref[...]).astype(BF)
-    part = dot_tn(final_ref[...], grad)
-
-    @pl.when(step == 0)
-    def _():
-        acc_ref[...] = part
-
-    @pl.when(step > 0)
-    def _():
-        acc_ref[...] += part
-
-    @pl.when(step == pl.num_programs(0) - 1)
-    def _():
-        gtab_out[...] = acc_ref[...].astype(BF)
-
-
-def head_back(table, final_all, goals, lines):
-    width, vocab = table.shape
-    count = final_all.shape[0]
-    tile = 256
-    return pl.pallas_call(
-        head_back_kernel,
-        grid=(count // tile,),
-        out_shape=[
-            jax.ShapeDtypeStruct((count, width), BF),
-            jax.ShapeDtypeStruct((width, vocab), BF),
+        **settings(18_000_000_000, 6_000_000, "head_forward"),
+    )
+
+
+def head_backward_kernel(
+    rows_ref, table_ref, goal_ref, line_ref, dy_out, gtab_out,
+    acc_scr, grad_scr, send_scr, core_scr, far_scr, low_scr, keep_scr,
+    core_send, core_recv, far_send, far_recv, low_send, low_recv
+):
+    rows = rows_ref.shape[1]
+
+    def to_core(place):
+        return remote(
+            send_scr.at[place + 4], core_scr.at[place], core_send.at[place], core_recv.at[place], *HEADS[0]
+        )
+
+    def to_far(place):
+        return remote(
+            send_scr.at[place + 2], far_scr.at[place], far_send.at[place], far_recv.at[place], *HEADS[1]
+        )
+
+    to_low = remote(send_scr.at[1], low_scr, low_send, low_recv, "dp", 1)
+
+    def pair(at, _):
+        base = 6 - 4 * (at % 2) - 2 * (at // 2)
+        for q in range(2):
+            place = base + q + (at // 3) * (1 - 2 * q)
+            logits = dot_nn(rows_ref[place], table_ref[...])
+            hit = iota(logits.shape, 1).astype(F32) == to_rows(goal_ref[place])
+            line = line_ref[place]
+            chance = jnp.exp(logits - to_rows(line[0:1]))
+            grad = ((chance - jnp.where(hit, 1.0, 0.0)) * to_rows(line[1:2])).astype(BF)
+            grad_scr[q * rows:(q + 1) * rows, :] = grad
+            part = dot_nt(grad, table_ref[...])
+
+            @pl.when((at == 0) | (at == 2))
+            def _():
+                send_scr[place] = part.astype(BF)
+                to_core(place - 4).start()
+
+            @pl.when(at == 1)
+            def _():
+                to_core(place).wait()
+                send_scr[place] = (part + core_scr[place].astype(F32)).astype(BF)
+                to_far(place - 2).start()
+
+            @pl.when(at == 3)
+            def _():
+                to_core(place).wait()
+                to_far(place).wait()
+                whole = part + core_scr[place].astype(F32) + far_scr[place].astype(F32)
+                if q == 0:
+                    send_scr[1] = whole.astype(BF)
+                    to_low.start()
+                else:
+                    keep_scr[...] = whole
+
+        both = [rows_ref[base + q + (at // 3) * (1 - 2 * q)] for q in range(2)]
+        part = dot_tn(jnp.concatenate(both, 0), grad_scr[...])
+
+        @pl.when(at == 0)
+        def _():
+            acc_scr[...] = part
+
+        @pl.when(at > 0)
+        def _():
+            acc_scr[...] += part
+
+        return 0
+
+    lax.fori_loop(0, SLOTS // 2, pair, 0)
+    gtab_out[...] = acc_scr[...].astype(BF)
+    to_low.wait()
+    dy_out[...] = keep_scr[...] + low_scr[...].astype(F32)
+
+
+def head_backward(rows_all, table, goals, lines, ident):
+    _, rows, width = rows_all.shape
+    vocab = table.shape[1]
+    return call(
+        head_backward_kernel,
+        [shape((rows, width), F32), shape((width, vocab), BF)],
+        [VM] * 4,
+        [VM] * 2,
+        (rows_all, table, goals, lines),
+        ident=ident,
+        greet=GREET_SLOTS,
+        scratch_shapes=[
+            pltpu.VMEM((width, vocab), F32),
+            pltpu.VMEM((2 * rows, vocab), BF),
+            pltpu.VMEM((SLOTS, rows, width), BF),
+            pltpu.VMEM((4, rows, width), BF),
+            pltpu.VMEM((2, rows, width), BF),
+            pltpu.VMEM((rows, width), BF),
+            pltpu.VMEM((rows, width), F32),
+            pltpu.SemaphoreType.DMA((4,)),
+            pltpu.SemaphoreType.DMA((4,)),
+            pltpu.SemaphoreType.DMA((2,)),
+            pltpu.SemaphoreType.DMA((2,)),
+            pltpu.SemaphoreType.DMA,
+            pltpu.SemaphoreType.DMA,
         ],
-        in_specs=[
-            pl.BlockSpec((width, vocab), lambda i: (0, 0)),
-            pl.BlockSpec((tile, width), lambda i: (i, 0)),
-            pl.BlockSpec((tile, 1), lambda i: (i, 0)),
-            pl.BlockSpec((2, tile), lambda i: (0, i)),
-        ],
-        out_specs=[
-            pl.BlockSpec((tile, width), lambda i: (i, 0)),
-            pl.BlockSpec((width, vocab), lambda i: (0, 0)),
-        ],
-        scratch_shapes=[pltpu.VMEM((width, vocab), F32)],
-        compiler_params=pltpu.CompilerParams(vmem_limit_bytes=VMEM_LIMIT),
-        cost_estimate=pl.CostEstimate(flops=35_000_000_000, bytes_accessed=14_000_000, transcendentals=0),
-        name="head_back",
-    )(table, final_all, goals, lines)
+        **settings(36_000_000_000, 14_000_000, "head_backward"),
+    )
 
 
 def swap(value, axis, bit):
@@ -957,12 +1421,6 @@
 def pieces_of_head(value):
     across = swap(value, "head", 2)
     return value, swap(value, "head", 1), across, swap(across, "head", 1)
-
-
-def settle_head(keep, send):
-    near = swap(send, "head", 1)
-    across = (keep[1].astype(F32) + near[1].astype(F32)).astype(BF)
-    return keep, near, swap(across, "head", 2)
 
 
 def pack_weights(attn_in, attn_out, ffn_up, ffn_down):
@@ -984,25 +1442,6 @@
 
 def depth_of(features):
     return max(64, features)
-
-
-def unpack_grads(packed, sort_width):
-    def cut(at, size=HD):
-        return packed[:, at:at + size]
-
-    kv = C_KVS[0]
-    srt = kv + 256
-    first = jnp.concatenate([cut(0), cut(kv), cut(kv + 64), cut(srt, sort_width)], 1)
-    second = jnp.concatenate(
-        [cut(64), cut(kv + 192), cut(kv + 128), cut(srt + sort_width, sort_width)], 1
-    )
-    out = packed[:, C_OUT[0]:C_OUT[1]].T
-    return (
-        jnp.stack([first, second], 1),
-        jnp.stack([out[HD:], out[:HD]], 0),
-        packed[:, ATTN + C_UP[0]:ATTN + C_UP[1]],
-        packed[:, ATTN + C_DOWN[0]:ATTN + C_DOWN[1]].T,
-    )
 
 
 class Gather:
@@ -1089,13 +1528,13 @@
     width = features * dp
     layers = attn_in.shape[0]
     rows = length // head
-    total = dp * length
+    total_tokens = dp * length
     odd = my_dp & 1
     outer = [[at for at in range(dp) if at % 2 == way] for way in range(2)]
 
     lines = jnp.concatenate([tokens, targets, jnp.broadcast_to(lengths[:, None], (seq_count, 128))], 1)
     lines = gather_dp(lines.reshape(-1))
-    all_tokens = lines[:, :length].reshape(1, total)
+    all_tokens = lines[:, :length].reshape(1, total_tokens)
     positions = jnp.arange(length, dtype=jnp.int32)
     counted = (positions[None, :] < lines[:, 2 * length:2 * length + 1]).astype(F32)
     nrm = norms
@@ -1151,11 +1590,6 @@
         if at + 1 < layers:
             hidden = pieces_of_head(hidden)
 
-    def spread_rows(value):
-        for axis, bit in (("dp", 1), ("head", 2), ("head", 1)):
-            value = jnp.stack([value, swap(value, axis, bit)])
-        return value
-
     def line_of(values):
         values = values.reshape(dp, head, rows)
         order = [(my_dp ^ y, my_head ^ (x * 2 + c)) for c in range(2) for x in range(2) for y in range(2)]
@@ -1164,29 +1598,15 @@
         ]
         return jnp.concatenate(picked)
 
-    final_all = spread_rows(hidden).reshape(-1, width)
     goals = line_of(lines[:, length:2 * length]) - (my_head * vocab + odd * half).astype(jnp.int32)
-    goals = goals.reshape(-1, 1)
-    counted_here = line_of(counted)
-    stats = head_stats(head_table, final_all, goals)
-    for dim, (axis, bit) in enumerate((("head", 1), ("head", 2), ("dp", 1))):
-        theirs = swap(stats, axis, bit).reshape(3, 2, 2, 2, rows)
-        theirs = jnp.flip(theirs, dim + 1).reshape(stats.shape)
-        peak = jnp.maximum(stats[0], theirs[0])
-        sums = stats[1] * jnp.exp(stats[0] - peak) + theirs[1] * jnp.exp(theirs[0] - peak)
-        stats = jnp.stack([peak, sums, stats[2] + theirs[2]])
-    lse = stats[0] + jnp.log(stats[1])
-    loss_here = jnp.sum((lse - stats[2]) * counted_here) / (2 * head)
+    goals = goals.astype(F32).reshape(SLOTS, 1, rows)
+    idents = iter(range(1, 64))
+    rows_all, stat_lines, loss_here, token = head_forward(
+        hidden, head_table, goals, line_of(counted).reshape(SLOTS, 1, rows), next(idents)
+    )
+    loss_here = loss_here / (2 * head)
     count_total = jnp.sum(counted)
-    grad_final, grad_half = head_back(head_table, final_all, goals, jnp.stack([lse, counted_here]))
-    grad_final = grad_final.reshape(2, 2, 2, rows, width)
-    near = swap(grad_final[1], "head", 1)
-    summed = grad_final[0].astype(F32) + near.astype(F32)
-    across = swap(summed[1].astype(BF), "head", 2)
-    summed = summed[0] + across.astype(F32)
-    far = swap(summed[1].astype(BF), "dp", 1)
-    nothing = jnp.zeros((1, rows, width), BF)
-    dy = (summed[0:1], nothing, far)
+    dy, grad_half, token = head_backward(rows_all, head_table, goals, stat_lines, next(idents))
     grad_half = lax.psum_scatter(
         grad_half, "dp", scatter_dimension=0, tiled=True, axis_index_groups=outer
     ).reshape(2, features, half)
@@ -1197,103 +1617,96 @@
     bits = bits_of("dp")
 
     def shaped(value):
-        return value.reshape((2,) + (2,) * len(bits) + (features, value.shape[-1]))
-
-    def attn_steps(keep, send):
-        keep, near = shaped(keep), shaped((yield send, "head", 1))
-        across = yield add_up(keep[1], near[1]).astype(BF), "head", 2
-        here, there = split(add_up(keep[0], near[0], across), "dp", bits[-1], len(bits) - 1)
-        return add_up(here, (yield there, "dp", bits[-1]))
-
-    def feed_steps(keep, send):
-        keep, near = shaped(keep), shaped((yield send, "head", 1))
-        here, there = split(add_up(keep, near), "dp", bits[-1], len(bits))
+        return value.reshape((2,) * len(bits) + (features, value.shape[-1]))
+
+    def attn_steps(mine, theirs):
+        across = yield theirs, "head", 2
+        here, there = split(shaped(add_up(mine, across)), "dp", bits[-1], len(bits) - 1)
+        return here, (yield there, "dp", bits[-1])
+
+    def feed_steps(here, there):
         value = add_up(here, (yield there, "dp", bits[-1]))
-        return add_up(value[0], (yield value[1].astype(BF), "head", 2))
+        parts = value[0], (yield value[1].astype(BF), "head", 2)
+        return tuple(part.reshape((2,) * (len(bits) - 1) + part.shape[-2:]) for part in parts)
 
     def last_steps(attn, feed):
-        value = jnp.concatenate([attn.value, feed.value], -1)
+        value = jnp.concatenate([add_up(*attn.parts), add_up(*feed.parts)], -1)
         for dim, bit in reversed(list(enumerate(bits[:-1]))):
             here, there = split(value, "dp", bit, dim)
-            value = add_up(here, (yield there, "dp", bit))
-        return value
+            parts = here, (yield there, "dp", bit)
+            value = add_up(*parts)
+        return parts
 
     attns, feeds, lasts = [None] * layers, [None] * layers, [None] * layers
 
     def active(*candidates):
         return [flow for flow in candidates if flow is not None and flow.ask is not None]
 
-    idents = iter(range(1, 64))
     for at in reversed(range(layers)):
         of = max(at - 1, 0)
         stream_in, for_feed, for_attend = kept[at]
         above_attn, above_feed = (attns + [None])[at + 1], (feeds + [None])[at + 1]
         top_attn, top_feed = (attns + [None] * 2)[at + 2], (feeds + [None] * 2)[at + 2]
-        fkeep, fsend, carry, pair_above, pair_two, token = feed_backward(
+        here, there, carry, pair_above, pair_two, token = feed_backward(
             of, dy, above, carry, nrm[2 * at + 2, 0:1], sources[at][1], nrm[2 * at + 1, 0:1], for_feed,
-            [grad_half] if at == 0 else [], active(above_attn, top_attn, top_feed), next(idents),
+            features, [grad_half] if at == 0 else [], active(top_attn, above_attn if at == 0 else None), next(idents),
         )
-        feeds[at] = Flow(feed_steps(fkeep, fsend))
+        feeds[at] = Flow(feed_steps(here, there))
         if at + 2 < layers:
             lasts[at + 2] = Flow(last_steps(top_attn, top_feed))
-        gkeep, gsend, akeep, asend, token = attend_backward(
+        dy, *attn_sums, token = attend_backward(
             of, carry, sources[at][0], for_attend, [],
             active(feeds[at], above_attn, above_feed, *lasts), next(idents),
         )
-        attns[at] = Flow(attn_steps(akeep, asend))
-        dy = settle_head(gkeep, gsend)
+        attns[at] = Flow(attn_steps(*attn_sums))
         pair_grads[2 * at + 2] = pair_above
         pair_grads[2 * at + 1] = pair_two
         above = stream_in
-    grad_stream, pair_grads[0], token = finish_stream(
-        dy, above, carry, nrm[0, 0:1], [], active(attns[0]), next(idents)
-    )
-
-    spread = lax.all_to_all(
-        grad_stream.reshape(dp, features, rows), "dp", split_axis=0, concat_axis=0, tiled=True
-    )
-    for flow in active(attns[0], feeds[0], attns[1], feeds[1], *lasts):
-        flow.give(swap(*flow.ask))
+    def once(value, axis, bit):
+        return (yield value, axis, bit)
+
+    grad_half = Flow(once(lax.dynamic_index_in_dim(grad_half, 1 - odd, 0, False), "dp", 1)), (
+        lax.dynamic_index_in_dim(grad_half, odd, 0, False)
+    )
     lasts[1] = Flow(last_steps(attns[1], feeds[1]))
-    other = swap(lax.dynamic_index_in_dim(grad_half, 1 - odd, 0, False), "dp", 1)
-    mine = lax.dynamic_index_in_dim(grad_half, odd, 0, False)
-    spread = in_order(spread[:, None], swap(spread[:, None], "head", 1), "head", 1, 1)[:, None]
-    spread = in_order(spread, swap(spread, "head", 2), "head", 2, 1)
-    spread = spread.reshape(dp * head, features, rows)
-    found, token = embed_back(
-        base, all_tokens, spread, vocab, [other], active(attns[0], feeds[0], *lasts), next(idents)
-    )
-    lasts[0] = Flow(last_steps(attns[0], feeds[0]))
-    grad_table = in_order(mine, other, "dp", 1, 1).astype(F32) + math.sqrt(width) * found
-    packed_grads = [flow.finish() for flow in lasts]
-
-    grad_norms = sum_all(jnp.stack(pair_grads))
-    grad_norms = lax.dynamic_slice_in_dim(grad_norms, my_head * norms.shape[2], norms.shape[2], 2)
+    pair_grads[0], spread, token = finish_stream(
+        dy, above, carry, nrm[0, 0:1], [], active(attns[0], grad_half[0], *lasts), next(idents)
+    )
+
+    head_grad = in_order(grad_half[1], grad_half[0].value, "dp", 1, 1)
+    spread = spread.reshape(head * dp, features, rows)
+    by_rows = all_tokens.reshape(dp, head, rows)
+    order = [lax.dynamic_index_in_dim(by_rows, my_head ^ p, 1, False) for p in range(head)]
+    grad_table, squares, grad_norms, token = embed_back(
+        base, jnp.stack(order).reshape(1, total_tokens), spread, head_grad,
+        pair_grads, [],
+        active(attns[0], feeds[0], *lasts), next(idents),
+    )
     sort_width = attn_in.shape[3] - 3 * HD
-    layer_grads = [unpack_grads(packed, sort_width) for packed in packed_grads]
-    grad_in, grad_out, grad_up, grad_down = (
-        jnp.stack([one[member] for one in layer_grads]) for member in range(4)
-    )
-    squares = jnp.sum(grad_table * grad_table) + jnp.sum(grad_norms * grad_norms) / dp
-    for packed in packed_grads:
-        squares = squares + jnp.sum(packed * packed)
-    totals = sum_all(jnp.stack([squares, loss_here]))
-    grad_norm = jnp.sqrt(totals[0])
-    loss_total = totals[1]
-    factor = jnp.minimum(1.0, CLIP_LIMIT / (grad_norm + 1e-06))
-
-    results = [jnp.stack([loss_total, count_total]), grad_norm]
-    for weight, gradient, first, second in (
-        (table, grad_table, table_first, table_second),
-        (attn_in, grad_in, attn_in_first, attn_in_second),
-        (attn_out, grad_out, attn_out_first, attn_out_second),
-        (ffn_up, grad_up, ffn_up_first, ffn_up_second),
-        (ffn_down, grad_down, ffn_down_first, ffn_down_second),
-    ):
-        new, one, two = adamw(weight, gradient, first, second, factor, RATE_MATRIX)
-        results += [new, new.astype(BF), one, two]
-    results += list(adamw(norms, grad_norms, norms_first, norms_second, factor, RATE_NORM))
-    return tuple(results)
+    thirds = [flow.finish() for flow in lasts[2:]]
+    while lasts[1].ask is not None:
+        lasts[1].give(swap(*lasts[1].ask))
+    lower, other, totals, token = last_sums(
+        attns[0].parts, feeds[0].parts, lasts[1].parts, thirds, squares, grad_norms, loss_here.reshape(1, 1),
+        tuple(reversed(bits[:-1])), next(idents),
+    )
+    grad_norms = lax.dynamic_slice_in_dim(
+        grad_norms, my_head * norms.shape[2], norms.shape[2], 2
+    )
+    results = update(
+        totals, [lower, other] + thirds, grad_table, grad_norms, sort_width,
+        [
+            (table, table_first, table_second),
+            (attn_in, attn_in_first, attn_in_second),
+            (attn_out, attn_out_first, attn_out_second),
+            (ffn_up, ffn_up_first, ffn_up_second),
+            [one.transpose(0, 2, 1) for one in (ffn_down, ffn_down_first, ffn_down_second)],
+            (norms, norms_first, norms_second),
+        ],
+    )
+    results = list(results)
+    results[16:20] = [one.transpose(0, 2, 1) for one in results[16:20]]
+    return (jnp.stack([totals[0, 1], count_total]), jnp.sqrt(totals[0, 0]), *results)
 
 
 def solution(mesh):

time: 769 us -> 661 us (0.86)
  waiting for transfers between devices: 188 us -> 68.7 us
  Pallas kernels: 363 us -> 474 us
  other arithmetic: 74 us -> 33.5 us
  starting transfers between devices: 64.6 us -> 25 us
  local copies, waits for them, and re-layouts: 47.8 us -> 32.7 us
    pallas_call x16 -> x20, Pallas kernels: 303 us -> 474 us  [call(): pl.pallas_call(run, out_shape=list(outs) + [jax.ShapeDtypeStruct((1, 128)...]
    ppermute x62 -> x26, waiting for transfers between devices: 187 us -> 68.6 us  [swap(): lax.ppermute(value, axis, [(at, at ^ bit) for at in range(lax.axis_size(a...]
    pallas_call x2 -> x0, Pallas kernels: 59.9 us -> none  [the longest x1 39.5 us: head_back(): pl.pallas_call(head_back_kernel, grid=(count // tile,), out_shape=[jax.Sh...]
    ppermute x62 -> x26, starting transfers between devices: 54.3 us -> 19.7 us  [swap(): lax.ppermute(value, axis, [(at, at ^ bit) for at in range(lax.axis_size(a...]
    unnamed x212 -> x112, local copies, waits for them, and re-layouts: 23.2 us -> 10.9 us
    convert_element_type x9 -> x1, other arithmetic: 12.3 us -> 0.67 us  [body(): goals = goals.astype(F32).reshape(SLOTS, 1, rows)]
    another operation x31 -> x10, other arithmetic: 13.6 us -> 4.08 us
  transfers between devices with their start and end apart: 67 -> 30, of which waited for: 41 -> 15; matrix products, arithmetic and copies ran while one was open for 10% -> 6% of each run, Pallas kernels for 28% -> 33%
where the time goes in v3:
time: 661 us; the launch traced here: 652 us
  Pallas kernels  474 us (72%)
  waiting for transfers between devices  68.7 us (10%)
  other arithmetic  33.5 us (5%)
  local copies, waits for them, and re-layouts  32.7 us (5%)
  starting transfers between devices  25 us (4%)
  between operations  18.4 us (3%)
    pallas_call x20, Pallas kernels, call(): pl.pallas_call(run, out_shape=list(outs) + [jax.ShapeDtypeStruct((1, 128)...  474 us
    ppermute x26, waiting for transfers between devices, swap(): lax.ppermute(value, axis, [(at, at ^ bit) for at in range(lax.axis_size(a...  68.6 us
    ppermute x26, starting transfers between devices, swap(): lax.ppermute(value, axis, [(at, at ^ bit) for at in range(lax.axis_size(a...  19.7 us
  transfers between devices with their start and end apart: 30, of which 15 were waited for; matrix products, arithmetic and copies ran while one was open for 6% of the time, Pallas kernels for 33%

profile of v3, /device:TPU:0, one launch (start us, length us, event | category | flops | bytes accessed | tf_op | source)
XLA Modules:
  0.0 652.0 jit_solution(12011068595897860832)
XLA Ops:
  8.7 4.1 collective-permute-start
  16.9 1.9 collective-permute-start.1
  18.9 2.8 collective-permute-done.1
  25.8 3.1 collective-permute-done.3
  30.6 9.3 %collective-permute-done.4 = bf16[2,1,1,64,1664]{4,3,2,1,0:T(8,128)(2,1)S(1)} collective-permute-done((bf16[2,1,1,64,1664]{4,3,2,1,0:T(8,128)(2,1)S(1)}, bf16[2,1,1,64,1664]{4,3,2,1,0:T(8,128)(2,1)S(1)}, u32[]{:S(2)}, u32[]{:S(2)}) %collective-permute-start.4) | collective-permute-done | bytes 426016 | tf_op jit(solution)/shard_map/ppermute | solution.py:1369
  40.9 13.9 %embed_lookup.1 = (bf16[64,8192]{1,0:T(8,128)(2,1)}, f32[1,128]{1,0:T(1,128)}) custom-call(s32[1]{0:T(128)} %bitcast.refs_0_, s32[1,8192]{1,0:T(1,128)} %bitcast.266, bf16[64,8192]{1,0:T(8,128)(2,1)} %convert_element_type.212.refs_2_, bf16[2,2,1,64,1664]{4,3,2,1,0:T(8,128)(2,1)} %pad_maximum_fusion.refs_3_), custom_call_target="tpu_custom_call" | custom-call | flops 15000000512 | bytes 4000000 | tf_op jit(solution)/shard_map/embed_lookup/pallas_call | solution.py:152
  65.2 2.7 constant_dynamic-slice_fusion.26
  73.6 5.4 collective-permute-done.14
  85.0 4.7 all-to-all-start
  90.8 17.9 %collective-permute-done.15 = bf16[2,2,1,64,640]{4,3,2,1,0:T(8,128)(2,1)} collective-permute-done((bf16[2,2,1,64,640]{4,3,2,1,0:T(8,128)(2,1)}, bf16[2,2,1,64,640]{4,3,2,1,0:T(8,128)(2,1)}, u32[]{:S(2)}, u32[]{:S(2)}) %collective-permute-start.15) | collective-permute-done | bytes 327712 | tf_op jit(solution)/shard_map/ppermute | solution.py:1369
  111.6 2.0 start_stream.1
  116.7 7.7 %collective-permute-done.10.refs_2_ = bf16[256,512]{1,0:T(8,128)(2,1)S(1)} collective-permute-done((bf16[256,512]{1,0:T(8,128)(2,1)}, bf16[256,512]{1,0:T(8,128)(2,1)S(1)}, u32[]{:S(2)}, u32[]{:S(2)}) %collective-permute-start.10) | collective-permute-done | bytes 262176 | tf_op jit(solution)/shard_map/ppermute | solution.py:1369
  127.5 44.7 %attend_forward.3 = (f32[256,512]{1,0:T(8,128)}, bf16[256,512]{1,0:T(8,128)(2,1)}, bf16[1024,512]{1,0:T(8,128)(2,1)}, bf16[4,1024,256]{2,1,0:T(8,128)(2,1)}, bf1...) custom-call(bf16[256,512]{1,0:T(8,128)(2,1)} %get-tuple-element.152., ...), custom_call_target="tpu_custom_call" | custom-call | flops 17999998976 | bytes 10000000 | tf_op jit(solution)/shard_map/attend_forward/pallas_call | solution.py:152
  177.0 7.6 %feed_forward.3 = (f32[256,512]{1,0:T(8,128)}, bf16[256,512]{1,0:T(8,128)(2,1)}, f32[4,256,512]{2,1,0:T(8,128)}, bf16[4,256,512]{2,1,0:T(8,128)(2,1)}, f32[1,128]{1,0:T(1,128)}) custom-call(f32[256,512]{1,0:T(8,128)} %get-tuple-element.155.refs_0_.refs_5_, bf16[256,512]{1,0:T(8,128)(2,1)} %get-tuple-element.156.refs_1_.refs_6_, ...), custom_call_target="tpu_custom_call" | custom-call | flops 8000000000 | bytes 8000000 | tf_op jit(solution)/shard_map/feed_forward/pallas_call | solution.py:152
  187.0 6.1 collective-permute-done.20.refs_2_
  195.3 23.5 %attend_forward.4 = (f32[256,512]{1,0:T(8,128)}, bf16[256,512]{1,0:T(8,128)(2,1)}, bf16[1024,512]{1,0:T(8,128)(2,1)}, bf16[4,1024,256]{2,1,0:T(8,128)(2,1)}, bf1...) custom-call(bf16[256,512]{1,0:T(8,128)(2,1)} %get-tuple-element.159., ...), custom_call_target="tpu_custom_call" | custom-call | flops 17999998976 | bytes 10000000 | tf_op jit(solution)/shard_map/attend_forward/pallas_call | solution.py:152
  218.8 7.4 %feed_forward.4 = (f32[256,512]{1,0:T(8,128)}, bf16[256,512]{1,0:T(8,128)(2,1)}, f32[4,256,512]{2,1,0:T(8,128)}, bf16[4,256,512]{2,1,0:T(8,128)(2,1)}, f32[1,128]{1,0:T(1,128)}) custom-call(f32[256,512]{1,0:T(8,128)} %get-tuple-element.161.refs_0_.refs_5_, bf16[256,512]{1,0:T(8,128)(2,1)} %get-tuple-element.162.refs_1_.refs_6_, ...), custom_call_target="tpu_custom_call" | custom-call | flops 8000000000 | bytes 8000000 | tf_op jit(solution)/shard_map/feed_forward/pallas_call | solution.py:152
  227.4 7.4 %collective-permute-done.23.refs_2_ = bf16[256,512]{1,0:T(8,128)(2,1)S(1)} collective-permute-done((bf16[256,512]{1,0:T(8,128)(2,1)}, bf16[256,512]{1,0:T(8,128)(2,1)S(1)}, u32[]{:S(2)}, u32[]{:S(2)}) %collective-permute-start.23) | collective-permute-done | bytes 262176 | tf_op jit(solution)/shard_map/ppermute | solution.py:1369
  237.1 23.5 %attend_forward.5 = (f32[256,512]{1,0:T(8,128)}, bf16[256,512]{1,0:T(8,128)(2,1)}, bf16[1024,512]{1,0:T(8,128)(2,1)}, bf16[4,1024,256]{2,1,0:T(8,128)(2,1)}, bf1...) custom-call(bf16[256,512]{1,0:T(8,128)(2,1)} %get-tuple-element.163., ...), custom_call_target="tpu_custom_call" | custom-call | flops 17999998976 | bytes 10000000 | tf_op jit(solution)/shard_map/attend_forward/pallas_call | solution.py:152
  260.6 7.5 %feed_forward.5 = (f32[256,512]{1,0:T(8,128)}, bf16[256,512]{1,0:T(8,128)(2,1)}, f32[4,256,512]{2,1,0:T(8,128)}, bf16[4,256,512]{2,1,0:T(8,128)(2,1)}, f32[1,128]{1,0:T(1,128)}) custom-call(f32[256,512]{1,0:T(8,128)} %get-tuple-element.165.refs_0_.refs_5_, bf16[256,512]{1,0:T(8,128)(2,1)} %get-tuple-element.166.refs_1_.refs_6_, ...), custom_call_target="tpu_custom_call" | custom-call | flops 8000000000 | bytes 8000000 | tf_op jit(solution)/shard_map/feed_forward/pallas_call | solution.py:152
  268.2 36.1 %head_forward.1 = (bf16[8,256,512]{2,1,0:T(8,128)(2,1)}, f32[8,2,256]{2,1,0:T(2,128)}, f32[1,1]{1,0:T(1,128)}, f32[1,128]{1,0:T(1,128)}) custom-call(bf16[256,512]{1,0:T(8,128)(2,1)} %get-tuple-element.167.refs_0_, bf16[512,4096]{1,0:T(8,128)(2,1)} %all-gather.5.cloned.1.call-done.refs_1_, f32[8,1,256]{2,1,0:T(1,128)} %subtract_convert_fusion.refs_2_, ...), custom_call_target="tpu_custom_call" | custom-call | flops 17999998976 | bytes 6000000 | tf_op jit(solution)/shard_map/head_forward/pallas_call | solution.py:152
  304.3 40.5 %head_backward.1 = (f32[256,512]{1,0:T(8,128)}, bf16[512,4096]{1,0:T(8,128)(2,1)}, f32[1,128]{1,0:T(1,128)}) custom-call(bf16[8,256,512]{2,1,0:T(8,128)(2,1)} %get-tuple-element.169.refs_0_, bf16[512,4096]{1,0:T(8,128)(2,1)} %all-gather.5.cloned.1.call-done.refs_1_, f32[8,1,256]{2,1,0:T(1,128)} %subtract_convert_fusion.refs_2_, ...), custom_call_target="tpu_custom_call" | custom-call | flops 35999997952 | bytes 14000000 | tf_op jit(solution)/shard_map/head_backward/pallas_call | solution.py:152
  348.3 12.4 %feed_backward.3 = (bf16[2,4,64,1024]{3,2,1,0:T(8,128)(2,1)}, bf16[2,4,64,1024]{3,2,1,0:T(8,128)(2,1)}, f32[256,512]{1,0:T(8,128)}, f32[2,512]{1,0:T(2,128)}, f32[2,512]{1,0:T(2,128)}, /*index=5*/f32[1,128]{1,0:T(1,128)}) custom-call(f32[256,512]{1,0:T(8,128)} %get-tuple-element.171.refs_0_, f32[256,512]{1,0:T(8,128)} %get-tuple-element.172.refs_1_, ...), custom_call_target="tpu_custom_call" | custom-call | flops 12000000000 | bytes 12000000 | tf_op jit(solution)/shard_map/feed_backward/pallas_call | solution.py:152
  360.8 36.9 %attend_backward.3 = (f32[256,512]{1,0:T(8,128)}, bf16[8,64,640]{2,1,0:T(8,128)(2,1)}, bf16[8,64,640]{2,1,0:T(8,128)(2,1)}, f32[1,128]{1,0:T(1,128)}, bf16[2,4,64,1024]{3,2,1,0:T(8,128)(2,1)}) custom-call(f32[256,512]{1,0:T(8,128)} %get-tuple-element.175.refs_0_.refs_2_, bf16[1024,512]{1,0:T(8,128)(2,1)} %get-tuple-element.176.refs_1_, ...), custom_call_target="tpu_custom_call" | custom-call | flops 20000000000 | bytes 16000000 | tf_op jit(solution)/shard_map/attend_backward/pallas_call | solution.py:152
  400.3 11.7 %feed_backward.4 = (bf16[2,4,64,1024]{3,2,1,0:T(8,128)(2,1)}, bf16[2,4,64,1024]{3,2,1,0:T(8,128)(2,1)}, f32[256,512]{1,0:T(8,128)}, f32[2,512]{1,0:T(2,128)}, f32[2,512]{1,0:T(2,128)}, /*index=5*/f32[1,128]{1,0:T(1,128)}) custom-call(f32[256,512]{1,0:T(8,128)} %get-tuple-element.185.refs_0_, f32[256,512]{1,0:T(8,128)} %get-tuple-element.164.refs_4_.refs_1_, ...), custom_call_target="tpu_custom_call" | custom-call | flops 12000000000 | bytes 12000000 | tf_op jit(solution)/shard_map/feed_backward/pallas_call | solution.py:152
  412.0 38.2 %attend_backward.4 = (f32[256,512]{1,0:T(8,128)}, bf16[8,64,640]{2,1,0:T(8,128)(2,1)}, bf16[8,64,640]{2,1,0:T(8,128)(2,1)}, f32[1,128]{1,0:T(1,128)}, bf16[2,4,6...) custom-call(f32[256,512]{1,0:T(8,128)} %get-tuple-element.188.refs_0_.refs_2_, ...), custom_call_target="tpu_custom_call" | custom-call | flops 20000000000 | bytes 16000000 | tf_op jit(solution)/shard_map/attend_backward/pallas_call | solution.py:152
  455.9 20.5 %feed_backward.5 = (bf16[2,4,64,1024]{3,2,1,0:T(8,128)(2,1)}, bf16[2,4,64,1024]{3,2,1,0:T(8,128)(2,1)}, f32[256,512]{1,0:T(8,128)}, f32[2,512]{1,0:T(2,128)}, f3...) custom-call(f32[256,512]{1,0:T(8,128)} %get-tuple-element.201.refs_0_, ...), custom_call_target="tpu_custom_call" | custom-call | flops 12000000000 | bytes 12000000 | tf_op jit(solution)/shard_map/feed_backward/pallas_call | solution.py:152
  479.4 37.1 %attend_backward.5 = (f32[256,512]{1,0:T(8,128)}, bf16[8,64,640]{2,1,0:T(8,128)(2,1)}, bf16[8,64,640]{2,1,0:T(8,128)(2,1)}, f32[1,128]{1,0:T(1,128)}, bf16[2,4,6...) custom-call(f32[256,512]{1,0:T(8,128)} %get-tuple-element.208.refs_0, ...), custom_call_target="tpu_custom_call" | custom-call | flops 20000000000 | bytes 16000000 | tf_op jit(solution)/shard_map/attend_backward/pallas_call | solution.py:152
  522.9 28.6 %finish_stream.1 = (f32[2,512]{1,0:T(2,128)}, bf16[4,8,64,256]{3,2,1,0:T(8,128)(2,1)}, f32[1,128]{1,0:T(1,128)}, bf16[8,64,640]{2,1,0:T(8,128)(2,1)}, bf16[64,40...) custom-call(f32[256,512]{1,0:T(8,128)} %get-tuple-element.225.refs_0_, ...), custom_call_target="tpu_custom_call" | custom-call | tf_op jit(solution)/shard_map/finish_stream/pallas_call | solution.py:152
  557.4 31.5 %embed_back.1 = (f32[64,8192]{1,0:T(8,128)}, f32[64,256]{1,0:T(8,128)}, f32[7,2,512]{2,1,0:T(2,128)}, f32[1,128]{1,0:T(1,128)}, bf16[2,2,64,640]{3,2,1,0:T(8,128...) custom-call(s32[1]{0:T(128)} %bitcast.refs_0_, s32[1,8192]{1,0:T(1,128)} %reshape.343.refs_1_, ...), custom_call_target="tpu_custom_call" | custom-call | flops 15000000512 | bytes 4000000 | tf_op jit(solution)/shard_map/embed_back/pallas_call | solution.py:152
  590.2 36.4 %last_sums.1 = (f32[64,1664]{1,0:T(8,128)}, f32[64,1664]{1,0:T(8,128)}, f32[8,128]{1,0:T(8,128)}, f32[1,128]{1,0:T(1,128)}) custom-call(bf16[4,64,640]{2,1,0:T(8,128)(2,1)} %bitcast.246, bf16[4,64,640]{2,1,0:T(8,128)(2,1)} %bitcast.261, f32[4,64,1024]{2,1,0:T(8,128)} %slice_bitcast_fusion.refs_2_, bf16[4,64,1024]{2,1,0:T(8,128)(2,1)} %get-tuple-element.244.refs_3_, ...), custom_call_target="tpu_custom_call" | custom-call | flops 1000000 | bytes 4000000 | tf_op jit(solution)/shard_map/last_sums/pallas_call | solution.py:152
  630.5 13.7 %update.1 = (f32[64,8192]{1,0:T(8,128)}, bf16[64,8192]{1,0:T(8,128)(2,1)}, f32[64,8192]{1,0:T(8,128)}, f32[64,8192]{1,0:T(8,128)}, f32[3,64,2,224]{3,2,1,0:T(2,1...) custom-call(f32[8,128]{1,0:T(8,128)} %get-tuple-element.250.refs_0_,, ...), custom_call_target="tpu_custom_call" | custom-call | flops 1000000 | bytes 30000000 | tf_op jit(solution)/shard_map/update/pallas_call | solution.py:152
  (274 shorter events, 86.7 us)
Async XLA Ops:
  7.2 187.4 %all-gather.3.cloned.1.call-start = ((), (), s32[]{:S(2)}) async-start(), calls=%async_computation.2 | async-start | bytes 14057472 | tf_op jit(solution)/shard_map/all_gather | solution.py:1495
  8.7 8.1 %collective-permute-start = (s32[1,1,1,2176]{3,2,1,0:T(1,128)S(1)}, s32[1,1,1,2176]{3,2,1,0:T(1,128)S(1)}, u32[]{:S(2)}, u32[]{:S(2)}) collective-permute-start(s32[1,1,1,2176]{3,2,1,0:T(1,128)S(1)} %fusion.20), channel_id=1, source_target_pairs={{0,16},{4,20},{8,24},{12,28},{16,0},{20,4},{24,8},{28,12},{1,17},{... | collective-permute-start | bytes 26120 | tf_op jit(solution)/shard_map/ppermute | solution.py:1369
  16.7 12.2 %collective-permute-start.3 = (bf16[1,1,1,64,1664]{4,3,2,1,0:T(8,128)(2,1)S(1)}, bf16[1,1,1,64,1664]{4,3,2,1,0:T(8,128)(2,1)S(1)}, u32[]{:S(2)}, u32[]{:S(2)}) collective-permute-start(bf16[1,1,1,64,1664]{4,3,2,1,0:T(8,128)(2,1)S(1)} %bitcast.253), channel_id=1, source_target_pairs={{0,16},{4,20},{8,24},{12,28},{16,0},{20,4},{24,8},{28,12},{1,17},{... | collective-permute-start | bytes 638984 | tf_op jit(solution)/shard_map/ppermute | solution.py:1369
  16.9 4.9 collective-permute-start.1
  21.8 4.0 collective-permute-start.2
  29.1 10.7 %collective-permute-start.4 = (bf16[2,1,1,64,1664]{4,3,2,1,0:T(8,128)(2,1)S(1)}, bf16[2,1,1,64,1664]{4,3,2,1,0:T(8,128)(2,1)S(1)}, u32[]{:S(2)}, u32[]{:S(2)}) collective-permute-start(bf16[2,1,1,64,1664]{4,3,2,1,0:T(8,128)(2,1)S(1)} %pad_maximum_fusion.5), channel_id=1, source_target_pairs={{0,8},{4,12},{8,0},{12,4},{16,24},{20,28},{24,16},{28,20},{1,9},{5... | collective-permute-start | bytes 1277960 | tf_op jit(solution)/shard_map/ppermute | solution.py:1369
  56.3 2.5 collective-permute-start.7
  57.2 115.0 %collective-permute-start.25 = (bf16[64,4096]{1,0:T(8,128)(2,1)}, bf16[64,4096]{1,0:T(8,128)(2,1)}, u32[]{:S(2)}, u32[]{:S(2)}) collective-permute-start(bf16[64,4096]{1,0:T(8,128)(2,1)} %constant_dynamic-slice_fusion.24), channel_id=1, source_target_pairs={{0,4},{4,0},{8,12},{12,8},{16,20},{20,16},{24,28},{28,24},{1,5},{5... | collective-permute-start | bytes 1572872 | tf_op jit(solution)/shard_map/ppermute | solution.py:1369
  58.8 3.8 collective-permute-start.8
  68.1 4.7 collective-permute-start.5
  68.3 47.9 %copy-start.33 = (s32[8]{0:T(128)}, s32[8]{0:T(128)S(1)}, u32[]{:S(2)}) copy-start(s32[8]{0:T(128)S(1)} %slice_reduce_fusion) | copy-start | bytes 100
  68.4 10.6 %collective-permute-start.14 = (bf16[2,2,1,64,640]{4,3,2,1,0:T(8,128)(2,1)S(1)}, bf16[2,2,1,64,640]{4,3,2,1,0:T(8,128)(2,1)S(1)}, u32[]{:S(2)}, u32[]{:S(2)}) collective-permute-start(bf16[2,2,1,64,640]{4,3,2,1,0:T(8,128)(2,1)S(1)} %fusion.19), channel_id=1, source_target_pairs={{0,2},{1,3},{2,0},{3,1},{4,6},{5,7},{6,4},{7,5},{8,10},{9,11},{10,... | collective-permute-start | bytes 983048 | tf_op jit(solution)/shard_map/ppermute | solution.py:1369
  69.9 12.3 %collective-permute-start.12 = (bf16[2,2,1,64,640]{4,3,2,1,0:T(8,128)(2,1)S(1)}, bf16[2,2,1,64,640]{4,3,2,1,0:T(8,128)(2,1)S(1)}, u32[]{:S(2)}, u32[]{:S(2)}) collective-permute-start(bf16[2,2,1,64,640]{4,3,2,1,0:T(8,128)(2,1)S(1)} %fusion.19), channel_id=1, source_target_pairs={{0,4},{4,0},{8,12},{12,8},{16,20},{20,16},{24,28},{28,24},{1,5},{5... | collective-permute-start | bytes 983048 | tf_op jit(solution)/shard_map/ppermute | solution.py:1369
  71.3 45.1 %collective-permute-start.17 = (bf16[2,2,1,64,1024]{4,3,2,1,0:T(8,128)(2,1)}, bf16[2,2,1,64,1024]{4,3,2,1,0:T(8,128)(2,1)}, u32[]{:S(2)}, u32[]{:S(2)}) collective-permute-start(bf16[2,2,1,64,1024]{4,3,2,1,0:T(8,128)(2,1)} %fusion.9), channel_id=1, source_target_pairs={{0,4},{4,0},{8,12},{12,8},{16,20},{20,16},{24,28},{28,24},{1,5},{5... | collective-permute-start | bytes 1572872 | tf_op jit(solution)/shard_map/ppermute | solution.py:1369
  73.0 11.2 %collective-permute-start.6 = (bf16[64,8,256]{2,1,0:T(8,128)(2,1)S(1)}, bf16[64,8,256]{2,1,0:T(8,128)(2,1)S(1)}, u32[]{:S(2)}, u32[]{:S(2)}) collective-permute-start(bf16[64,8,256]{2,1,0:T(8,128)(2,1)S(1)} %dynamic-slice_bitcast_fusion.4), channel_id=1, source_target_pairs={{0,2},{1,3},{2,0},{3,1},{4,6},{5,7},{6,4},{7,5},{8,10},{9,11},{10,... | collective-permute-start | bytes 786440 | tf_op jit(solution)/shard_map/ppermute | solution.py:1369
  79.8 28.9 %collective-permute-start.15 = (bf16[2,2,1,64,640]{4,3,2,1,0:T(8,128)(2,1)}, bf16[2,2,1,64,640]{4,3,2,1,0:T(8,128)(2,1)}, u32[]{:S(2)}, u32[]{:S(2)}) collective-permute-start(bf16[2,2,1,64,640]{4,3,2,1,0:T(8,128)(2,1)} %broadcast_add_fusion), channel_id=1, source_target_pairs={{0,4},{4,0},{8,12},{12,8},{16,20},{20,16},{24,28},{28,24},{1,5},{5... | collective-permute-start | bytes 983048 | tf_op jit(solution)/shard_map/ppermute | solution.py:1369
  85.0 25.9 %all-to-all-start = ((bf16[64,8,256]{2,0,1:T(8,128)(2,1)}), bf16[64,8,256]{2,0,1:T(8,128)(2,1)S(1)}, u32[]{:S(2)}, u32[]{:S(2)}) async-start(bf16[64,8,256]{2,0,1:T(8,128)(2,1)} %copy.127), calls=%async_computation | async-start | bytes 524288 | tf_op jit(solution)/shard_map/all_to_all | solution.py:1567
  89.7 178.5 %all-gather.5.cloned.1.call-start = ((), (), s32[]{:S(2)}) async-start(), calls=%async_computation.3 | async-start | bytes 5242880 | tf_op jit(solution)/shard_map/all_gather | solution.py:1569
  90.8 35.8 %collective-permute-start.13 = (bf16[2,2,2,64,640]{4,3,2,1,0:T(8,128)(2,1)}, bf16[2,2,2,64,640]{4,3,2,1,0:T(8,128)(2,1)}, u32[]{:S(2)}, u32[]{:S(2)}) collective-permute-start(bf16[2,2,2,64,640]{4,3,2,1,0:T(8,128)(2,1)} %pad_maximum_fusion.3), channel_id=1, source_target_pairs={{0,1},{1,0},{2,3},{3,2},{4,5},{5,4},{6,7},{7,6},{8,9},{9,8},{10,11... | collective-permute-start | bytes 1966088 | tf_op jit(solution)/shard_map/ppermute | solution.py:1369
  110.9 15.8 %collective-permute-start.16 = (bf16[2,2,2,64,640]{4,3,2,1,0:T(8,128)(2,1)}, bf16[2,2,2,64,640]{4,3,2,1,0:T(8,128)(2,1)}, u32[]{:S(2)}, u32[]{:S(2)}) collective-permute-start(bf16[2,2,2,64,640]{4,3,2,1,0:T(8,128)(2,1)} %pad_maximum_fusion.4), channel_id=1, source_target_pairs={{0,1},{1,0},{2,3},{3,2},{4,5},{5,4},{6,7},{7,6},{8,9},{9,8},{10,11... | collective-permute-start | bytes 1966088 | tf_op jit(solution)/shard_map/ppermute | solution.py:1369
  113.5 10.8 %collective-permute-start.10 = (bf16[256,512]{1,0:T(8,128)(2,1)}, bf16[256,512]{1,0:T(8,128)(2,1)S(1)}, u32[]{:S(2)}, u32[]{:S(2)}) collective-permute-start(bf16[256,512]{1,0:T(8,128)(2,1)} %get-tuple-element.152.refs_0_), channel_id=1, source_target_pairs={{0,2},{1,3},{2,0},{3,1},{4,6},{5,7},{6,4},{7,5},{8,10},{9,11},{10,... | collective-permute-start | bytes 786440 | tf_op jit(solution)/shard_map/ppermute | solution.py:1369
  116.4 10.3 %collective-permute-start.9 = (bf16[256,512]{1,0:T(8,128)(2,1)}, bf16[256,512]{1,0:T(8,128)(2,1)S(1)}, u32[]{:S(2)}, u32[]{:S(2)}) collective-permute-start(bf16[256,512]{1,0:T(8,128)(2,1)} %get-tuple-element.152.refs_0_), channel_id=1, source_target_pairs={{0,1},{1,0},{2,3},{3,2},{4,5},{5,4},{6,7},{7,6},{8,9},{9,8},{10,11... | collective-permute-start | bytes 786440 | tf_op jit(solution)/shard_map/ppermute | solution.py:1369
  124.4 2.3 collective-permute-start.11
  172.2 3.8 collective-permute-start.18
  174.9 280.9 %reduce-scatter.2.cloned.1.call-start = ((), (), s32[]{:S(2)}) async-start(), calls=%async_computation.4 | async-start | bytes 5242880 | tf_op jit(solution)/shard_map/reduce_scatter | solution.py:1610
  184.6 8.4 %collective-permute-start.20 = (bf16[256,512]{1,0:T(8,128)(2,1)}, bf16[256,512]{1,0:T(8,128)(2,1)S(1)}, u32[]{:S(2)}, u32[]{:S(2)}) collective-permute-start(bf16[256,512]{1,0:T(8,128)(2,1)} %get-tuple-element.159.refs_0_), channel_id=1, source_target_pairs={{0,2},{1,3},{2,0},{3,1},{4,6},{5,7},{6,4},{7,5},{8,10},{9,11},{10,... | collective-permute-start | bytes 786440 | tf_op jit(solution)/shard_map/ppermute | solution.py:1369
  186.9 6.2 collective-permute-start.19
  193.0 1.5 collective-permute-start.21
  226.2 8.6 %collective-permute-start.23 = (bf16[256,512]{1,0:T(8,128)(2,1)}, bf16[256,512]{1,0:T(8,128)(2,1)S(1)}, u32[]{:S(2)}, u32[]{:S(2)}) collective-permute-start(bf16[256,512]{1,0:T(8,128)(2,1)} %get-tuple-element.163.refs_0_), channel_id=1, source_target_pairs={{0,2},{1,3},{2,0},{3,1},{4,6},{5,7},{6,4},{7,5},{8,10},{9,11},{10,... | collective-permute-start | bytes 786440 | tf_op jit(solution)/shard_map/ppermute | solution.py:1369
  227.3 8.2 %collective-permute-start.22 = (bf16[256,512]{1,0:T(8,128)(2,1)}, bf16[256,512]{1,0:T(8,128)(2,1)S(1)}, u32[]{:S(2)}, u32[]{:S(2)}) collective-permute-start(bf16[256,512]{1,0:T(8,128)(2,1)} %get-tuple-element.163.refs_0_), channel_id=1, source_target_pairs={{0,1},{1,0},{2,3},{3,2},{4,5},{5,4},{6,7},{7,6},{8,9},{9,8},{10,11... | collective-permute-start | bytes 786440 | tf_op jit(solution)/shard_map/ppermute | solution.py:1369
  234.8 1.5 collective-permute-start.24
  412.0 38.2 %copy-start.9 = (bf16[2,4,64,1024]{3,2,1,0:T(8,128)(2,1)S(1)}, bf16[2,4,64,1024]{3,2,1,0:T(8,128)(2,1)}, u32[]{:S(2)}) copy-start(bf16[2,4,64,1024]{3,2,1,0:T(8,128)(2,1)} %get-tuple-element.220) | copy-start | bytes 3145732
  (47 other events, 368.5 us)
Sparse Core Ops, SparseCore 0:
  56.4 122.4 all-gather.2
  180.5 80.3 all-gather.4
  345.0 75.8 reduce-scatter.1

commit v4 on v3

--- a/solution.py
+++ b/solution.py
@@ -25,7 +25,7 @@
 
 BF = jnp.bfloat16
 F32 = jnp.float32
-GROUP = 2
+GROUP = 4
 GELU_C = math.sqrt(2.0 / math.pi)
 GELU_A = 0.044715
 
@@ -78,12 +78,12 @@
 
 
 def call(
-    kernel, outs, in_specs, out_specs, operands, after=(), flows=(), ident=0, greet=(), greet_all=None, hold=None, **options
+    kernel, outs, in_specs, out_specs, operands, after=(), flows=(), ident=0, greet=(), greet_all=(), hold=None, **options
 ):
     used, spare, token, riders = len(operands), len(after), len(outs), len(flows)
     asks = [flow.ask for flow in flows]
     pairs = sorted({ask[1:] for ask in asks} | set(greet))
-    pairs = [pair for pair in pairs if pair[0] != greet_all]
+    pairs = [pair for pair in pairs if pair[0] not in greet_all]
     grid = options.get("grid")
     scratch = list(options.pop("scratch_shapes", []))
     far = pl.BlockSpec(memory_space=pl.ANY)
@@ -110,10 +110,13 @@
                 pl.semaphore_signal(
                     barrier, inc=1, device_id={axis: flipped(axis, bit)}, device_id_type=MESH
                 )
-            others = lax.axis_size(greet_all) - 1 if greet_all else 0
-            for step in range(others):
-                peer = (lax.axis_index(greet_all) + step + 1) % (others + 1)
-                pl.semaphore_signal(barrier, inc=1, device_id={greet_all: peer}, device_id_type=MESH)
+            others = 0
+            for axis in greet_all:
+                count = lax.axis_size(axis)
+                for step in range(1, count):
+                    peer = (lax.axis_index(axis) + step) % count
+                    pl.semaphore_signal(barrier, inc=1, device_id={axis: peer}, device_id_type=MESH)
+                others += count - 1
             pl.semaphore_wait(barrier, len(pairs) + others)
             if hold is None:
                 fly()
@@ -126,7 +129,7 @@
             for copy in copies():
                 copy.wait()
 
-        if riders or greet:
+        if riders or greet or greet_all:
             pl.when(pl.program_id(0) == 0)(launch) if grid else launch()
         token_ref[...] = jnp.zeros((1, 128), F32)
         if hold is not None and grid:
@@ -140,7 +143,7 @@
         if riders:
             pl.when(pl.program_id(0) == grid[0] - 1)(settle) if grid else settle()
 
-    if riders or greet:
+    if riders or greet or greet_all:
         options["compiler_params"] = pltpu.CompilerParams(
             vmem_limit_bytes=VMEM_LIMIT, collective_id=ident, has_side_effects=True
         )
@@ -272,23 +275,23 @@
     return rest + (1 - low if p & 1 else low) + 2 * (1 - high if p & 2 else high)
 
 
-def load_weights(sources, columns, layer, w_ref, sems):
+def load_weights(sources, low, w_ref, sems):
     copies = []
     for p in range(w_ref.shape[0]):
         if len(sources) > 1:
             source = sources[p]
         else:
-            source = sources[0].at[:, turned(p), layer, :, columns[0]:columns[1]]
+            source = sources[0].at[:, turned(p), :, low:low + w_ref.shape[3]]
         copies.append(pltpu.make_async_copy(source, w_ref.at[p], sems.at[p]))
         copies[p].start()
     return copies
 
 
-def attend_forward_kernel(layer, count, hid0_ref, hid1_ref, hid2in_ref, hid3_ref, stream_ref, nrm_ref, *refs):
+def attend_forward_kernel(low, count, hidden_ref, stream_ref, nrm_ref, *refs):
     sources = refs[:count]
     (
         mid_out, hid2_out, hid_ref, kv_out, q_out, skv_out, attw_out, mixed_out, permo_out, sort_out,
-        w_ref, perm_scr, acc_scr, sems,
+        w_ref, perm_scr, acc_scr, piece_scr, sems, send_sems, recv_sems,
     ) = refs[count:]
     length, width = hid_ref.shape
     rows = stream_ref.shape[0]
@@ -299,24 +302,43 @@
     own = pl.multiple_of(my * rows, rows)
     own_block = pl.multiple_of(my * own_blocks, own_blocks)
     lower = iota((1, 128), 1) < HD
-    copies = load_weights(sources, (0, ATTN), layer, w_ref, sems)
-    for p, piece in enumerate((hid0_ref, hid1_ref, hid2in_ref, hid3_ref)):
-        hid_ref[pl.ds(pl.multiple_of(turned(p) * rows, rows), rows), :] = piece[...]
+    copies = load_weights(sources, low, w_ref, sems)
+
+    def hop(at, source, target, which):
+        return remote(
+            piece_scr.at[source], piece_scr.at[target], send_sems.at[at], recv_sems.at[at], *HEADS[which]
+        )
+
+    far, near, cross = hop(0, 0, 2, 1), hop(1, 0, 1, 0), hop(2, 2, 3, 0)
+    piece_scr[0] = hidden_ref[...]
+    far.start()
+    near.start()
     for copy in copies:
         copy.wait()
 
-    def project(step, _):
-        j, tile = step // (length // rows), step % (length // rows)
-        at = pl.multiple_of(tile * rows, rows)
-        w = w_ref[j, :, :, C_KVS[0]:C_KVS[1]].reshape(width, C_KVS[1] - C_KVS[0])
-        got = dot_nn(hid_ref[pl.ds(at, rows), :], w)
-        kv_out[j, pl.ds(at, rows), :] = got[:, :256].astype(BF)
-        sort_out[j, pl.ds(pl.multiple_of(tile * own_blocks, own_blocks), own_blocks), :] = jnp.sum(
-            got[:, 256:].reshape(own_blocks, BLOCK, 128), 1
-        ) / math.sqrt(BLOCK)
-        return 0
-
-    lax.fori_loop(0, pairs * (length // rows), project, 0)
+    def project(p):
+        tile = turned(p)
+        at = pl.ds(pl.multiple_of(tile * rows, rows), rows)
+        blocks_at = pl.ds(pl.multiple_of(tile * own_blocks, own_blocks), own_blocks)
+        hid_ref[at, :] = piece_scr[p]
+
+        def columns(j, _):
+            w = w_ref[j, :, :, C_KVS[0]:C_KVS[1]].reshape(width, C_KVS[1] - C_KVS[0])
+            got = dot_nn(piece_scr[p], w)
+            kv_out[j, at, :] = got[:, :256].astype(BF)
+            sort_out[j, blocks_at, :] = jnp.sum(got[:, 256:].reshape(own_blocks, BLOCK, 128), 1) / math.sqrt(BLOCK)
+            return 0
+
+        lax.fori_loop(0, pairs, columns, 0)
+
+    project(0)
+    near.wait()
+    project(1)
+    far.wait()
+    cross.start()
+    project(2)
+    cross.wait()
+    project(3)
 
     scores = jnp.stack(
         [sort_out[h // 2][:, (h % 2) * BLOCK:(h % 2) * BLOCK + blocks] for h in range(2 * pairs)]
@@ -361,12 +383,12 @@
     hid2_out[...] = norm_apply(middle, nrm_ref[0:1, :], nrm_ref[1:2, :])
 
 
-def feed_forward_kernel(layer, count, mid_ref, hid2_ref, nrm_ref, *refs):
+def feed_forward_kernel(low, count, mid_ref, hid2_ref, nrm_ref, *refs):
     sources = refs[:count]
     stream_out, hnext_out, upw_out, act_out, w_ref, acc_scr, sems = refs[count:]
     width = mid_ref.shape[1]
     pairs = w_ref.shape[0]
-    copies = load_weights(sources, (ATTN, ATTN + FEED), layer, w_ref, sems)
+    copies = load_weights(sources, low, w_ref, sems)
     acc_scr[...] = mid_ref[...]
     for copy in copies:
         copy.wait()
@@ -407,9 +429,9 @@
     return pltpu.VMEM((pairs, parts, depth, columns), BF)
 
 
-def attend_forward(layer, hidden, stream, sources, nrm, after=(), flows=(), ident=0):
+def attend_forward(low, hidden, stream, sources, nrm, after=(), flows=(), ident=0):
     rows, width = stream.shape
-    pairs = len(hidden)
+    pairs = lax.axis_size("head")
     length = rows * pairs
     own_blocks, blocks = rows // BLOCK, length // BLOCK
     outs = [
@@ -425,25 +447,29 @@
         shape((pairs, blocks, 128), F32),
     ]
     return call(
-        functools.partial(attend_forward_kernel, layer, len(sources)),
+        functools.partial(attend_forward_kernel, low, len(sources)),
         outs,
-        [VM] * (pairs + 2) + [FAR] * len(sources),
+        [VM] * 3 + [FAR] * len(sources),
         [VM] * len(outs),
-        (*hidden, stream, nrm, *sources),
+        (hidden, stream, nrm, *sources),
         after,
         flows,
         ident,
+        HEADS,
         scratch_shapes=[
             weight_slots(sources, pairs, ATTN),
             pltpu.VMEM((2 * pairs, blocks, blocks), F32),
             pltpu.VMEM((rows, width), F32),
+            pltpu.VMEM((pairs, rows, width), BF),
             pltpu.SemaphoreType.DMA((pairs,)),
+            pltpu.SemaphoreType.DMA((3,)),
+            pltpu.SemaphoreType.DMA((3,)),
         ],
         **settings(18_000_000_000, 10_000_000, "attend_forward"),
     )
 
 
-def feed_forward(layer, middle, hidden, sources, nrm, after=(), flows=(), ident=0):
+def feed_forward(low, middle, hidden, sources, nrm, after=(), flows=(), ident=0):
     rows, width = middle.shape
     pairs = lax.axis_size("head")
     outs = [
@@ -453,7 +479,7 @@
         shape((pairs, rows, 512), BF),
     ]
     return call(
-        functools.partial(feed_forward_kernel, layer, len(sources)),
+        functools.partial(feed_forward_kernel, low, len(sources)),
         outs,
         [VM] * 3 + [FAR] * len(sources),
         [VM] * len(outs),
@@ -488,7 +514,7 @@
 
 
 def feed_backward_kernel(
-    layer, count, dy_ref, above_ref, carry_ref, gain_above_ref, gain_two_ref,
+    low, count, dy_ref, above_ref, carry_ref, gain_above_ref, gain_two_ref,
     mid_ref, hid2_ref, upw_ref, act_ref, *refs
 ):
     sources = refs[:count]
@@ -498,7 +524,7 @@
     ) = refs[count:]
     width = carry_ref.shape[1]
     pairs = w_ref.shape[0]
-    copies = load_weights(sources, (ATTN, ATTN + FEED), layer, w_ref, sems)
+    copies = load_weights(sources, low, w_ref, sems)
 
     back, pair = norm_back(dy_ref[...], above_ref[...], gain_above_ref[...])
     pair_above_out[...] = pair
@@ -516,9 +542,9 @@
 
     def feed(at, _):
         j = near_first(at)
-        low = low_scr[...]
+        rounded = low_scr[...]
         w_dn = w_ref[j, :, :, C_DOWN[0]:C_DOWN[1]].reshape(width, 512)
-        grad_act = dot_nn(low, w_dn)
+        grad_act = dot_nn(rounded, w_dn)
         x = upw_ref[j]
         squared = x * x
         bent = jnp.tanh(GELU_C * (x + GELU_A * squared * x))
@@ -526,7 +552,7 @@
             GELU_C * (1.0 + 3.0 * GELU_A * squared)
         )
         grad_up = (grad_act * slope).astype(BF)
-        put(wgrad_scr, j, C_DOWN, dot_tn(low, act_ref[j]))
+        put(wgrad_scr, j, C_DOWN, dot_tn(rounded, act_ref[j]))
         put(wgrad_scr, j, C_UP, dot_tn(hid2_ref[...], grad_up))
         w_up = w_ref[j, :, :, C_UP[0]:C_UP[1]].reshape(width, 512)
         acc_scr[...] += dot_nt(grad_up, w_up)
@@ -554,7 +580,7 @@
 
 
 def attend_backward_kernel(
-    layer, count, carry_ref, hid_ref, kv_ref, q_ref, skv_ref, attw_ref, mixed_ref, permo_ref, sort_ref,
+    low, count, carry_ref, hid_ref, kv_ref, q_ref, skv_ref, attw_ref, mixed_ref, permo_ref, sort_ref,
     *refs
 ):
     sources = refs[:count]
@@ -573,7 +599,7 @@
     own_block = pl.multiple_of(my * own_blocks, own_blocks)
     lower = iota((1, 128), 1) < HD
     take = GROUP * BLOCK
-    copies = load_weights(sources, (0, ATTN), layer, w_ref, sems)
+    copies = load_weights(sources, low, w_ref, sems)
     low_scr[...] = carry_ref[...].astype(BF)
     dperm_scr[...] = jnp.zeros_like(dperm_scr)
     for copy in copies:
@@ -581,10 +607,10 @@
     scale_key = 1.0 / math.sqrt(HD)
 
     def attend(j, _):
-        low = low_scr[...]
+        rounded = low_scr[...]
         w_o = w_ref[j, :, :, C_OUT[0]:C_OUT[1]].reshape(width, 128)
-        grad_mixed = dot_nn(low, w_o).astype(BF)
-        put(wgrad_scr, j, C_OUT, dot_tn(low, mixed_ref[j]))
+        grad_mixed = dot_nn(rounded, w_o).astype(BF)
+        put(wgrad_scr, j, C_OUT, dot_tn(rounded, mixed_ref[j]))
         q = q_ref[j]
         zero = jnp.zeros_like(q)
         queries = []
@@ -700,14 +726,14 @@
     dy_out[...] = piece(0) + gnear_scr[0].astype(F32) + gfar_scr[...].astype(F32)
 
 
-def feed_backward(layer, dy, above, carry, gain_above, sources, gain_two, kept, features, after=(), flows=(), ident=0):
+def feed_backward(low, dy, above, carry, gain_above, sources, gain_two, kept, features, after=(), flows=(), ident=0):
     rows, width = carry.shape
     pairs = lax.axis_size("head")
     slots = weight_slots(sources, pairs, FEED)
     half = shape((pairs // 2, lax.axis_size("dp") // 2, features, FEED), BF)
     outs = [half, half, shape((rows, width), F32), shape((2, width), F32), shape((2, width), F32)]
     return call(
-        functools.partial(feed_backward_kernel, layer, len(sources)),
+        functools.partial(feed_backward_kernel, low, len(sources)),
         outs,
         [VM] * (5 + len(kept)) + [FAR] * len(sources),
         [VM] * 5,
@@ -730,14 +756,14 @@
     )
 
 
-def attend_backward(layer, carry, sources, kept, after=(), flows=(), ident=0):
+def attend_backward(low, carry, sources, kept, after=(), flows=(), ident=0):
     rows, width = carry.shape
     pairs = lax.axis_size("head")
     length = rows * pairs
     own_blocks, blocks = rows // BLOCK, length // BLOCK
     slots = weight_slots(sources, pairs, ATTN)
     return call(
-        functools.partial(attend_backward_kernel, layer, len(sources)),
+        functools.partial(attend_backward_kernel, low, len(sources)),
         [shape((rows, width), F32)] + [shape(slots.shape[1:], BF)] * 2,
         [VM] * (1 + len(kept)) + [FAR] * len(sources),
         [VM] * 3,
@@ -812,7 +838,7 @@
 
 
 def stages_of_all():
-    return [(axis, bit) for axis in ("head", "dp") for bit in reversed(bits_of(axis))]
+    return [("head", bit) for bit in bits_of("head")] + [("dp", bit) for bit in reversed(bits_of("dp"))]
 
 
 def embed_back_kernel(
@@ -820,19 +846,20 @@
 ):
     pair_refs = refs[:count_pairs]
     out_ref, square_out, pair_out, acc_ref, sum_scr, come_scr, send_sems, recv_sems = refs[count_pairs:]
-    features = grad_ref.shape[0]
-    count = grad_ref.shape[1]
+    pieces, features, tile = grad_ref.shape
+    count = pieces * tile
     bins = acc_ref.shape[0] // features
     step = pl.program_id(0)
     stages = stages_of_all()
-    first_hop = pl.num_programs(0) // 2
+    first_hop = pl.num_programs(0) - len(stages) - 1
+    hop_step = [0] + [first_hop + at for at in range(1, len(stages) + 1)]
 
     def hop(at):
         return remote(sum_scr, come_scr.at[at], send_sems.at[at], recv_sems.at[at], *stages[at])
 
     for at in range(len(stages) + 1):
 
-        @pl.when(step == first_hop + 3 * at)
+        @pl.when(step == hop_step[at])
         def _(at=at):
             if at == 0:
                 for place, pair_ref in enumerate(pair_refs):
@@ -848,7 +875,7 @@
     local = tok_ref[...] - base_ref[0]
     high, low = local >> 8, local & 255
     hot = (iota((256, count), 0) == low).astype(BF)
-    grad = grad_ref[...]
+    grad = jnp.concatenate([grad_ref[at] for at in range(pieces)], 1)
     wide = jnp.concatenate(
         [jnp.where(high == at, grad, jnp.zeros_like(grad)) for at in range(bins)], 0
     )
@@ -886,8 +913,8 @@
         [shape((features, vocab), F32), shape((features, 256), F32), shape(all_pairs, F32)],
         [
             SM,
-            pl.BlockSpec((1, tile), lambda i: (0, i)),
-            pl.BlockSpec((None, features, tile), lambda i: (i, 0, 0)),
+            pl.BlockSpec((1, 4 * tile), lambda i: (0, i)),
+            pl.BlockSpec((4, features, tile), lambda i: (i, 0, 0)),
             pl.BlockSpec((features, vocab), still),
         ]
         + [pl.BlockSpec((2, width), still)] * count_pairs,
@@ -901,7 +928,8 @@
         flows,
         ident,
         tuple(stages_of_all()),
-        grid=(pieces,),
+        hold=1,
+        grid=(pieces // 4,),
         scratch_shapes=[
             pltpu.VMEM((features * (vocab // 256), 256), F32),
             pltpu.VMEM(all_pairs, F32),
@@ -957,11 +985,29 @@
     part_scr[...] = jnp.where(
         row == 0, jnp.where(lane == 0, square, jnp.where(lane == 1, loss_ref[...], 0.0)), 0.0
     )
-    for at, (axis, bit) in enumerate(stages_of_all()):
-        hop = remote(part_scr, parts_scr.at[at], part_send.at[at], part_recv.at[at], axis, bit)
-        hop.start()
-        hop.wait()
-        part_scr[...] += parts_scr[at]
+    place = 0
+    for axis in ("head", "dp"):
+        count = lax.axis_size(axis)
+        hops = []
+        here = place + lax.axis_index(axis)
+        parts_scr[here] = part_scr[...]
+        for step in range(1, count):
+            at = place + step - 1
+            hops.append(
+                pltpu.make_async_remote_copy(
+                    src_ref=part_scr,
+                    dst_ref=parts_scr.at[here],
+                    send_sem=part_send.at[at],
+                    recv_sem=part_recv.at[at],
+                    device_id={axis: (lax.axis_index(axis) + step) % count},
+                    device_id_type=MESH,
+                )
+            )
+            hops[-1].start()
+        for hop in hops:
+            hop.wait()
+        part_scr[...] = jnp.sum(parts_scr[place:place + count], 0)
+        place += count
     total_out[...] = part_scr[...]
 
 
@@ -972,7 +1018,7 @@
     operands = [flat(one) for one in (*attn, *feed)] + [*other]
     count, features = operands[0].shape[:2]
     columns = ATTN + FEED
-    stages = len(stages_of_all())
+    stages = lax.axis_size("head") + lax.axis_size("dp")
     one = shape((features, columns), F32)
     fixed, extra = len(operands), len(thirds)
 
@@ -989,7 +1035,7 @@
         [VM] * 3,
         (*operands, *thirds, squares, pair_grads, loss),
         ident=ident,
-        greet=tuple(stages_of_all()),
+        greet_all=("head", "dp"),
         scratch_shapes=[
             pltpu.VMEM((count, features, columns), F32),
             pltpu.VMEM((count - 1, features, columns), BF),
@@ -1136,7 +1182,7 @@
         flows,
         ident,
         HEADS,
-        "dp",
+        ("dp",),
         hold=0,
         scratch_shapes=[
             pltpu.VMEM((dp, features, rows), BF),
@@ -1418,11 +1464,6 @@
     return value
 
 
-def pieces_of_head(value):
-    across = swap(value, "head", 2)
-    return value, swap(value, "head", 1), across, swap(across, "head", 1)
-
-
 def pack_weights(attn_in, attn_out, ffn_up, ffn_down):
     features = attn_in.shape[0]
     low = attn_in.astype(BF)
@@ -1446,58 +1487,31 @@
 
 class Gather:
     def __init__(self, packed):
-        self.bits = bits_of("dp")
-        self.features = packed.shape[0]
-        value = packed.reshape((1,) * len(self.bits) + packed.shape)
-        for dim, bit in enumerate(self.bits[:-1]):
+        bits = bits_of("dp")
+        value = packed.reshape((1,) * len(bits) + packed.shape)
+        for dim, bit in enumerate(bits[:-1]):
             value = in_order(value, swap(value, "dp", bit), "dp", bit, dim)
         self.value = value
 
-    def last(self, value):
-        dim, bit = len(self.bits) - 1, self.bits[-1]
-        return in_order(value, swap(value, "dp", bit), "dp", bit, dim)
-
-    def first_step(self):
-        self.one, two = self.value[..., :ATTN], self.value[..., ATTN:]
-        self.across = swap(self.one, "head", 2)
-        self.two = two, swap(two, "dp", self.bits[-1])
-
-    def second_step(self, token):
-        dim, bit = len(self.bits) - 1, self.bits[-1]
-        self.two = in_order(self.two[0], self.two[1] + token.astype(BF), "dp", bit, dim)
-        self.one = self.last(self.one)
-        self.across = self.last(self.across + token.astype(BF))
-
-    def pieces(self, mine, across):
-        return self.shape_pieces(mine, swap(mine, "head", 1), across, swap(across, "head", 1))
-
-    def shape_pieces(self, *got):
-        return [one.reshape(-1, depth_of(self.features), one.shape[-1]) for one in got]
-
     def finish(self):
-        return self.pieces(self.one, self.across)
-
-    def feed_flows(self):
-        def once(bit):
-            return (yield self.two, "head", bit)
-
-        self.flows = [Flow(once(2)), Flow(once(1))]
-        return self.flows
-
-    def finish_feed(self):
-        across, near = (flow.finish() for flow in self.flows)
-        return self.shape_pieces(self.two, near, across, swap(across, "head", 1))
+        bits = bits_of("dp")
+        across = swap(self.value, "head", 2)
+        got = []
+        for value in (self.value, across):
+            whole = in_order(value, swap(value, "dp", bits[-1]), "dp", bits[-1], len(bits) - 1)
+            got += [whole, swap(whole, "head", 1)]
+        features, columns = self.value.shape[-2:]
+        return [one.reshape(-1, depth_of(features), columns) for one in got]
 
 
 def gather_rest(packed):
     dp, head = lax.axis_size("dp"), lax.axis_size("head")
-    layers, features, columns = packed.shape
+    features, columns = packed.shape
     whole = lax.all_gather(packed, ("dp", "head"), axis=0, tiled=True)
     fold = depth_of(features) // features
     if fold > 1:
-        whole = whole.reshape(dp // fold, fold, head, layers, features, columns)
-        whole = whole.transpose(0, 2, 3, 1, 4, 5)
-    return whole.reshape(dp // fold, head, layers, fold * features, columns)
+        whole = whole.reshape(dp // fold, fold, head, features, columns).transpose(0, 2, 1, 3, 4)
+    return whole.reshape(dp // fold, head, fold * features, columns)
 
 
 def adamw(weight, gradient, moment_one, moment_two, factor, step_rate):
@@ -1545,7 +1559,8 @@
     packs = [
         pack_weights(attn_in[at], attn_out[at], ffn_up[at], ffn_down[at]) for at in range(layers)
     ]
-    leader = Gather(packs[0])
+    leader = Gather(packs[0][:, :ATTN])
+    idents = iter(range(1, 64))
 
     half = vocab // 2
     other = swap(lax.dynamic_slice_in_dim(low_table, (1 - odd) * half, half, 1), "dp", 1)
@@ -1554,8 +1569,7 @@
 
     base = (my_head * vocab).astype(jnp.int32).reshape(1)
     found, token = embed_lookup(base, all_tokens, low_table, [leader.value])
-    leader.first_step()
-    rest_weights = gather_rest(jnp.stack(packs[1:]) + token.astype(BF))
+    rest_weights = gather_rest(jnp.concatenate([packs[0][:, ATTN:]] + packs[1:], 1))
     found = found.reshape(features, dp, head, rows)
     for bit in (1, 2):
         flag = (my_head & bit) // bit
@@ -1563,32 +1577,27 @@
         dim = 3 if bit == 1 else 2
         other = swap(lax.dynamic_index_in_dim(found, 1 - flag, dim, False), "head", bit)
         found = lax.dynamic_index_in_dim(found, flag, dim, False) + other
-    leader.second_step(token)
     found = lax.all_to_all(found, "dp", split_axis=1, concat_axis=0, tiled=True)
     stream, hidden, token = start_stream(found.reshape(width, rows), nrm[0])
     head_table = lax.all_gather(
         head_table + token.astype(BF), "dp", axis=0, tiled=True, axis_index_groups=outer
     )
-    hidden = pieces_of_head(hidden)
-    sources = [[leader.finish(), None]] + [[[rest_weights], [rest_weights]]] * (layers - 1)
+    sources = [((leader.finish(), 0), ([rest_weights], 0))]
+    for at in range(1, layers):
+        start = FEED + (at - 1) * (ATTN + FEED)
+        sources.append((([rest_weights], start), ([rest_weights], start + ATTN)))
 
     kept = []
     for at in range(layers):
-        of = max(at - 1, 0)
-        for_attend, for_feed = sources[at]
+        (for_attend, attend_low), (for_feed, feed_low) = sources[at]
         middle, hidden_two, *saved, token = attend_forward(
-            of, hidden, stream, for_attend, nrm[2 * at + 1], [],
-            leader.feed_flows() if at == 0 else [],
+            attend_low, hidden, stream, for_attend, nrm[2 * at + 1], ident=next(idents)
         )
-        if at == 0:
-            for_feed = sources[0][1] = leader.finish_feed()
-        result, hidden, upward, active, _ = feed_forward(
-            of, middle, hidden_two, for_feed, nrm[2 * at + 2]
+        result, hidden, upward, active_rows, _ = feed_forward(
+            feed_low, middle, hidden_two, for_feed, nrm[2 * at + 2]
         )
-        kept.append((stream, (middle, hidden_two, upward, active), saved))
+        kept.append((stream, (middle, hidden_two, upward, active_rows), saved))
         stream = result
-        if at + 1 < layers:
-            hidden = pieces_of_head(hidden)
 
     def line_of(values):
         values = values.reshape(dp, head, rows)
@@ -1600,7 +1609,6 @@
 
     goals = line_of(lines[:, length:2 * length]) - (my_head * vocab + odd * half).astype(jnp.int32)
     goals = goals.astype(F32).reshape(SLOTS, 1, rows)
-    idents = iter(range(1, 64))
     rows_all, stat_lines, loss_here, token = head_forward(
         hidden, head_table, goals, line_of(counted).reshape(SLOTS, 1, rows), next(idents)
     )
@@ -1643,19 +1651,19 @@
         return [flow for flow in candidates if flow is not None and flow.ask is not None]
 
     for at in reversed(range(layers)):
-        of = max(at - 1, 0)
         stream_in, for_feed, for_attend = kept[at]
+        (attend_sources, attend_low), (feed_sources, feed_low) = sources[at]
         above_attn, above_feed = (attns + [None])[at + 1], (feeds + [None])[at + 1]
         top_attn, top_feed = (attns + [None] * 2)[at + 2], (feeds + [None] * 2)[at + 2]
         here, there, carry, pair_above, pair_two, token = feed_backward(
-            of, dy, above, carry, nrm[2 * at + 2, 0:1], sources[at][1], nrm[2 * at + 1, 0:1], for_feed,
+            feed_low, dy, above, carry, nrm[2 * at + 2, 0:1], feed_sources, nrm[2 * at + 1, 0:1], for_feed,
             features, [grad_half] if at == 0 else [], active(top_attn, above_attn if at == 0 else None), next(idents),
         )
         feeds[at] = Flow(feed_steps(here, there))
         if at + 2 < layers:
             lasts[at + 2] = Flow(last_steps(top_attn, top_feed))
         dy, *attn_sums, token = attend_backward(
-            of, carry, sources[at][0], for_attend, [],
+            attend_low, carry, attend_sources, for_attend, [],
             active(feeds[at], above_attn, above_feed, *lasts), next(idents),
         )
         attns[at] = Flow(attn_steps(*attn_sums))

time: 661 us -> 600 us (0.908)
  Pallas kernels: 474 us -> 447 us
  waiting for transfers between devices: 68.7 us -> 51.1 us
  other arithmetic: 33.5 us -> 23.2 us
    ppermute x26 -> x15, waiting for transfers between devices: 68.6 us -> 32.9 us  [swap(): lax.ppermute(value, axis, [(at, at ^ bit) for at in range(lax.axis_size(a...]
    pallas_call x20, Pallas kernels: 474 us -> 447 us  [call(): pl.pallas_call(run, out_shape=list(outs) + [jax.ShapeDtypeStruct((1, 128)...]
    all_to_all x1, waiting for transfers between devices: 0.01 us -> 15.5 us  [body(): found = lax.all_to_all(found, 'dp', split_axis=1, concat_axis=0, tiled=True)]
    ppermute x26 -> x15, starting transfers between devices: 19.7 us -> 18.5 us  [swap(): lax.ppermute(value, axis, [(at, at ^ bit) for at in range(lax.axis_size(a...]
  transfers between devices with their start and end apart: 30 -> 19, of which waited for: 15 -> 9; matrix products, arithmetic and copies ran while one was open for 6% -> 4% of each run, Pallas kernels for 33% -> 36%
where the time goes in v4:
time: 600 us; the launch traced here: 592 us
  Pallas kernels  447 us (74%)
  waiting for transfers between devices  51.1 us (9%)
  local copies, waits for them, and re-layouts  28 us (5%)
  starting transfers between devices  24.4 us (4%)
  other arithmetic  23.2 us (4%)
  between operations  18.5 us (3%)
    pallas_call x20, Pallas kernels, call(): pl.pallas_call(run, out_shape=list(outs) + [jax.ShapeDtypeStruct((1, 128)...  447 us
    ppermute x15, waiting for transfers between devices, swap(): lax.ppermute(value, axis, [(at, at ^ bit) for at in range(lax.axis_size(a...  32.9 us
    ppermute x15, starting transfers between devices, swap(): lax.ppermute(value, axis, [(at, at ^ bit) for at in range(lax.axis_size(a...  18.5 us
    all_to_all x1, waiting for transfers between devices, body(): found = lax.all_to_all(found, 'dp', split_axis=1, concat_axis=0, tiled=True)  15.5 us
  transfers between devices with their start and end apart: 19, of which 9 were waited for; matrix products, arithmetic and copies ran while one was open for 4% of the time, Pallas kernels for 36%

profile of v4, /device:TPU:0, one launch (start us, length us, event | category | flops | bytes accessed | tf_op | source)
XLA Modules:
  0.0 592.2 jit_solution(15708333516014848277)
XLA Ops:
  12.0 4.1 collective-permute-start.3
  27.5 9.8 %collective-permute-done.2 = s32[2,2,1,2176]{3,2,1,0:T(1,128)S(1)} collective-permute-done((s32[2,2,1,2176]{3,2,1,0:T(1,128)S(1)}, s32[2,2,1,2176]{3,2,1,0:T(1,128)S(1)}, u32[]{:S(2)}, u32[]{:S(2)}) %collective-permute-start.2) | collective-permute-done | bytes 34848 | tf_op jit(solution)/shard_map/ppermute | solution.py:1415
  39.3 1.9 collective-permute-start.4
  41.8 4.0 collective-permute-done.4
  47.2 13.8 %embed_lookup.1 = (bf16[64,8192]{1,0:T(8,128)(2,1)}, f32[1,128]{1,0:T(1,128)}) custom-call(s32[1]{0:T(128)} %bitcast.refs_0_, s32[1,8192]{1,0:T(1,128)} %bitcast.256, bf16[64,8192]{1,0:T(8,128)(2,1)} %copy-done.3, bf16[2,2,1,64,640]{4,3,2,1,0:T(8,128)(2,1)} %copy-done.22), custom_call_target="tpu_custom_call" | custom-call | flops 15000000512 | bytes 4000000 | tf_op jit(solution)/shard_map/embed_lookup/pallas_call | solution.py:155
  61.0 1.8 reshape_reshape.10
  62.8 2.7 constant_dynamic-slice_fusion.26
  68.9 7.1 %collective-permute-done.11 = bf16[2,2,1,64,640]{4,3,2,1,0:T(8,128)(2,1)S(1)} collective-permute-done((bf16[2,2,1,64,640]{4,3,2,1,0:T(8,128)(2,1)S(1)}, bf16[2,2,1,64,640]{4,3,2,1,0:T(8,128)(2,1)S(1)}, u32[]{:S(2)}, u32[]{:S(2)}) %collective-permute-start.11) | collective-permute-done | bytes 327712 | tf_op jit(solution)/shard_map/ppermute | solution.py:1415
  78.8 9.8 %collective-permute-done.12 = bf16[2,2,1,64,640]{4,3,2,1,0:T(8,128)(2,1)S(1)} collective-permute-done((bf16[2,2,1,64,640]{4,3,2,1,0:T(8,128)(2,1)S(1)}, bf16[2,2,1,64,640]{4,3,2,1,0:T(8,128)(2,1)S(1)}, u32[]{:S(2)}, u32[]{:S(2)}) %collective-permute-start.12) | collective-permute-done | bytes 327712 | tf_op jit(solution)/shard_map/ppermute | solution.py:1415
  90.4 5.8 all-to-all-start
  97.5 15.5 %all-to-all-done = bf16[64,8,256]{2,0,1:T(8,128)(2,1)S(1)} async-done(((bf16[64,8,256]{2,0,1:T(8,128)(2,1)}), bf16[64,8,256]{2,0,1:T(8,128)(2,1)S(1)}, u32[]{:S(2)}, u32[]{:S(2)}) %all-to-all-start) | async-done | bytes 262176 | tf_op jit(solution)/shard_map/all_to_all | solution.py:1580
  113.7 2.0 start_stream.1
  117.7 23.3 %attend_forward.3 = (f32[256,512]{1,0:T(8,128)}, bf16[256,512]{1,0:T(8,128)(2,1)}, bf16[1024,512]{1,0:T(8,128)(2,1)}, bf16[4,1024,256]{2,1,0:T(8,128)(2,1)}, bf1...) custom-call(bf16[256,512]{1,0:T(8,128)(2,1)} %get-tuple-element.149., ...), custom_call_target="tpu_custom_call" | custom-call | flops 17999998976 | bytes 10000000 | tf_op jit(solution)/shard_map/attend_forward/pallas_call | solution.py:155
  141.0 1.8 all-gather.3.cloned.1.call-done
  142.8 7.4 %feed_forward.3 = (f32[256,512]{1,0:T(8,128)}, bf16[256,512]{1,0:T(8,128)(2,1)}, f32[4,256,512]{2,1,0:T(8,128)}, bf16[4,256,512]{2,1,0:T(8,128)(2,1)}, f32[1,128]{1,0:T(1,128)}) custom-call(f32[256,512]{1,0:T(8,128)} %get-tuple-element.151.refs_0_.refs_5_, bf16[256,512]{1,0:T(8,128)(2,1)} %get-tuple-element.152.refs_1_.refs_6_, ...), custom_call_target="tpu_custom_call" | custom-call | flops 8000000000 | bytes 8000000 | tf_op jit(solution)/shard_map/feed_forward/pallas_call | solution.py:155
  150.2 23.3 %attend_forward.4 = (f32[256,512]{1,0:T(8,128)}, bf16[256,512]{1,0:T(8,128)(2,1)}, bf16[1024,512]{1,0:T(8,128)(2,1)}, bf16[4,1024,256]{2,1,0:T(8,128)(2,1)}, bf1...) custom-call(bf16[256,512]{1,0:T(8,128)(2,1)} %get-tuple-element.153., ...), custom_call_target="tpu_custom_call" | custom-call | flops 17999998976 | bytes 10000000 | tf_op jit(solution)/shard_map/attend_forward/pallas_call | solution.py:155
  173.6 7.5 %feed_forward.4 = (f32[256,512]{1,0:T(8,128)}, bf16[256,512]{1,0:T(8,128)(2,1)}, f32[4,256,512]{2,1,0:T(8,128)}, bf16[4,256,512]{2,1,0:T(8,128)(2,1)}, f32[1,128]{1,0:T(1,128)}) custom-call(f32[256,512]{1,0:T(8,128)} %get-tuple-element.155.refs_0_.refs_5_, bf16[256,512]{1,0:T(8,128)(2,1)} %get-tuple-element.156.refs_1_.refs_6_, ...), custom_call_target="tpu_custom_call" | custom-call | flops 8000000000 | bytes 8000000 | tf_op jit(solution)/shard_map/feed_forward/pallas_call | solution.py:155
  181.1 34.5 %attend_forward.5 = (f32[256,512]{1,0:T(8,128)}, bf16[256,512]{1,0:T(8,128)(2,1)}, bf16[1024,512]{1,0:T(8,128)(2,1)}, bf16[4,1024,256]{2,1,0:T(8,128)(2,1)}, bf1...) custom-call(bf16[256,512]{1,0:T(8,128)(2,1)} %get-tuple-element.157., ...), custom_call_target="tpu_custom_call" | custom-call | flops 17999998976 | bytes 10000000 | tf_op jit(solution)/shard_map/attend_forward/pallas_call | solution.py:155
  215.6 7.4 %feed_forward.5 = (f32[256,512]{1,0:T(8,128)}, bf16[256,512]{1,0:T(8,128)(2,1)}, f32[4,256,512]{2,1,0:T(8,128)}, bf16[4,256,512]{2,1,0:T(8,128)(2,1)}, f32[1,128]{1,0:T(1,128)}) custom-call(f32[256,512]{1,0:T(8,128)} %get-tuple-element.159.refs_0_.refs_5_, bf16[256,512]{1,0:T(8,128)(2,1)} %get-tuple-element.160.refs_1_.refs_6_, ...), custom_call_target="tpu_custom_call" | custom-call | flops 8000000000 | bytes 8000000 | tf_op jit(solution)/shard_map/feed_forward/pallas_call | solution.py:155
  223.8 35.4 %head_forward.1 = (bf16[8,256,512]{2,1,0:T(8,128)(2,1)}, f32[8,2,256]{2,1,0:T(2,128)}, f32[1,1]{1,0:T(1,128)}, f32[1,128]{1,0:T(1,128)}) custom-call(bf16[256,512]{1,0:T(8,128)(2,1)} %get-tuple-element.161.refs_0_, bf16[512,4096]{1,0:T(8,128)(2,1)} %all-gather.5.cloned.1.call-done.refs_1_, f32[8,1,256]{2,1,0:T(1,128)} %subtract_convert_fusion.refs_2_, ...), custom_call_target="tpu_custom_call" | custom-call | flops 17999998976 | bytes 6000000 | tf_op jit(solution)/shard_map/head_forward/pallas_call | solution.py:155
  259.2 40.6 %head_backward.1 = (f32[256,512]{1,0:T(8,128)}, bf16[512,4096]{1,0:T(8,128)(2,1)}, f32[1,128]{1,0:T(1,128)}) custom-call(bf16[8,256,512]{2,1,0:T(8,128)(2,1)} %get-tuple-element.163.refs_0_, bf16[512,4096]{1,0:T(8,128)(2,1)} %all-gather.5.cloned.1.call-done.refs_1_, f32[8,1,256]{2,1,0:T(1,128)} %subtract_convert_fusion.refs_2_, ...), custom_call_target="tpu_custom_call" | custom-call | flops 35999997952 | bytes 14000000 | tf_op jit(solution)/shard_map/head_backward/pallas_call | solution.py:155
  303.4 12.3 %feed_backward.3 = (bf16[2,4,64,1024]{3,2,1,0:T(8,128)(2,1)}, bf16[2,4,64,1024]{3,2,1,0:T(8,128)(2,1)}, f32[256,512]{1,0:T(8,128)}, f32[2,512]{1,0:T(2,128)}, f32[2,512]{1,0:T(2,128)}, /*index=5*/f32[1,128]{1,0:T(1,128)}) custom-call(f32[256,512]{1,0:T(8,128)} %get-tuple-element.165.refs_0_, f32[256,512]{1,0:T(8,128)} %get-tuple-element.166.refs_1_, ...), custom_call_target="tpu_custom_call" | custom-call | flops 12000000000 | bytes 12000000 | tf_op jit(solution)/shard_map/feed_backward/pallas_call | solution.py:155
  315.7 33.7 %attend_backward.3 = (f32[256,512]{1,0:T(8,128)}, bf16[8,64,640]{2,1,0:T(8,128)(2,1)}, bf16[8,64,640]{2,1,0:T(8,128)(2,1)}, f32[1,128]{1,0:T(1,128)}, bf16[2,4,64,1024]{3,2,1,0:T(8,128)(2,1)}) custom-call(f32[256,512]{1,0:T(8,128)} %get-tuple-element.169.refs_0_.refs_2_, bf16[1024,512]{1,0:T(8,128)(2,1)} %get-tuple-element.170.refs_1_, ...), custom_call_target="tpu_custom_call" | custom-call | flops 20000000000 | bytes 16000000 | tf_op jit(solution)/shard_map/attend_backward/pallas_call | solution.py:155
  352.1 11.7 %feed_backward.4 = (bf16[2,4,64,1024]{3,2,1,0:T(8,128)(2,1)}, bf16[2,4,64,1024]{3,2,1,0:T(8,128)(2,1)}, f32[256,512]{1,0:T(8,128)}, f32[2,512]{1,0:T(2,128)}, f32[2,512]{1,0:T(2,128)}, /*index=5*/f32[1,128]{1,0:T(1,128)}) custom-call(f32[256,512]{1,0:T(8,128)} %get-tuple-element.179.refs_0_, f32[256,512]{1,0:T(8,128)} %get-tuple-element.158.refs_1_, ...), custom_call_target="tpu_custom_call" | custom-call | flops 12000000000 | bytes 12000000 | tf_op jit(solution)/shard_map/feed_backward/pallas_call | solution.py:155
  363.8 38.5 %attend_backward.4 = (f32[256,512]{1,0:T(8,128)}, bf16[8,64,640]{2,1,0:T(8,128)(2,1)}, bf16[8,64,640]{2,1,0:T(8,128)(2,1)}, f32[1,128]{1,0:T(1,128)}, bf16[2,4,6...) custom-call(f32[256,512]{1,0:T(8,128)} %get-tuple-element.182.refs_0_.refs_2_, ...), custom_call_target="tpu_custom_call" | custom-call | flops 20000000000 | bytes 16000000 | tf_op jit(solution)/shard_map/attend_backward/pallas_call | solution.py:155
  408.0 21.5 %feed_backward.5 = (bf16[2,4,64,1024]{3,2,1,0:T(8,128)(2,1)}, bf16[2,4,64,1024]{3,2,1,0:T(8,128)(2,1)}, f32[256,512]{1,0:T(8,128)}, f32[2,512]{1,0:T(2,128)}, f3...) custom-call(f32[256,512]{1,0:T(8,128)} %get-tuple-element.195.refs_0_, ...), custom_call_target="tpu_custom_call" | custom-call | flops 12000000000 | bytes 12000000 | tf_op jit(solution)/shard_map/feed_backward/pallas_call | solution.py:155
  432.5 36.2 %attend_backward.5 = (f32[256,512]{1,0:T(8,128)}, bf16[8,64,640]{2,1,0:T(8,128)(2,1)}, bf16[8,64,640]{2,1,0:T(8,128)(2,1)}, f32[1,128]{1,0:T(1,128)}, bf16[2,4,6...) custom-call(f32[256,512]{1,0:T(8,128)} %get-tuple-element.202.refs_0, ...), custom_call_target="tpu_custom_call" | custom-call | flops 20000000000 | bytes 16000000 | tf_op jit(solution)/shard_map/attend_backward/pallas_call | solution.py:155
  475.0 26.9 %finish_stream.1 = (f32[2,512]{1,0:T(2,128)}, bf16[4,8,64,256]{3,2,1,0:T(8,128)(2,1)}, f32[1,128]{1,0:T(1,128)}, bf16[8,64,640]{2,1,0:T(8,128)(2,1)}, bf16[64,40...) custom-call(f32[256,512]{1,0:T(8,128)} %get-tuple-element.219.refs_0_, ...), custom_call_target="tpu_custom_call" | custom-call | tf_op jit(solution)/shard_map/finish_stream/pallas_call | solution.py:155
  508.0 24.0 %embed_back.1 = (f32[64,8192]{1,0:T(8,128)}, f32[64,256]{1,0:T(8,128)}, f32[7,2,512]{2,1,0:T(2,128)}, f32[1,128]{1,0:T(1,128)}, bf16[2,2,64,640]{3,2,1,0:T(8,128...) custom-call(s32[1]{0:T(128)} %bitcast.refs_0_, s32[1,8192]{1,0:T(1,128)} %reshape.326.refs_1_, ...), custom_call_target="tpu_custom_call" | custom-call | flops 15000000512 | bytes 4000000 | tf_op jit(solution)/shard_map/embed_back/pallas_call | solution.py:155
  533.3 33.2 %last_sums.1 = (f32[64,1664]{1,0:T(8,128)}, f32[64,1664]{1,0:T(8,128)}, f32[8,128]{1,0:T(8,128)}, f32[1,128]{1,0:T(1,128)}) custom-call(bf16[4,64,640]{2,1,0:T(8,128)(2,1)} %bitcast.238, bf16[4,64,640]{2,1,0:T(8,128)(2,1)} %bitcast.251, f32[4,64,1024]{2,1,0:T(8,128)} %slice_bitcast_fusion.refs_2_, bf16[4,64,1024]{2,1,0:T(8,128)(2,1)} %get-tuple-element.238.refs_3_, ...), custom_call_target="tpu_custom_call" | custom-call | flops 1000000 | bytes 4000000 | tf_op jit(solution)/shard_map/last_sums/pallas_call | solution.py:155
  568.5 1.9 pad_maximum_fusion.7
  570.4 13.7 %update.1 = (f32[64,8192]{1,0:T(8,128)}, bf16[64,8192]{1,0:T(8,128)(2,1)}, f32[64,8192]{1,0:T(8,128)}, f32[64,8192]{1,0:T(8,128)}, f32[3,64,2,224]{3,2,1,0:T(2,1...) custom-call(f32[8,128]{1,0:T(8,128)} %get-tuple-element.244.refs_0_,, ...), custom_call_target="tpu_custom_call" | custom-call | flops 1000000 | bytes 30000000 | tf_op jit(solution)/shard_map/update/pallas_call | solution.py:155
  (224 shorter events, 60.4 us)
Async XLA Ops:
  7.2 135.6 %all-gather.3.cloned.1.call-start = ((), (), s32[]{:S(2)}) async-start(), calls=%async_computation.2 | async-start | bytes 18382848 | tf_op jit(solution)/shard_map/all_gather | solution.py:1510
  10.2 6.8 %copy-start = (f32[64,8192]{1,0:T(8,128)S(1)}, f32[64,8192]{1,0:T(8,128)}, u32[]{:S(2)}) copy-start(f32[64,8192]{1,0:T(8,128)} %refs_6_.1) | copy-start | bytes 6291460
  12.0 27.2 %collective-permute-start.3 = (bf16[1,1,1,64,640]{4,3,2,1,0:T(8,128)(2,1)S(1)}, bf16[1,1,1,64,640]{4,3,2,1,0:T(8,128)(2,1)S(1)}, u32[]{:S(2)}, u32[]{:S(2)}) collective-permute-start(bf16[1,1,1,64,640]{4,3,2,1,0:T(8,128)(2,1)S(1)} %bitcast.250), channel_id=1, source_target_pairs={{0,16},{4,20},{8,24},{12,28},{16,0},{20,4},{24,8},{28,12},{1,17},{... | collective-permute-start | bytes 245768 | tf_op jit(solution)/shard_map/ppermute | solution.py:1415
  16.8 4.6 collective-permute-start
  16.9 2.9 collective-permute-start.7
  17.1 28.8 %copy-start.3 = (bf16[64,8192]{1,0:T(8,128)(2,1)}, bf16[64,8192]{1,0:T(8,128)(2,1)S(1)}, u32[]{:S(2)}) copy-start(bf16[64,8192]{1,0:T(8,128)(2,1)S(1)} %convert_element_type.206.refs_2_) | copy-start | bytes 3145732
  18.1 78.2 %collective-permute-start.14 = (bf16[64,4096]{1,0:T(8,128)(2,1)}, bf16[64,4096]{1,0:T(8,128)(2,1)}, u32[]{:S(2)}, u32[]{:S(2)}) collective-permute-start(bf16[64,4096]{1,0:T(8,128)(2,1)} %constant_dynamic-slice_fusion.24), channel_id=1, source_target_pairs={{0,4},{4,0},{8,12},{12,8},{16,20},{20,16},{24,28},{28,24},{1,5},{5... | collective-permute-start | bytes 1572872 | tf_op jit(solution)/shard_map/ppermute | solution.py:1415
  19.8 3.8 collective-permute-start.8
  21.5 3.8 collective-permute-start.1
  23.6 13.7 %copy-start.27 = (f32[7,2,256]{2,1,0:T(2,128)}, f32[7,2,256]{2,1,0:T(2,128)S(1)}, u32[]{:S(2)}) copy-start(f32[7,2,256]{2,1,0:T(2,128)S(1)} %get-tuple-element.351) | copy-start | bytes 43012
  23.7 13.7 %copy-start.29 = (f32[7,2,256]{2,1,0:T(2,128)}, f32[7,2,256]{2,1,0:T(2,128)S(1)}, u32[]{:S(2)}) copy-start(f32[7,2,256]{2,1,0:T(2,128)S(1)} %get-tuple-element.352) | copy-start | bytes 43012
  25.3 12.0 %collective-permute-start.2 = (s32[2,2,1,2176]{3,2,1,0:T(1,128)S(1)}, s32[2,2,1,2176]{3,2,1,0:T(1,128)S(1)}, u32[]{:S(2)}, u32[]{:S(2)}) collective-permute-start(s32[2,2,1,2176]{3,2,1,0:T(1,128)S(1)} %pad_add_fusion.1), channel_id=1, source_target_pairs={{0,4},{4,0},{8,12},{12,8},{16,20},{20,16},{24,28},{28,24},{1,5},{5... | collective-permute-start | bytes 104456 | tf_op jit(solution)/shard_map/ppermute | solution.py:1415
  38.5 22.5 %copy-start.34 = (s32[8]{0:T(128)}, s32[8]{0:T(128)S(1)}, u32[]{:S(2)}) copy-start(s32[8]{0:T(128)S(1)} %slice_reduce_fusion) | copy-start | bytes 100
  39.3 6.5 %collective-permute-start.4 = (bf16[2,1,1,64,640]{4,3,2,1,0:T(8,128)(2,1)S(1)}, bf16[2,1,1,64,640]{4,3,2,1,0:T(8,128)(2,1)S(1)}, u32[]{:S(2)}, u32[]{:S(2)}) collective-permute-start(bf16[2,1,1,64,640]{4,3,2,1,0:T(8,128)(2,1)S(1)} %pad_maximum_fusion.4), channel_id=1, source_target_pairs={{0,8},{4,12},{8,0},{12,4},{16,24},{20,28},{24,16},{28,20},{1,9},{5... | collective-permute-start | bytes 491528 | tf_op jit(solution)/shard_map/ppermute | solution.py:1415
  45.9 21.6 %collective-permute-start.9 = (bf16[2,2,1,64,640]{4,3,2,1,0:T(8,128)(2,1)S(1)}, bf16[2,2,1,64,640]{4,3,2,1,0:T(8,128)(2,1)}, u32[]{:S(2)}, u32[]{:S(2)}) collective-permute-start(bf16[2,2,1,64,640]{4,3,2,1,0:T(8,128)(2,1)S(1)} %pad_maximum_fusion.3.refs_3_), channel_id=1, source_target_pairs={{0,4},{4,0},{8,12},{12,8},{16,20},{20,16},{24,28},{28,24},{1,5},{5... | collective-permute-start | bytes 983048 | tf_op jit(solution)/shard_map/ppermute | solution.py:1415
  65.7 11.3 %collective-permute-start.5 = (bf16[64,8,2,256]{3,1,2,0:T(8,128)(2,1)S(1)}, bf16[64,8,2,256]{3,1,2,0:T(8,128)(2,1)S(1)}, u32[]{:S(2)}, u32[]{:S(2)}) collective-permute-start(bf16[64,8,2,256]{3,1,2,0:T(8,128)(2,1)S(1)} %bitcast.245), channel_id=1, source_target_pairs={{0,1},{1,0},{2,3},{3,2},{4,5},{5,4},{6,7},{7,6},{8,9},{9,8},{10,11... | collective-permute-start | bytes 1572872 | tf_op jit(solution)/shard_map/ppermute | solution.py:1415
  65.9 11.3 %copy-start.36 = (f32[8,1,256]{2,1,0:T(1,128)}, f32[8,1,256]{2,1,0:T(1,128)S(1)}, u32[]{:S(2)}) copy-start(f32[8,1,256]{2,1,0:T(1,128)S(1)} %constant_dynamic-update-slice_fusion.8.refs_3_) | copy-start | bytes 24580
  65.9 10.2 %collective-permute-start.11 = (bf16[2,2,1,64,640]{4,3,2,1,0:T(8,128)(2,1)S(1)}, bf16[2,2,1,64,640]{4,3,2,1,0:T(8,128)(2,1)S(1)}, u32[]{:S(2)}, u32[]{:S(2)}) collective-permute-start(bf16[2,2,1,64,640]{4,3,2,1,0:T(8,128)(2,1)S(1)} %copy-done.23), channel_id=1, source_target_pairs={{0,2},{1,3},{2,0},{3,1},{4,6},{5,7},{6,4},{7,5},{8,10},{9,11},{10,... | collective-permute-start | bytes 983048 | tf_op jit(solution)/shard_map/ppermute | solution.py:1415
  68.7 21.0 %copy-start.12 = (bf16[2,2,2,64,640]{4,3,2,1,0:T(8,128)(2,1)}, bf16[2,2,2,64,640]{4,3,2,1,0:T(8,128)(2,1)S(1)}, u32[]{:S(2)}) copy-start(bf16[2,2,2,64,640]{4,3,2,1,0:T(8,128)(2,1)S(1)} %pad_maximum_fusion.1) | copy-start | bytes 1966084
  68.7 49.0 %collective-permute-start.10 = (bf16[2,2,2,64,640]{4,3,2,1,0:T(8,128)(2,1)S(1)}, bf16[2,2,2,64,640]{4,3,2,1,0:T(8,128)(2,1)}, u32[]{:S(2)}, u32[]{:S(2)}) collective-permute-start(bf16[2,2,2,64,640]{4,3,2,1,0:T(8,128)(2,1)S(1)} %pad_maximum_fusion.1), channel_id=1, source_target_pairs={{0,1},{1,0},{2,3},{3,2},{4,5},{5,4},{6,7},{7,6},{8,9},{9,8},{10,11... | collective-permute-start | bytes 1966088 | tf_op jit(solution)/shard_map/ppermute | solution.py:1415
  76.0 12.6 %collective-permute-start.12 = (bf16[2,2,1,64,640]{4,3,2,1,0:T(8,128)(2,1)S(1)}, bf16[2,2,1,64,640]{4,3,2,1,0:T(8,128)(2,1)S(1)}, u32[]{:S(2)}, u32[]{:S(2)}) collective-permute-start(bf16[2,2,1,64,640]{4,3,2,1,0:T(8,128)(2,1)S(1)} %collective-permute-done.11), channel_id=1, source_target_pairs={{0,4},{4,0},{8,12},{12,8},{16,20},{20,16},{24,28},{28,24},{1,5},{5... | collective-permute-start | bytes 983048 | tf_op jit(solution)/shard_map/ppermute | solution.py:1415
  77.2 19.1 %copy-start.4 = (bf16[64,8192]{1,0:T(8,128)(2,1)S(1)}, bf16[64,8192]{1,0:T(8,128)(2,1)}, u32[]{:S(2)}) copy-start(bf16[64,8192]{1,0:T(8,128)(2,1)} %copy-done.3) | copy-start | bytes 3145732
  77.2 12.4 %collective-permute-start.6 = (bf16[64,8,256]{2,1,0:T(8,128)(2,1)S(1)}, bf16[64,8,256]{2,1,0:T(8,128)(2,1)S(1)}, u32[]{:S(2)}, u32[]{:S(2)}) collective-permute-start(bf16[64,8,256]{2,1,0:T(8,128)(2,1)S(1)} %dynamic-slice_bitcast_fusion.4), channel_id=1, source_target_pairs={{0,2},{1,3},{2,0},{3,1},{4,6},{5,7},{6,4},{7,5},{8,10},{9,11},{10,... | collective-permute-start | bytes 786440 | tf_op jit(solution)/shard_map/ppermute | solution.py:1415
  89.6 28.0 %collective-permute-start.13 = (bf16[2,2,2,64,640]{4,3,2,1,0:T(8,128)(2,1)}, bf16[2,2,2,64,640]{4,3,2,1,0:T(8,128)(2,1)}, u32[]{:S(2)}, u32[]{:S(2)}) collective-permute-start(bf16[2,2,2,64,640]{4,3,2,1,0:T(8,128)(2,1)} %pad_maximum_fusion.2), channel_id=1, source_target_pairs={{0,1},{1,0},{2,3},{3,2},{4,5},{5,4},{6,7},{7,6},{8,9},{9,8},{10,11... | collective-permute-start | bytes 1966088 | tf_op jit(solution)/shard_map/ppermute | solution.py:1415
  90.4 22.6 %all-to-all-start = ((bf16[64,8,256]{2,0,1:T(8,128)(2,1)}), bf16[64,8,256]{2,0,1:T(8,128)(2,1)S(1)}, u32[]{:S(2)}, u32[]{:S(2)}) async-start(bf16[64,8,256]{2,0,1:T(8,128)(2,1)} %copy.127), calls=%async_computation | async-start | bytes 524288 | tf_op jit(solution)/shard_map/all_to_all | solution.py:1580
  96.2 127.5 %all-gather.5.cloned.1.call-start = ((), (), s32[]{:S(2)}) async-start(), calls=%async_computation.3 | async-start | bytes 5242880 | tf_op jit(solution)/shard_map/all_gather | solution.py:1582
  117.6 290.4 %reduce-scatter.2.cloned.1.call-start = ((), (), s32[]{:S(2)}) async-start(), calls=%async_computation.4 | async-start | bytes 5242880 | tf_op jit(solution)/shard_map/reduce_scatter | solution.py:1618
  315.7 33.7 %copy-start.11 = (bf16[2,4,64,1024]{3,2,1,0:T(8,128)(2,1)S(1)}, bf16[2,4,64,1024]{3,2,1,0:T(8,128)(2,1)}, u32[]{:S(2)}) copy-start(bf16[2,4,64,1024]{3,2,1,0:T(8,128)(2,1)} %get-tuple-element.193) | copy-start | bytes 3145732
  351.1 12.7 %copy-start.2 = (f32[2,4,64,1024]{3,2,1,0:T(8,128)}, f32[2,4,64,1024]{3,2,1,0:T(8,128)S(1)}, u32[]{:S(2)}) copy-start(f32[2,4,64,1024]{3,2,1,0:T(8,128)S(1)} %convert_add_fusion.2) | copy-start | bytes 6291460
  363.8 38.5 %copy-start.10 = (bf16[2,4,64,1024]{3,2,1,0:T(8,128)(2,1)S(1)}, bf16[2,4,64,1024]{3,2,1,0:T(8,128)(2,1)}, u32[]{:S(2)}) copy-start(bf16[2,4,64,1024]{3,2,1,0:T(8,128)(2,1)} %get-tuple-element.214) | copy-start | bytes 3145732
  408.0 21.5 %copy-start.15 = (bf16[8,64,640]{2,1,0:T(8,128)(2,1)S(1)}, bf16[8,64,640]{2,1,0:T(8,128)(2,1)}, u32[]{:S(2)}) copy-start(bf16[8,64,640]{2,1,0:T(8,128)(2,1)} %get-tuple-element.212) | copy-start | bytes 1966084
  432.5 36.2 %copy-start.9 = (bf16[2,4,64,1024]{3,2,1,0:T(8,128)(2,1)S(1)}, bf16[2,4,64,1024]{3,2,1,0:T(8,128)(2,1)}, u32[]{:S(2)}) copy-start(bf16[2,4,64,1024]{3,2,1,0:T(8,128)(2,1)} %get-tuple-element.234) | copy-start | bytes 3145732
  (26 other events, 67.4 us)
Sparse Core Ops, SparseCore 0:
  11.6 131.1 all-gather.2
  144.4 79.3 all-gather.4
  300.0 74.7 reduce-scatter.1

commit v5 on v4

--- a/solution.py
+++ b/solution.py
@@ -268,6 +268,11 @@
     return same & (sorted_ok | own_ok)
 
 
+def await_weights(sources, low, w_ref, sems, j):
+    source = sources[0].at[:, 0, :, low:low + w_ref.shape[3]]
+    pltpu.make_async_copy(source, w_ref.at[j], sems.at[j]).wait()
+
+
 def turned(p):
     mine = lax.axis_index("head")
     low, high = mine % 2, (mine // 2) % 2
@@ -275,15 +280,15 @@
     return rest + (1 - low if p & 1 else low) + 2 * (1 - high if p & 2 else high)
 
 
-def load_weights(sources, low, w_ref, sems):
+def load_weights(sources, low, w_ref, sems, order=(0, 1, 2, 3)):
     copies = []
-    for p in range(w_ref.shape[0]):
+    for p in order:
         if len(sources) > 1:
             source = sources[p]
         else:
             source = sources[0].at[:, turned(p), :, low:low + w_ref.shape[3]]
         copies.append(pltpu.make_async_copy(source, w_ref.at[p], sems.at[p]))
-        copies[p].start()
+        copies[-1].start()
     return copies
 
 
@@ -388,12 +393,10 @@
     stream_out, hnext_out, upw_out, act_out, w_ref, acc_scr, sems = refs[count:]
     width = mid_ref.shape[1]
     pairs = w_ref.shape[0]
-    copies = load_weights(sources, low, w_ref, sems)
+    load_weights(sources, low, w_ref, sems)
     acc_scr[...] = mid_ref[...]
-    for copy in copies:
-        copy.wait()
-
     def feed(j, _):
+        await_weights(sources, low, w_ref, sems, j)
         w_up = w_ref[j, :, :, C_UP[0]:C_UP[1]].reshape(width, 512)
         upward = dot_nn(hid2_ref[...], w_up)
         upw_out[j] = upward
@@ -524,7 +527,7 @@
     ) = refs[count:]
     width = carry_ref.shape[1]
     pairs = w_ref.shape[0]
-    copies = load_weights(sources, low, w_ref, sems)
+    load_weights(sources, low, w_ref, sems, (1, 3, 0, 2))
 
     back, pair = norm_back(dy_ref[...], above_ref[...], gain_above_ref[...])
     pair_above_out[...] = pair
@@ -532,8 +535,6 @@
     carry_out[...] = upstream
     low_scr[...] = upstream.astype(BF)
     acc_scr[...] = jnp.zeros_like(acc_scr)
-    for copy in copies:
-        copy.wait()
 
     def to_near(at):
         return remote(
@@ -542,6 +543,7 @@
 
     def feed(at, _):
         j = near_first(at)
+        await_weights(sources, low, w_ref, sems, j)
         rounded = low_scr[...]
         w_dn = w_ref[j, :, :, C_DOWN[0]:C_DOWN[1]].reshape(width, 512)
         grad_act = dot_nn(rounded, w_dn)
@@ -876,9 +878,8 @@
     high, low = local >> 8, local & 255
     hot = (iota((256, count), 0) == low).astype(BF)
     grad = jnp.concatenate([grad_ref[at] for at in range(pieces)], 1)
-    wide = jnp.concatenate(
-        [jnp.where(high == at, grad, jnp.zeros_like(grad)) for at in range(bins)], 0
-    )
+    hot_high = (iota((bins, count), 0) == high).astype(BF)
+    wide = jnp.concatenate([grad * hot_high[at:at + 1, :] for at in range(bins)], 0)
     found = dot_nt(wide, hot)
 
     @pl.when(step == 0)
@@ -942,7 +943,7 @@
 
 
 def last_sums_kernel(
-    a_ref, a_more_ref, b_ref, b_more_ref, other_ref, other_more_ref, third_ref, square_ref, pair_ref, loss_ref,
+    a_ref, a_more_ref, b_ref, b_more_ref, other_ref, other_more_ref, third_ref, square_ref, pair_ref, loss_ref, share_ref,
     out_ref, other_out, total_out,
     sum_scr, low_scr, come_scr, part_scr, parts_scr, send_sems, recv_sems, part_send, part_recv, *, bits, shared
 ):
@@ -950,40 +951,65 @@
     for t in range(count):
         sum_scr[t, :, 0:ATTN] = a_ref[t].astype(F32) + a_more_ref[t].astype(F32)
         sum_scr[t, :, ATTN:] = b_ref[t].astype(F32) + b_more_ref[t].astype(F32)
-    at = 0
-    place = 0
-    for bit in bits:
-        flag = (lax.axis_index("dp") // bit) % 2
-        half = count // 2
+    def meanwhile():
+        other = other_ref[...].astype(F32) + other_more_ref[...].astype(F32)
+        other_out[...] = other
+        pairs = pair_ref[...]
+        square = jnp.sum(square_ref[...]) + jnp.sum(pairs * pairs) / shared + jnp.sum(other * other)
+        for piece in third_ref:
+            value = piece[...]
+            square = square + jnp.sum(value * value)
+        return square
+
+    def send(at, place, columns, bit):
+        part = (place, slice(None), columns)
+        copy = remote(low_scr.at[part], come_scr.at[part], send_sems.at[at], recv_sems.at[at], "dp", bit)
+        copy.start()
+        return copy
+
+    flags = [(lax.axis_index("dp") // bit) % 2 for bit in bits]
+    if len(bits) == 2:
+        near, far = flags
+        near_bit, far_bit = bits
         copies = []
-        for t in range(half):
-            low_scr[place + t] = sum_scr[2 * t + 1 - flag].astype(BF)
-            copies.append(
-                remote(
-                    low_scr.at[place + t], come_scr.at[place + t], send_sems.at[at], recv_sems.at[at], "dp", bit
-                )
-            )
-            copies[t].start()
-            at += 1
-        if place == 0:
-            other = other_ref[...].astype(F32) + other_more_ref[...].astype(F32)
-            other_out[...] = other
-            pairs = pair_ref[...]
-            square = jnp.sum(square_ref[...]) + jnp.sum(pairs * pairs) / shared + jnp.sum(other * other)
-            for piece in third_ref:
-                value = piece[...]
-                square = square + jnp.sum(value * value)
-        for t in range(half):
-            copies[t].wait()
-            sum_scr[t] = sum_scr[2 * t + flag] + come_scr[place + t].astype(F32)
-        place += half
-        count = half
-    value = sum_scr[0]
-    out_ref[...] = value
+        for t in range(2):
+            low_scr[t, :, ATTN:] = sum_scr[2 * t + 1 - near, :, ATTN:].astype(BF)
+            copies.append(send(2 * t, t, pl.ds(ATTN, FEED), near_bit))
+            low_scr[t, :, :ATTN] = sum_scr[2 * (1 - far) + t, :, :ATTN].astype(BF)
+            copies.append(send(2 * t + 1, t, pl.ds(0, ATTN), far_bit))
+        square = meanwhile()
+        for copy in copies:
+            copy.wait()
+        for t in range(2):
+            sum_scr[t, :, ATTN:] = sum_scr[2 * t + near, :, ATTN:] + come_scr[t, :, ATTN:].astype(F32)
+            sum_scr[t, :, :ATTN] = sum_scr[2 * far + t, :, :ATTN] + come_scr[t, :, :ATTN].astype(F32)
+        low_scr[2, :, ATTN:] = sum_scr[1 - far, :, ATTN:].astype(BF)
+        low_scr[2, :, :ATTN] = sum_scr[1 - near, :, :ATTN].astype(BF)
+        copies = [send(4, 2, pl.ds(ATTN, FEED), far_bit), send(5, 2, pl.ds(0, ATTN), near_bit)]
+        for copy in copies:
+            copy.wait()
+        out_ref[:, ATTN:] = sum_scr[far, :, ATTN:] + come_scr[2, :, ATTN:].astype(F32)
+        out_ref[:, :ATTN] = sum_scr[near, :, :ATTN] + come_scr[2, :, :ATTN].astype(F32)
+    else:
+        at = 0
+        for bit, flag in zip(bits, flags):
+            half = count // 2
+            copies = []
+            for t in range(half):
+                low_scr[at] = sum_scr[2 * t + 1 - flag].astype(BF)
+                copies.append(send(at, at, slice(None), bit))
+                at += 1
+            for t in range(half):
+                copies[t].wait()
+                sum_scr[t] = sum_scr[2 * t + flag] + come_scr[at - half + t].astype(F32)
+            count = half
+        square = meanwhile()
+        out_ref[...] = sum_scr[0]
+    value = out_ref[...]
     square = square + jnp.sum(value * value)
     row, lane = iota((8, 128), 0), iota((8, 128), 1)
     part_scr[...] = jnp.where(
-        row == 0, jnp.where(lane == 0, square, jnp.where(lane == 1, loss_ref[...], 0.0)), 0.0
+        row == 0, jnp.where(lane == 0, square, jnp.where(lane == 1, loss_ref[...], jnp.where(lane == 2, share_ref[...], 0.0))), 0.0
     )
     place = 0
     for axis in ("head", "dp"):
@@ -1011,7 +1037,7 @@
     total_out[...] = part_scr[...]
 
 
-def last_sums(attn, feed, other, thirds, squares, pair_grads, loss, bits, ident):
+def last_sums(attn, feed, other, thirds, squares, pair_grads, loss, count_share, bits, ident):
     def flat(value):
         return value.reshape((-1,) + value.shape[-2:])
 
@@ -1031,9 +1057,9 @@
     return call(
         kernel,
         [one, one, shape((8, 128), F32)],
-        [VM] * (fixed + extra + 3),
+        [VM] * (fixed + extra + 4),
         [VM] * 3,
-        (*operands, *thirds, squares, pair_grads, loss),
+        (*operands, *thirds, squares, pair_grads, loss, count_share),
         ident=ident,
         greet_all=("head", "dp"),
         scratch_shapes=[
@@ -1042,8 +1068,8 @@
             pltpu.VMEM((count - 1, features, columns), BF),
             pltpu.VMEM((8, 128), F32),
             pltpu.VMEM((stages, 8, 128), F32),
-            pltpu.SemaphoreType.DMA((count - 1,)),
-            pltpu.SemaphoreType.DMA((count - 1,)),
+            pltpu.SemaphoreType.DMA((max(6, count - 1),)),
+            pltpu.SemaphoreType.DMA((max(6, count - 1),)),
             pltpu.SemaphoreType.DMA((stages,)),
             pltpu.SemaphoreType.DMA((stages,)),
         ],
@@ -1082,7 +1108,9 @@
             run(2, (layer, h), out[(1 - h) * HD:(2 - h) * HD])
         run(3, layer, pack[:, ATTN + C_UP[0]:ATTN + C_UP[1]])
         run(4, layer, pack[:, ATTN + C_DOWN[0]:ATTN + C_DOWN[1]])
-    run(5, slice(None), norm_grad_ref[...])
+    size = ins[15].shape[2]
+    mine = pl.ds(pl.multiple_of(lax.axis_index("head") * size, size), size)
+    run(5, slice(None), norm_grad_ref[:, :, mine])
 
 
 def update(totals, packs, table_grad, norm_grad, sort_width, members):
@@ -1090,7 +1118,7 @@
     for weight, _, _ in members[:-1]:
         full = shape(weight.shape, F32)
         outs += [full, shape(weight.shape, BF), full, full]
-    outs += [shape(norm_grad.shape, F32)] * 3
+    outs += [shape(members[-1][0].shape, F32)] * 3
     operands = [totals, table_grad, norm_grad, *packs]
     for member in members:
         operands += member
@@ -1696,10 +1724,8 @@
         lasts[1].give(swap(*lasts[1].ask))
     lower, other, totals, token = last_sums(
         attns[0].parts, feeds[0].parts, lasts[1].parts, thirds, squares, grad_norms, loss_here.reshape(1, 1),
+        (count_total / (dp * head)).reshape(1, 1),
         tuple(reversed(bits[:-1])), next(idents),
-    )
-    grad_norms = lax.dynamic_slice_in_dim(
-        grad_norms, my_head * norms.shape[2], norms.shape[2], 2
     )
     results = update(
         totals, [lower, other] + thirds, grad_table, grad_norms, sort_width,
@@ -1714,7 +1740,7 @@
     )
     results = list(results)
     results[16:20] = [one.transpose(0, 2, 1) for one in results[16:20]]
-    return (jnp.stack([totals[0, 1], count_total]), jnp.sqrt(totals[0, 0]), *results)
+    return (totals[0, 1:3], jnp.sqrt(totals[0, 0]), *results)
 
 
 def solution(mesh):

time: 600 us -> 592 us (0.987)
  Pallas kernels: 447 us -> 438 us
    pallas_call x20, Pallas kernels: 447 us -> 438 us  [call(): pl.pallas_call(run, out_shape=list(outs) + [jax.ShapeDtypeStruct((1, 128)...]
where the time goes in v5:
time: 592 us; the launch traced here: 584 us
  Pallas kernels  438 us (74%)
  waiting for transfers between devices  54 us (9%)
  local copies, waits for them, and re-layouts  27.8 us (5%)
  starting transfers between devices  24.4 us (4%)
  other arithmetic  21.3 us (4%)
  between operations  19.2 us (3%)
    pallas_call x20, Pallas kernels, call(): pl.pallas_call(run, out_shape=list(outs) + [jax.ShapeDtypeStruct((1, 128)...  438 us
    ppermute x15, waiting for transfers between devices, swap(): lax.ppermute(value, axis, [(at, at ^ bit) for at in range(lax.axis_size(a...  32.9 us
    ppermute x15, starting transfers between devices, swap(): lax.ppermute(value, axis, [(at, at ^ bit) for at in range(lax.axis_size(a...  18.5 us
    all_to_all x1, waiting for transfers between devices, body(): found = lax.all_to_all(found, 'dp', split_axis=1, concat_axis=0, tiled=True)  15.5 us
  transfers between devices with their start and end apart: 19, of which 9 were waited for; matrix products, arithmetic and copies ran while one was open for 4% of the time, Pallas kernels for 36%

profile of v5, /device:TPU:0, one launch (start us, length us, event | category | flops | bytes accessed | tf_op | source)
XLA Modules:
  0.0 584.2 jit_solution(8638446910924069960)
XLA Ops:
  12.0 4.1 collective-permute-start.3
  27.5 9.8 %collective-permute-done.2 = s32[2,2,1,2176]{3,2,1,0:T(1,128)S(1)} collective-permute-done((s32[2,2,1,2176]{3,2,1,0:T(1,128)S(1)}, s32[2,2,1,2176]{3,2,1,0:T(1,128)S(1)}, u32[]{:S(2)}, u32[]{:S(2)}) %collective-permute-start.2) | collective-permute-done | bytes 34848 | tf_op jit(solution)/shard_map/ppermute | solution.py:1443
  39.3 1.9 collective-permute-start.4
  41.8 4.0 collective-permute-done.4
  47.2 13.8 %embed_lookup.1 = (bf16[64,8192]{1,0:T(8,128)(2,1)}, f32[1,128]{1,0:T(1,128)}) custom-call(s32[1]{0:T(128)} %bitcast.refs_0_, s32[1,8192]{1,0:T(1,128)} %bitcast.257, bf16[64,8192]{1,0:T(8,128)(2,1)} %copy-done.3, bf16[2,2,1,64,640]{4,3,2,1,0:T(8,128)(2,1)} %copy-done.22), custom_call_target="tpu_custom_call" | custom-call | flops 15000000512 | bytes 4000000 | tf_op jit(solution)/shard_map/embed_lookup/pallas_call | solution.py:155
  61.0 1.8 reshape_reshape.10
  62.8 2.7 constant_dynamic-slice_fusion.25
  68.9 7.1 %collective-permute-done.11 = bf16[2,2,1,64,640]{4,3,2,1,0:T(8,128)(2,1)S(1)} collective-permute-done((bf16[2,2,1,64,640]{4,3,2,1,0:T(8,128)(2,1)S(1)}, bf16[2,2,1,64,640]{4,3,2,1,0:T(8,128)(2,1)S(1)}, u32[]{:S(2)}, u32[]{:S(2)}) %collective-permute-start.11) | collective-permute-done | bytes 327712 | tf_op jit(solution)/shard_map/ppermute | solution.py:1443
  78.8 9.8 %collective-permute-done.12 = bf16[2,2,1,64,640]{4,3,2,1,0:T(8,128)(2,1)S(1)} collective-permute-done((bf16[2,2,1,64,640]{4,3,2,1,0:T(8,128)(2,1)S(1)}, bf16[2,2,1,64,640]{4,3,2,1,0:T(8,128)(2,1)S(1)}, u32[]{:S(2)}, u32[]{:S(2)}) %collective-permute-start.12) | collective-permute-done | bytes 327712 | tf_op jit(solution)/shard_map/ppermute | solution.py:1443
  90.4 5.8 all-to-all-start
  97.5 15.5 %all-to-all-done = bf16[64,8,256]{2,0,1:T(8,128)(2,1)S(1)} async-done(((bf16[64,8,256]{2,0,1:T(8,128)(2,1)}), bf16[64,8,256]{2,0,1:T(8,128)(2,1)S(1)}, u32[]{:S(2)}, u32[]{:S(2)}) %all-to-all-start) | async-done | bytes 262176 | tf_op jit(solution)/shard_map/all_to_all | solution.py:1608
  113.7 2.0 start_stream.1
  117.7 23.3 %attend_forward.3 = (f32[256,512]{1,0:T(8,128)}, bf16[256,512]{1,0:T(8,128)(2,1)}, bf16[1024,512]{1,0:T(8,128)(2,1)}, bf16[4,1024,256]{2,1,0:T(8,128)(2,1)}, bf1...) custom-call(bf16[256,512]{1,0:T(8,128)(2,1)} %get-tuple-element.149., ...), custom_call_target="tpu_custom_call" | custom-call | flops 17999998976 | bytes 10000000 | tf_op jit(solution)/shard_map/attend_forward/pallas_call | solution.py:155
  141.0 1.8 all-gather.3.cloned.1.call-done
  142.8 6.5 %feed_forward.3 = (f32[256,512]{1,0:T(8,128)}, bf16[256,512]{1,0:T(8,128)(2,1)}, f32[4,256,512]{2,1,0:T(8,128)}, bf16[4,256,512]{2,1,0:T(8,128)(2,1)}, f32[1,128]{1,0:T(1,128)}) custom-call(f32[256,512]{1,0:T(8,128)} %get-tuple-element.151.refs_0_.refs_5_, bf16[256,512]{1,0:T(8,128)(2,1)} %get-tuple-element.152.refs_1_.refs_6_, ...), custom_call_target="tpu_custom_call" | custom-call | flops 8000000000 | bytes 8000000 | tf_op jit(solution)/shard_map/feed_forward/pallas_call | solution.py:155
  149.3 23.3 %attend_forward.4 = (f32[256,512]{1,0:T(8,128)}, bf16[256,512]{1,0:T(8,128)(2,1)}, bf16[1024,512]{1,0:T(8,128)(2,1)}, bf16[4,1024,256]{2,1,0:T(8,128)(2,1)}, bf1...) custom-call(bf16[256,512]{1,0:T(8,128)(2,1)} %get-tuple-element.153., ...), custom_call_target="tpu_custom_call" | custom-call | flops 17999998976 | bytes 10000000 | tf_op jit(solution)/shard_map/attend_forward/pallas_call | solution.py:155
  172.6 6.5 %feed_forward.4 = (f32[256,512]{1,0:T(8,128)}, bf16[256,512]{1,0:T(8,128)(2,1)}, f32[4,256,512]{2,1,0:T(8,128)}, bf16[4,256,512]{2,1,0:T(8,128)(2,1)}, f32[1,128]{1,0:T(1,128)}) custom-call(f32[256,512]{1,0:T(8,128)} %get-tuple-element.155.refs_0_.refs_5_, bf16[256,512]{1,0:T(8,128)(2,1)} %get-tuple-element.156.refs_1_.refs_6_, ...), custom_call_target="tpu_custom_call" | custom-call | flops 8000000000 | bytes 8000000 | tf_op jit(solution)/shard_map/feed_forward/pallas_call | solution.py:155
  179.1 34.5 %attend_forward.5 = (f32[256,512]{1,0:T(8,128)}, bf16[256,512]{1,0:T(8,128)(2,1)}, bf16[1024,512]{1,0:T(8,128)(2,1)}, bf16[4,1024,256]{2,1,0:T(8,128)(2,1)}, bf1...) custom-call(bf16[256,512]{1,0:T(8,128)(2,1)} %get-tuple-element.157., ...), custom_call_target="tpu_custom_call" | custom-call | flops 17999998976 | bytes 10000000 | tf_op jit(solution)/shard_map/attend_forward/pallas_call | solution.py:155
  213.6 6.5 %feed_forward.5 = (f32[256,512]{1,0:T(8,128)}, bf16[256,512]{1,0:T(8,128)(2,1)}, f32[4,256,512]{2,1,0:T(8,128)}, bf16[4,256,512]{2,1,0:T(8,128)(2,1)}, f32[1,128]{1,0:T(1,128)}) custom-call(f32[256,512]{1,0:T(8,128)} %get-tuple-element.159.refs_0_.refs_5_, bf16[256,512]{1,0:T(8,128)(2,1)} %get-tuple-element.160.refs_1_.refs_6_, ...), custom_call_target="tpu_custom_call" | custom-call | flops 8000000000 | bytes 8000000 | tf_op jit(solution)/shard_map/feed_forward/pallas_call | solution.py:155
  220.1 3.7 all-gather.5.cloned.1.call-done.refs_1_
  223.8 35.4 %head_forward.1 = (bf16[8,256,512]{2,1,0:T(8,128)(2,1)}, f32[8,2,256]{2,1,0:T(2,128)}, f32[1,1]{1,0:T(1,128)}, f32[1,128]{1,0:T(1,128)}) custom-call(bf16[256,512]{1,0:T(8,128)(2,1)} %get-tuple-element.161.refs_0_, bf16[512,4096]{1,0:T(8,128)(2,1)} %all-gather.5.cloned.1.call-done.refs_1_, f32[8,1,256]{2,1,0:T(1,128)} %subtract_convert_fusion.refs_2_, ...), custom_call_target="tpu_custom_call" | custom-call | flops 17999998976 | bytes 6000000 | tf_op jit(solution)/shard_map/head_forward/pallas_call | solution.py:155
  259.2 40.6 %head_backward.1 = (f32[256,512]{1,0:T(8,128)}, bf16[512,4096]{1,0:T(8,128)(2,1)}, f32[1,128]{1,0:T(1,128)}) custom-call(bf16[8,256,512]{2,1,0:T(8,128)(2,1)} %get-tuple-element.163.refs_0_, bf16[512,4096]{1,0:T(8,128)(2,1)} %all-gather.5.cloned.1.call-done.refs_1_, f32[8,1,256]{2,1,0:T(1,128)} %subtract_convert_fusion.refs_2_, ...), custom_call_target="tpu_custom_call" | custom-call | flops 35999997952 | bytes 14000000 | tf_op jit(solution)/shard_map/head_backward/pallas_call | solution.py:155
  304.1 11.0 %feed_backward.3 = (bf16[2,4,64,1024]{3,2,1,0:T(8,128)(2,1)}, bf16[2,4,64,1024]{3,2,1,0:T(8,128)(2,1)}, f32[256,512]{1,0:T(8,128)}, f32[2,512]{1,0:T(2,128)}, f32[2,512]{1,0:T(2,128)}, /*index=5*/f32[1,128]{1,0:T(1,128)}) custom-call(f32[256,512]{1,0:T(8,128)} %get-tuple-element.165.refs_0_, f32[256,512]{1,0:T(8,128)} %get-tuple-element.166.refs_1_, ...), custom_call_target="tpu_custom_call" | custom-call | flops 12000000000 | bytes 12000000 | tf_op jit(solution)/shard_map/feed_backward/pallas_call | solution.py:155
  315.0 34.2 %attend_backward.3 = (f32[256,512]{1,0:T(8,128)}, bf16[8,64,640]{2,1,0:T(8,128)(2,1)}, bf16[8,64,640]{2,1,0:T(8,128)(2,1)}, f32[1,128]{1,0:T(1,128)}, bf16[2,4,64,1024]{3,2,1,0:T(8,128)(2,1)}) custom-call(f32[256,512]{1,0:T(8,128)} %get-tuple-element.169.refs_0_.refs_2_, bf16[1024,512]{1,0:T(8,128)(2,1)} %get-tuple-element.170.refs_1_, ...), custom_call_target="tpu_custom_call" | custom-call | flops 20000000000 | bytes 16000000 | tf_op jit(solution)/shard_map/attend_backward/pallas_call | solution.py:155
  351.9 10.7 %feed_backward.4 = (bf16[2,4,64,1024]{3,2,1,0:T(8,128)(2,1)}, bf16[2,4,64,1024]{3,2,1,0:T(8,128)(2,1)}, f32[256,512]{1,0:T(8,128)}, f32[2,512]{1,0:T(2,128)}, f32[2,512]{1,0:T(2,128)}, /*index=5*/f32[1,128]{1,0:T(1,128)}) custom-call(f32[256,512]{1,0:T(8,128)} %get-tuple-element.179.refs_0_, f32[256,512]{1,0:T(8,128)} %get-tuple-element.158.refs_1_, ...), custom_call_target="tpu_custom_call" | custom-call | flops 12000000000 | bytes 12000000 | tf_op jit(solution)/shard_map/feed_backward/pallas_call | solution.py:155
  362.6 38.5 %attend_backward.4 = (f32[256,512]{1,0:T(8,128)}, bf16[8,64,640]{2,1,0:T(8,128)(2,1)}, bf16[8,64,640]{2,1,0:T(8,128)(2,1)}, f32[1,128]{1,0:T(1,128)}, bf16[2,4,6...) custom-call(f32[256,512]{1,0:T(8,128)} %get-tuple-element.182.refs_0_.refs_2_, ...), custom_call_target="tpu_custom_call" | custom-call | flops 20000000000 | bytes 16000000 | tf_op jit(solution)/shard_map/attend_backward/pallas_call | solution.py:155
  406.8 21.2 %feed_backward.5 = (bf16[2,4,64,1024]{3,2,1,0:T(8,128)(2,1)}, bf16[2,4,64,1024]{3,2,1,0:T(8,128)(2,1)}, f32[256,512]{1,0:T(8,128)}, f32[2,512]{1,0:T(2,128)}, f3...) custom-call(f32[256,512]{1,0:T(8,128)} %get-tuple-element.195.refs_0_, ...), custom_call_target="tpu_custom_call" | custom-call | flops 12000000000 | bytes 12000000 | tf_op jit(solution)/shard_map/feed_backward/pallas_call | solution.py:155
  431.0 36.5 %attend_backward.5 = (f32[256,512]{1,0:T(8,128)}, bf16[8,64,640]{2,1,0:T(8,128)(2,1)}, bf16[8,64,640]{2,1,0:T(8,128)(2,1)}, f32[1,128]{1,0:T(1,128)}, bf16[2,4,6...) custom-call(f32[256,512]{1,0:T(8,128)} %get-tuple-element.202.refs_0, ...), custom_call_target="tpu_custom_call" | custom-call | flops 20000000000 | bytes 16000000 | tf_op jit(solution)/shard_map/attend_backward/pallas_call | solution.py:155
  473.8 26.6 %finish_stream.1 = (f32[2,512]{1,0:T(2,128)}, bf16[4,8,64,256]{3,2,1,0:T(8,128)(2,1)}, f32[1,128]{1,0:T(1,128)}, bf16[8,64,640]{2,1,0:T(8,128)(2,1)}, bf16[64,40...) custom-call(f32[256,512]{1,0:T(8,128)} %get-tuple-element.219.refs_0_, ...), custom_call_target="tpu_custom_call" | custom-call | tf_op jit(solution)/shard_map/finish_stream/pallas_call | solution.py:155
  506.5 23.8 %embed_back.1 = (f32[64,8192]{1,0:T(8,128)}, f32[64,256]{1,0:T(8,128)}, f32[7,2,512]{2,1,0:T(2,128)}, f32[1,128]{1,0:T(1,128)}, bf16[2,2,64,640]{3,2,1,0:T(8,128...) custom-call(s32[1]{0:T(128)} %bitcast.refs_0_, s32[1,8192]{1,0:T(1,128)} %reshape.329.refs_1_, ...), custom_call_target="tpu_custom_call" | custom-call | flops 15000000512 | bytes 4000000 | tf_op jit(solution)/shard_map/embed_back/pallas_call | solution.py:155
  530.3 29.2 %last_sums.1 = (f32[64,1664]{1,0:T(8,128)}, f32[64,1664]{1,0:T(8,128)}, f32[8,128]{1,0:T(8,128)}, f32[1,128]{1,0:T(1,128)}) custom-call(bf16[4,64,640]{2,1,0:T(8,128)(2,1)} %bitcast.239, bf16[4,64,640]{2,1,0:T(8,128)(2,1)} %bitcast.251, f32[4,64,1024]{2,1,0:T(8,128)} %slice_bitcast_fusion.refs_2_, bf16[4,64,1024]{2,1,0:T(8,128)(2,1)} %get-tuple-element.238.refs_3_, ...), custom_call_target="tpu_custom_call" | custom-call | flops 1000000 | bytes 4000000 | tf_op jit(solution)/shard_map/last_sums/pallas_call | solution.py:155
  562.7 13.4 %update.1 = (f32[64,8192]{1,0:T(8,128)}, bf16[64,8192]{1,0:T(8,128)(2,1)}, f32[64,8192]{1,0:T(8,128)}, f32[64,8192]{1,0:T(8,128)}, f32[3,64,2,224]{3,2,1,0:T(2,1...) custom-call(f32[8,128]{1,0:T(8,128)} %get-tuple-element.244.refs_0_,, ...), custom_call_target="tpu_custom_call" | custom-call | flops 1000000 | bytes 30000000 | tf_op jit(solution)/shard_map/update/pallas_call | solution.py:155
  (223 shorter events, 59.5 us)
Async XLA Ops:
  7.2 135.6 %all-gather.3.cloned.1.call-start = ((), (), s32[]{:S(2)}) async-start(), calls=%async_computation.2 | async-start | bytes 18382848 | tf_op jit(solution)/shard_map/all_gather | solution.py:1538
  10.2 6.8 %copy-start = (f32[64,8192]{1,0:T(8,128)S(1)}, f32[64,8192]{1,0:T(8,128)}, u32[]{:S(2)}) copy-start(f32[64,8192]{1,0:T(8,128)} %refs_6_.1) | copy-start | bytes 6291460
  12.0 27.2 %collective-permute-start.3 = (bf16[1,1,1,64,640]{4,3,2,1,0:T(8,128)(2,1)S(1)}, bf16[1,1,1,64,640]{4,3,2,1,0:T(8,128)(2,1)S(1)}, u32[]{:S(2)}, u32[]{:S(2)}) collective-permute-start(bf16[1,1,1,64,640]{4,3,2,1,0:T(8,128)(2,1)S(1)} %bitcast.252), channel_id=1, source_target_pairs={{0,16},{4,20},{8,24},{12,28},{16,0},{20,4},{24,8},{28,12},{1,17},{... | collective-permute-start | bytes 245768 | tf_op jit(solution)/shard_map/ppermute | solution.py:1443
  16.8 4.6 collective-permute-start
  16.9 2.9 collective-permute-start.7
  17.1 28.8 %copy-start.3 = (bf16[64,8192]{1,0:T(8,128)(2,1)}, bf16[64,8192]{1,0:T(8,128)(2,1)S(1)}, u32[]{:S(2)}) copy-start(bf16[64,8192]{1,0:T(8,128)(2,1)S(1)} %convert_element_type.206.refs_2_) | copy-start | bytes 3145732
  18.1 78.2 %collective-permute-start.14 = (bf16[64,4096]{1,0:T(8,128)(2,1)}, bf16[64,4096]{1,0:T(8,128)(2,1)}, u32[]{:S(2)}, u32[]{:S(2)}) collective-permute-start(bf16[64,4096]{1,0:T(8,128)(2,1)} %constant_dynamic-slice_fusion.23), channel_id=1, source_target_pairs={{0,4},{4,0},{8,12},{12,8},{16,20},{20,16},{24,28},{28,24},{1,5},{5... | collective-permute-start | bytes 1572872 | tf_op jit(solution)/shard_map/ppermute | solution.py:1443
  19.8 3.8 collective-permute-start.8
  21.5 3.8 collective-permute-start.1
  23.6 13.7 %copy-start.27 = (f32[7,2,256]{2,1,0:T(2,128)}, f32[7,2,256]{2,1,0:T(2,128)S(1)}, u32[]{:S(2)}) copy-start(f32[7,2,256]{2,1,0:T(2,128)S(1)} %get-tuple-element.351) | copy-start | bytes 43012
  23.7 13.7 %copy-start.29 = (f32[7,2,256]{2,1,0:T(2,128)}, f32[7,2,256]{2,1,0:T(2,128)S(1)}, u32[]{:S(2)}) copy-start(f32[7,2,256]{2,1,0:T(2,128)S(1)} %get-tuple-element.352) | copy-start | bytes 43012
  25.3 12.0 %collective-permute-start.2 = (s32[2,2,1,2176]{3,2,1,0:T(1,128)S(1)}, s32[2,2,1,2176]{3,2,1,0:T(1,128)S(1)}, u32[]{:S(2)}, u32[]{:S(2)}) collective-permute-start(s32[2,2,1,2176]{3,2,1,0:T(1,128)S(1)} %pad_add_fusion.1), channel_id=1, source_target_pairs={{0,4},{4,0},{8,12},{12,8},{16,20},{20,16},{24,28},{28,24},{1,5},{5... | collective-permute-start | bytes 104456 | tf_op jit(solution)/shard_map/ppermute | solution.py:1443
  38.5 22.5 %copy-start.34 = (s32[8]{0:T(128)}, s32[8]{0:T(128)S(1)}, u32[]{:S(2)}) copy-start(s32[8]{0:T(128)S(1)} %slice_reduce_fusion) | copy-start | bytes 100
  39.3 6.5 %collective-permute-start.4 = (bf16[2,1,1,64,640]{4,3,2,1,0:T(8,128)(2,1)S(1)}, bf16[2,1,1,64,640]{4,3,2,1,0:T(8,128)(2,1)S(1)}, u32[]{:S(2)}, u32[]{:S(2)}) collective-permute-start(bf16[2,1,1,64,640]{4,3,2,1,0:T(8,128)(2,1)S(1)} %pad_maximum_fusion.4), channel_id=1, source_target_pairs={{0,8},{4,12},{8,0},{12,4},{16,24},{20,28},{24,16},{28,20},{1,9},{5... | collective-permute-start | bytes 491528 | tf_op jit(solution)/shard_map/ppermute | solution.py:1443
  45.9 21.6 %collective-permute-start.9 = (bf16[2,2,1,64,640]{4,3,2,1,0:T(8,128)(2,1)S(1)}, bf16[2,2,1,64,640]{4,3,2,1,0:T(8,128)(2,1)}, u32[]{:S(2)}, u32[]{:S(2)}) collective-permute-start(bf16[2,2,1,64,640]{4,3,2,1,0:T(8,128)(2,1)S(1)} %pad_maximum_fusion.3.refs_3_), channel_id=1, source_target_pairs={{0,4},{4,0},{8,12},{12,8},{16,20},{20,16},{24,28},{28,24},{1,5},{5... | collective-permute-start | bytes 983048 | tf_op jit(solution)/shard_map/ppermute | solution.py:1443
  65.7 11.3 %collective-permute-start.5 = (bf16[64,8,2,256]{3,1,2,0:T(8,128)(2,1)S(1)}, bf16[64,8,2,256]{3,1,2,0:T(8,128)(2,1)S(1)}, u32[]{:S(2)}, u32[]{:S(2)}) collective-permute-start(bf16[64,8,2,256]{3,1,2,0:T(8,128)(2,1)S(1)} %bitcast.246), channel_id=1, source_target_pairs={{0,1},{1,0},{2,3},{3,2},{4,5},{5,4},{6,7},{7,6},{8,9},{9,8},{10,11... | collective-permute-start | bytes 1572872 | tf_op jit(solution)/shard_map/ppermute | solution.py:1443
  65.9 11.3 %copy-start.36 = (f32[8,1,256]{2,1,0:T(1,128)}, f32[8,1,256]{2,1,0:T(1,128)S(1)}, u32[]{:S(2)}) copy-start(f32[8,1,256]{2,1,0:T(1,128)S(1)} %constant_dynamic-update-slice_fusion.8.refs_3_) | copy-start | bytes 24580
  65.9 10.2 %collective-permute-start.11 = (bf16[2,2,1,64,640]{4,3,2,1,0:T(8,128)(2,1)S(1)}, bf16[2,2,1,64,640]{4,3,2,1,0:T(8,128)(2,1)S(1)}, u32[]{:S(2)}, u32[]{:S(2)}) collective-permute-start(bf16[2,2,1,64,640]{4,3,2,1,0:T(8,128)(2,1)S(1)} %copy-done.23), channel_id=1, source_target_pairs={{0,2},{1,3},{2,0},{3,1},{4,6},{5,7},{6,4},{7,5},{8,10},{9,11},{10,... | collective-permute-start | bytes 983048 | tf_op jit(solution)/shard_map/ppermute | solution.py:1443
  68.7 21.0 %copy-start.12 = (bf16[2,2,2,64,640]{4,3,2,1,0:T(8,128)(2,1)}, bf16[2,2,2,64,640]{4,3,2,1,0:T(8,128)(2,1)S(1)}, u32[]{:S(2)}) copy-start(bf16[2,2,2,64,640]{4,3,2,1,0:T(8,128)(2,1)S(1)} %pad_maximum_fusion.1) | copy-start | bytes 1966084
  68.7 49.0 %collective-permute-start.10 = (bf16[2,2,2,64,640]{4,3,2,1,0:T(8,128)(2,1)S(1)}, bf16[2,2,2,64,640]{4,3,2,1,0:T(8,128)(2,1)}, u32[]{:S(2)}, u32[]{:S(2)}) collective-permute-start(bf16[2,2,2,64,640]{4,3,2,1,0:T(8,128)(2,1)S(1)} %pad_maximum_fusion.1), channel_id=1, source_target_pairs={{0,1},{1,0},{2,3},{3,2},{4,5},{5,4},{6,7},{7,6},{8,9},{9,8},{10,11... | collective-permute-start | bytes 1966088 | tf_op jit(solution)/shard_map/ppermute | solution.py:1443
  76.0 12.6 %collective-permute-start.12 = (bf16[2,2,1,64,640]{4,3,2,1,0:T(8,128)(2,1)S(1)}, bf16[2,2,1,64,640]{4,3,2,1,0:T(8,128)(2,1)S(1)}, u32[]{:S(2)}, u32[]{:S(2)}) collective-permute-start(bf16[2,2,1,64,640]{4,3,2,1,0:T(8,128)(2,1)S(1)} %collective-permute-done.11), channel_id=1, source_target_pairs={{0,4},{4,0},{8,12},{12,8},{16,20},{20,16},{24,28},{28,24},{1,5},{5... | collective-permute-start | bytes 983048 | tf_op jit(solution)/shard_map/ppermute | solution.py:1443
  77.2 19.1 %copy-start.4 = (bf16[64,8192]{1,0:T(8,128)(2,1)S(1)}, bf16[64,8192]{1,0:T(8,128)(2,1)}, u32[]{:S(2)}) copy-start(bf16[64,8192]{1,0:T(8,128)(2,1)} %copy-done.3) | copy-start | bytes 3145732
  77.2 12.4 %collective-permute-start.6 = (bf16[64,8,256]{2,1,0:T(8,128)(2,1)S(1)}, bf16[64,8,256]{2,1,0:T(8,128)(2,1)S(1)}, u32[]{:S(2)}, u32[]{:S(2)}) collective-permute-start(bf16[64,8,256]{2,1,0:T(8,128)(2,1)S(1)} %dynamic-slice_bitcast_fusion.4), channel_id=1, source_target_pairs={{0,2},{1,3},{2,0},{3,1},{4,6},{5,7},{6,4},{7,5},{8,10},{9,11},{10,... | collective-permute-start | bytes 786440 | tf_op jit(solution)/shard_map/ppermute | solution.py:1443
  89.6 28.0 %collective-permute-start.13 = (bf16[2,2,2,64,640]{4,3,2,1,0:T(8,128)(2,1)}, bf16[2,2,2,64,640]{4,3,2,1,0:T(8,128)(2,1)}, u32[]{:S(2)}, u32[]{:S(2)}) collective-permute-start(bf16[2,2,2,64,640]{4,3,2,1,0:T(8,128)(2,1)} %pad_maximum_fusion.2), channel_id=1, source_target_pairs={{0,1},{1,0},{2,3},{3,2},{4,5},{5,4},{6,7},{7,6},{8,9},{9,8},{10,11... | collective-permute-start | bytes 1966088 | tf_op jit(solution)/shard_map/ppermute | solution.py:1443
  90.4 22.6 %all-to-all-start = ((bf16[64,8,256]{2,0,1:T(8,128)(2,1)}), bf16[64,8,256]{2,0,1:T(8,128)(2,1)S(1)}, u32[]{:S(2)}, u32[]{:S(2)}) async-start(bf16[64,8,256]{2,0,1:T(8,128)(2,1)} %copy.127), calls=%async_computation | async-start | bytes 524288 | tf_op jit(solution)/shard_map/all_to_all | solution.py:1608
  96.2 127.5 %all-gather.5.cloned.1.call-start = ((), (), s32[]{:S(2)}) async-start(), calls=%async_computation.3 | async-start | bytes 5242880 | tf_op jit(solution)/shard_map/all_gather | solution.py:1610
  117.6 289.2 %reduce-scatter.2.cloned.1.call-start = ((), (), s32[]{:S(2)}) async-start(), calls=%async_computation.4 | async-start | bytes 5242880 | tf_op jit(solution)/shard_map/reduce_scatter | solution.py:1646
  315.0 34.2 %copy-start.11 = (bf16[2,4,64,1024]{3,2,1,0:T(8,128)(2,1)S(1)}, bf16[2,4,64,1024]{3,2,1,0:T(8,128)(2,1)}, u32[]{:S(2)}) copy-start(bf16[2,4,64,1024]{3,2,1,0:T(8,128)(2,1)} %get-tuple-element.193) | copy-start | bytes 3145732
  350.9 11.7 %copy-start.2 = (f32[2,4,64,1024]{3,2,1,0:T(8,128)}, f32[2,4,64,1024]{3,2,1,0:T(8,128)S(1)}, u32[]{:S(2)}) copy-start(f32[2,4,64,1024]{3,2,1,0:T(8,128)S(1)} %convert_add_fusion.2) | copy-start | bytes 6291460
  362.6 38.5 %copy-start.10 = (bf16[2,4,64,1024]{3,2,1,0:T(8,128)(2,1)S(1)}, bf16[2,4,64,1024]{3,2,1,0:T(8,128)(2,1)}, u32[]{:S(2)}) copy-start(bf16[2,4,64,1024]{3,2,1,0:T(8,128)(2,1)} %get-tuple-element.214) | copy-start | bytes 3145732
  406.8 21.2 %copy-start.15 = (bf16[8,64,640]{2,1,0:T(8,128)(2,1)S(1)}, bf16[8,64,640]{2,1,0:T(8,128)(2,1)}, u32[]{:S(2)}) copy-start(bf16[8,64,640]{2,1,0:T(8,128)(2,1)} %get-tuple-element.212) | copy-start | bytes 1966084
  431.0 36.5 %copy-start.9 = (bf16[2,4,64,1024]{3,2,1,0:T(8,128)(2,1)S(1)}, bf16[2,4,64,1024]{3,2,1,0:T(8,128)(2,1)}, u32[]{:S(2)}) copy-start(bf16[2,4,64,1024]{3,2,1,0:T(8,128)(2,1)} %get-tuple-element.234) | copy-start | bytes 3145732
  (26 other events, 67.4 us)
Sparse Core Ops, SparseCore 0:
  11.6 131.1 all-gather.2
  144.4 79.3 all-gather.4
  300.0 74.7 reduce-scatter.1
